TPU v7x, 32 devices: a whole 2x2x4 slice. The times are simulated.
32 devices in a mesh: gx: 4 (over z), gy: 8 (over y, x, core).
Axes of the slice: x: 2, y: 2, z: 4, core: 2. Of those that a mesh axis runs over, the one named last changes fastest.
Arguments:
- tokens: bfloat16 [8192, 1152], P('gy'), may hold values from -6 to 6
- parents: int32 [32], replicated, may hold values from -1 to 23, as said below
- w_query: bfloat16 [1152, 1024], P('gy', 'gx'), may hold values from -0.1875 to 0.1875
- w_key: bfloat16 [1152, 256], P(('gx', 'gy')), may hold values from -0.1875 to 0.1875
- w_value: bfloat16 [1152, 256], P(('gx', 'gy')), may hold values from -0.1875 to 0.1875
- w_out: bfloat16 [1024, 1152], P('gx', 'gy'), may hold values from -0.1875 to 0.1875
- w_gate: bfloat16 [1152, 6912], P('gy', 'gx'), may hold values from -0.1875 to 0.1875
- w_up: bfloat16 [1152, 6912], P('gy', 'gx'), may hold values from -0.1875 to 0.1875
- w_down: bfloat16 [6912, 1152], P('gx', 'gy'), may hold values from -0.078125 to 0.078125
- g_attn_in: bfloat16 [1152], P('gy'), may hold values from 0.25 to 1.75
- g_attn_out: bfloat16 [1152], P('gy'), may hold values from 0.25 to 1.75
- g_ffn_in: bfloat16 [1152], P('gy'), may hold values from 0.25 to 1.75
- g_ffn_out: bfloat16 [1152], P('gy'), may hold values from 0.25 to 1.75
- g_query: bfloat16 [256], P('gy'), may hold values from 0.25 to 1.75
- g_key: bfloat16 [256], P('gy'), may hold values from 0.25 to 1.75
- cotangent: bfloat16 [8192, 1152], P('gy'), may hold values from -6 to 6
Outputs:
- output: bfloat16 [8192, 1152], P('gy')
- grad_tokens: float32 [8192, 1152], P('gy')
- grad_g_attn_in: float32 [1152], P('gy')
- grad_g_attn_out: float32 [1152], P('gy')
- grad_g_ffn_in: float32 [1152], P('gy')
- grad_g_ffn_out: float32 [1152], P('gy')
- grad_g_query: float32 [256], P('gy')
- grad_g_key: float32 [256], P('gy')
- grad_w_query: float32 [1152, 1024], P('gy', 'gx')
- grad_w_key: float32 [1152, 256], P(('gx', 'gy'))
- grad_w_value: float32 [1152, 256], P(('gx', 'gy'))
- grad_w_out: float32 [1024, 1152], P('gx', 'gy')
- grad_w_gate: float32 [1152, 6912], P('gy', 'gx')
- grad_w_up: float32 [1152, 6912], P('gy', 'gx')
- grad_w_down: float32 [6912, 1152], P('gx', 'gy')
Inputs may be any that keep to these rules, and one draw needn't show every extreme that they name: Segments come in trees of 16, aligned runs of 16 segment numbers. In each run, the first 4 form a chain in some order whose first has parent -1, the next 4 all have the chain's last as parent, and the last 8 have the middle 4 as parents, two each. Parents are global segment numbers.
All inputs are finite; a program needn't handle non-finite values.
Results may differ from a plain program's by a relative error of at most 0.022.
Values may be sent and summed in bfloat16 or wider, within the bound.
No kernel may reach another device: no remote copies, remote signals or barrier semaphores. Data moves between devices by JAX's collectives and lax.ppermute only.
A program may use at most 192 MiB of HBM per device.

v0:
```python
import jax
import jax.numpy as jnp
from jax import lax
from jax.sharding import PartitionSpec as P

WIN = 512
NANC = 2


EPSILON = 1e-06
MASKED = -1e30


def from_behind(block, axis, distance):
    devices = range(lax.axis_size(axis))
    route = [(i - distance, i) for i in devices if i - distance in devices]
    return lax.ppermute(block, axis, route)


def rms_norm(values, gain):
    return values * lax.rsqrt(jnp.mean(values * values, axis=-1, keepdims=True) + EPSILON) * gain


def angles(depth, head_width):
    half_width = head_width // 2
    rates = 10000.0 ** (-jnp.arange(half_width, dtype=jnp.float32) / half_width)
    turned = depth.astype(jnp.float32)[:, None] * rates[None, :]
    return (jnp.cos(turned), jnp.sin(turned))


def rotate(values, cos_table, sin_table):
    half_width = values.shape[-1] // 2
    first_half = values[..., :half_width]
    second_half = values[..., half_width:]
    return jnp.concatenate(
        [
            first_half * cos_table - second_half * sin_table,
            second_half * cos_table + first_half * sin_table,
        ],
        axis=-1,
    )


def ancestry(parents, levels):
    lineage = []
    current = parents
    seg_level = jnp.zeros_like(parents)
    for level_step in range(5):
        lineage.append(current)
        seg_level = seg_level + (current >= 0).astype(jnp.int32)
        current = jnp.where(current >= 0, jnp.take(parents, jnp.maximum(current, 0)), -1)
    while len(lineage) < levels:
        lineage.append(jnp.full_like(parents, -1))
    return (seg_level, jnp.stack(lineage[:levels], axis=1))


def path_mask(level_query, level_key, alive_slot, seg_len, window):
    offsets = jnp.arange(seg_len, dtype=jnp.int32)
    depth_query = level_query[:, None] * seg_len + offsets[None, :]
    depth_key = level_key[:, :, None] * seg_len + offsets[None, None, :]
    distance = depth_query[:, :, None, None] - depth_key[:, None, :, :]
    visible = alive_slot[:, None, :, None] & (distance >= 0) & (distance < window)
    return visible.reshape(level_query.shape[0], seg_len, -1)


def contract_last(left_side, right_side):
    return lax.dot_general(
        left_side, right_side, (((1,), (1,)), ((), ())), preferred_element_type=jnp.float32
    )


def contract_first(left_side, right_side):
    return lax.dot_general(
        left_side, right_side, (((0,), (0,)), ((), ())), preferred_element_type=jnp.float32
    )


def glu_product(gate_proj, up_proj):
    return jax.nn.gelu(gate_proj, approximate=True) * up_proj


def gain_share(values, gain, incoming):
    return jax.vjp(rms_norm, values, gain)[1](incoming)[1]


def body(
    tokens,
    parents,
    w_query,
    w_key,
    w_value,
    w_out,
    w_gate,
    w_up,
    w_down,
    g_attn_in,
    g_attn_out,
    g_ffn_in,
    g_ffn_out,
    g_query,
    g_key,
    cotangent,
):
    column = lax.axis_index("gy")
    head_part = lax.axis_index("gx")
    part_count = lax.axis_size("gx")
    row_count, model_width = tokens.shape
    seg_len = row_count // 4
    head_width = w_key.shape[1]
    heads_here = w_query.shape[1] // head_width
    rows_here = row_count // part_count
    row_start = head_part * rows_here

    def rows_of(values):
        return lax.dynamic_slice_in_dim(values, row_start, rows_here, 0)

    gathered = (
        lax.all_gather(w_query, "gy", axis=0, tiled=True),
        lax.all_gather(w_out, "gy", axis=1, tiled=True),
        lax.all_gather(w_gate, "gy", axis=0, tiled=True),
        lax.all_gather(w_up, "gy", axis=0, tiled=True),
        lax.all_gather(w_down, "gy", axis=1, tiled=True),
        lax.all_gather(g_attn_in, "gy", axis=0, tiled=True),
        lax.all_gather(g_attn_out, "gy", axis=0, tiled=True),
        lax.all_gather(g_ffn_in, "gy", axis=0, tiled=True),
        lax.all_gather(g_ffn_out, "gy", axis=0, tiled=True),
        lax.all_gather(g_query, "gy", axis=0, tiled=True),
        lax.all_gather(g_key, "gy", axis=0, tiled=True),
    )
    query_full, out_full, gate_full, up_full, down_full = (
        gathered[0],
        gathered[1],
        gathered[2],
        gathered[3],
        gathered[4],
    )
    gain_in, gain_post, gain_ffn, gain_last, gain_query, gain_key = [
        gain_piece.astype(jnp.float32) for gain_piece in gathered[5:]
    ]
    key_full, value_full = (
        lax.all_gather(w_key, ("gx", "gy"), axis=0, tiled=True),
        lax.all_gather(w_value, ("gx", "gy"), axis=0, tiled=True),
    )
    seg_level, lineage = ancestry(parents, NANC)
    own_segs = 4 * column + jnp.arange(4, dtype=jnp.int32)
    own_level = jnp.take(seg_level, own_segs)
    slots = jnp.concatenate([own_segs[:, None], jnp.take(lineage, own_segs, axis=0)], axis=1)
    alive_slot = slots >= 0
    window_slot = jnp.clip(slots - 4 * column + 12, 0, 15).reshape(-1)
    key_level = jnp.take(seg_level, jnp.maximum(slots, 0))
    visible = path_mask(own_level, key_level, alive_slot, seg_len, WIN)
    offsets = jnp.arange(seg_len, dtype=jnp.int32)
    depth_own = (own_level[:, None] * seg_len + offsets[None, :]).reshape(-1)
    cos_table, sin_table = angles(depth_own, head_width)

    def query_path(raw_values, gain):
        shaped = rms_norm(raw_values.reshape(row_count, heads_here, head_width), gain)
        return rotate(shaped, cos_table[:, None], sin_table[:, None])

    def key_path(raw_values, gain):
        return rotate(rms_norm(raw_values, gain), cos_table, sin_table)

    residual = tokens.astype(jnp.float32)
    normed = rms_norm(residual, gain_in).astype(jnp.bfloat16)
    query_raw = jnp.dot(normed, query_full, preferred_element_type=jnp.float32)
    key_raw = jnp.dot(normed, key_full, preferred_element_type=jnp.float32)
    value_used = jnp.dot(normed, value_full, preferred_element_type=jnp.float32).astype(
        jnp.bfloat16
    )
    query_used = query_path(query_raw, gain_query).astype(jnp.bfloat16)
    key_used = key_path(key_raw, gain_key).astype(jnp.bfloat16)
    own_pair = jnp.concatenate([key_used, value_used], axis=1)
    columns = []
    for distance in (3, 2, 1):
        columns.append(from_behind(own_pair, "gy", distance))
    window_pairs = jnp.concatenate(columns + [own_pair], axis=0).reshape(
        16, seg_len, 2 * head_width
    )
    picked = jnp.take(window_pairs, window_slot, axis=0).reshape(4, -1, 2 * head_width)
    keys_used = picked[:, :, :head_width]
    values_used = picked[:, :, head_width:]
    queries = query_used.reshape(4, seg_len, heads_here, head_width)
    score_scale = head_width ** (-0.5)

    def masked_scores():
        raw_scores = (
            jnp.einsum("sqhd,skd->shqk", queries, keys_used, preferred_element_type=jnp.float32)
            * score_scale
        )
        return jnp.where(visible[:, None], raw_scores, MASKED)

    scores = masked_scores()
    row_max = jnp.max(scores, axis=-1, keepdims=True)
    weights = jnp.exp(scores - row_max)
    totals = jnp.sum(weights, axis=-1, keepdims=True)
    soft_weights = weights / totals
    log_total = row_max + jnp.log(totals)
    heads_out = jnp.einsum(
        "shqk,skd->sqhd",
        soft_weights.astype(jnp.bfloat16),
        values_used,
        preferred_element_type=jnp.float32,
    )
    heads_low = heads_out.reshape(row_count, -1).astype(jnp.bfloat16)
    attn_part = jnp.dot(heads_low, out_full, preferred_element_type=jnp.float32)
    upstream = cotangent.astype(jnp.float32)
    upstream_rows = rows_of(upstream)
    attn_total = lax.psum(attn_part, "gx")
    mid_residual = residual + rms_norm(attn_total, gain_post)
    normed_ffn = rms_norm(mid_residual, gain_ffn).astype(jnp.bfloat16)
    gate_part = jnp.dot(normed_ffn, gate_full, preferred_element_type=jnp.float32)
    up_part = jnp.dot(normed_ffn, up_full, preferred_element_type=jnp.float32)
    hidden = glu_product(gate_part, up_part).astype(jnp.bfloat16)
    ffn_total = lax.psum(jnp.dot(hidden, down_full, preferred_element_type=jnp.float32), "gx")
    output = (mid_residual + rms_norm(ffn_total, gain_last)).astype(jnp.bfloat16)
    d_ffn = jax.vjp(rms_norm, ffn_total, gain_last)[1](upstream)[0]
    d_ffn_low = d_ffn.astype(jnp.bfloat16)
    d_gain_last = gain_share(rows_of(ffn_total), gain_last, upstream_rows)
    d_hidden = contract_last(d_ffn_low, down_full)
    grad_down = contract_first(hidden, d_ffn_low)
    pull_glu = jax.vjp(glu_product, gate_part, up_part)[1]
    d_gate, d_up = pull_glu(d_hidden)
    d_gate_low = d_gate.astype(jnp.bfloat16)
    d_up_low = d_up.astype(jnp.bfloat16)
    grad_gate = contract_first(normed_ffn, d_gate_low)
    grad_up = contract_first(normed_ffn, d_up_low)
    ffn_back_part = contract_last(d_gate_low, gate_full) + contract_last(d_up_low, up_full)
    d_normed_ffn = lax.psum(ffn_back_part, "gx")
    d_mid = upstream + jax.vjp(rms_norm, mid_residual, gain_ffn)[1](d_normed_ffn)[0]
    d_gain_ffn = gain_share(rows_of(mid_residual), gain_ffn, rows_of(d_normed_ffn))
    d_attn = jax.vjp(rms_norm, attn_total, gain_post)[1](d_mid)[0]
    d_gain_post = gain_share(rows_of(attn_total), gain_post, rows_of(d_mid))
    d_attn_low = d_attn.astype(jnp.bfloat16)
    grad_out = contract_first(heads_low, d_attn_low)
    d_heads = (
        contract_last(d_attn_low, out_full)
        .astype(jnp.bfloat16)
        .reshape(4, seg_len, heads_here, head_width)
    )
    probs_back = jnp.exp(masked_scores() - log_total)
    d_probs = jnp.einsum("sqhd,skd->shqk", d_heads, values_used, preferred_element_type=jnp.float32)
    d_scores = (
        probs_back * (d_probs - jnp.sum(d_probs * probs_back, axis=-1, keepdims=True))
    ).astype(jnp.bfloat16)
    d_queries = (
        jnp.einsum("shqk,skd->sqhd", d_scores, keys_used, preferred_element_type=jnp.float32)
        * score_scale
    )
    d_keys = (
        jnp.einsum("shqk,sqhd->skd", d_scores, queries, preferred_element_type=jnp.float32)
        * score_scale
    )
    d_values = jnp.einsum(
        "shqk,sqhd->skd",
        probs_back.astype(jnp.bfloat16),
        d_heads,
        preferred_element_type=jnp.float32,
    )
    d_picked = jnp.concatenate([d_keys, d_values], axis=-1).reshape(-1, seg_len, 2 * head_width)
    d_window = jnp.zeros((16, seg_len, 2 * head_width), jnp.float32).at[window_slot].add(d_picked)
    d_window = d_window.reshape(4, row_count, 2 * head_width)
    d_own = d_window[3]
    for distance in (3, 2, 1):
        d_own = d_own + from_behind(d_window[3 - distance], "gy", -distance)
    d_own = lax.psum(d_own, "gx")
    pull_key = jax.vjp(key_path, key_raw, gain_key)[1]
    d_key_raw, d_gain_key = pull_key(d_own[:, :head_width])
    pull_query = jax.vjp(query_path, query_raw, gain_query)[1]
    d_query_raw, d_gain_query = pull_query(d_queries.reshape(row_count, heads_here, head_width))
    d_query_low = d_query_raw.astype(jnp.bfloat16)
    d_pair_low = jnp.concatenate(
        [d_key_raw.astype(jnp.bfloat16), d_own[:, head_width:].astype(jnp.bfloat16)], axis=1
    )
    block_width = model_width // part_count
    block_start = head_part * block_width
    kv_rows = jnp.concatenate(
        [
            lax.dynamic_slice_in_dim(key_full, block_start, block_width, 0),
            lax.dynamic_slice_in_dim(value_full, block_start, block_width, 0),
        ],
        axis=1,
    )
    d_normed_part = contract_last(d_query_low, query_full)
    kv_term = contract_last(d_pair_low, kv_rows)
    d_normed_part = lax.dynamic_update_slice_in_dim(
        d_normed_part,
        lax.dynamic_slice_in_dim(d_normed_part, block_start, block_width, 1) + kv_term,
        block_start,
        1,
    )
    d_normed, d_gain_query, d_gain_post, d_gain_ffn, d_gain_last = (
        lax.psum(d_normed_part.astype(jnp.bfloat16), "gx").astype(jnp.float32),
        lax.psum(d_gain_query.astype(jnp.bfloat16), "gx").astype(jnp.float32),
        lax.psum(d_gain_post.astype(jnp.bfloat16), "gx").astype(jnp.float32),
        lax.psum(d_gain_ffn.astype(jnp.bfloat16), "gx").astype(jnp.float32),
        lax.psum(d_gain_last.astype(jnp.bfloat16), "gx").astype(jnp.float32),
    )
    grad_query = contract_first(normed, d_query_low)
    grad_pair = contract_first(
        lax.dynamic_slice_in_dim(normed, block_start, block_width, 1), d_pair_low
    )
    pull_in = jax.vjp(rms_norm, residual, gain_in)[1]
    d_res_add, d_gain_in = pull_in(d_normed)
    grad_tokens = d_mid + d_res_add
    summed = (
        lax.psum_scatter(
            grad_query.astype(jnp.bfloat16), "gy", scatter_dimension=0, tiled=True
        ).astype(jnp.float32),
        lax.psum_scatter(
            grad_out.astype(jnp.bfloat16), "gy", scatter_dimension=1, tiled=True
        ).astype(jnp.float32),
        lax.psum_scatter(
            grad_gate.astype(jnp.bfloat16), "gy", scatter_dimension=0, tiled=True
        ).astype(jnp.float32),
        lax.psum_scatter(
            grad_up.astype(jnp.bfloat16), "gy", scatter_dimension=0, tiled=True
        ).astype(jnp.float32),
        lax.psum_scatter(
            grad_down.astype(jnp.bfloat16), "gy", scatter_dimension=1, tiled=True
        ).astype(jnp.float32),
        lax.psum_scatter(
            grad_pair[:, :head_width].astype(jnp.bfloat16), "gy", scatter_dimension=0, tiled=True
        ).astype(jnp.float32),
        lax.psum_scatter(
            grad_pair[:, head_width:].astype(jnp.bfloat16), "gy", scatter_dimension=0, tiled=True
        ).astype(jnp.float32),
        lax.psum_scatter(
            d_gain_in.astype(jnp.bfloat16), "gy", scatter_dimension=0, tiled=True
        ).astype(jnp.float32),
        lax.psum_scatter(
            d_gain_post.astype(jnp.bfloat16), "gy", scatter_dimension=0, tiled=True
        ).astype(jnp.float32),
        lax.psum_scatter(
            d_gain_ffn.astype(jnp.bfloat16), "gy", scatter_dimension=0, tiled=True
        ).astype(jnp.float32),
        lax.psum_scatter(
            d_gain_last.astype(jnp.bfloat16), "gy", scatter_dimension=0, tiled=True
        ).astype(jnp.float32),
        lax.psum_scatter(
            d_gain_query.astype(jnp.bfloat16), "gy", scatter_dimension=0, tiled=True
        ).astype(jnp.float32),
        lax.psum_scatter(
            d_gain_key.astype(jnp.bfloat16), "gy", scatter_dimension=0, tiled=True
        ).astype(jnp.float32),
    )
    return (
        output,
        grad_tokens,
        summed[7],
        summed[8],
        summed[9],
        summed[10],
        summed[11],
        summed[12],
        summed[0],
        summed[5],
        summed[6],
        summed[1],
        summed[2],
        summed[3],
        summed[4],
    )


def solution(mesh):
    return jax.shard_map(
        body,
        mesh=mesh,
        in_specs=(
            P("gy", None),
            P(),
            P("gy", "gx"),
            P(("gx", "gy"), None),
            P(("gx", "gy"), None),
            P("gx", "gy"),
            P("gy", "gx"),
            P("gy", "gx"),
            P("gx", "gy"),
            P("gy"),
            P("gy"),
            P("gy"),
            P("gy"),
            P("gy"),
            P("gy"),
            P("gy", None),
        ),
        out_specs=(
            P("gy", None),
            P("gy", None),
            P("gy"),
            P("gy"),
            P("gy"),
            P("gy"),
            P("gy"),
            P("gy"),
            P("gy", "gx"),
            P(("gx", "gy"), None),
            P(("gx", "gy"), None),
            P("gx", "gy"),
            P("gy", "gx"),
            P("gy", "gx"),
            P("gx", "gy"),
        ),
        check_vma=False,
    )
```

profile of v0, /device:TPU:0, one launch (start us, length us, event | category | flops | bytes accessed | tf_op | source)
XLA Modules:
  0.0 1338.4 jit_solution(12406976230415359213)
XLA Ops:
  16.4 26.1 %all-reduce.21 = (bf16[1152]{0:T(1024)(128)(2,1)S(1)}, bf16[256]{0:T(256)(128)(2,1)}, bf16[256]{0:T(256)(128)(2,1)}, bf16[1152]{0:T(1024)(128)(2,1)}, bf16[1152]{0:T(1024)(128)(2,1)}, /*index=5*/bf16[1152]{0:T(1024)(128)(2,1)}) all-reduce(bf16[1152]{0:T(1024)(128)(2,1)S(1)} %dynamic-update-slice, ...), channel_id=1, replica_groups=mesh['gx'=4,'gy'=8] {'gy'}, use_global_device_ids=true, to_apply=%add.4 | all-reduce | flops 5120 | bytes 20480
  54.2 40.3 %all-gather.1 = bf16[32,36,256]{2,1,0:T(8,128)(2,1)S(1)} all-gather(bf16[1,36,256]{2,1,0:T(8,128)(2,1)S(1)} %bitcast.153), channel_id=1, replica_groups=mesh['gx'=4,'gy'=8] {'gx','gy'}, dimensions={0}, use_global_device_ids=true | all-gather | bytes 608256 | tf_op jit(solution)/shard_map/all_gather | solution.py:142
  95.4 41.4 %all-gather = bf16[32,36,256]{2,1,0:T(8,128)(2,1)} all-gather(bf16[1,36,256]{2,1,0:T(8,128)(2,1)} %bitcast.154), channel_id=1, replica_groups=mesh['gx'=4,'gy'=8] {'gx','gy'}, dimensions={0}, use_global_device_ids=true | all-gather | bytes 608256 | tf_op jit(solution)/shard_map/all_gather | solution.py:141
  154.3 57.1 %all_gather.43 = bf16[1152,256]{1,0:T(8,128)(2,1)S(1)} all-gather(bf16[144,256]{1,0:T(8,128)(2,1)S(1)} %copy-done.47), channel_id=1, replica_groups=mesh['gx'=4,'gy'=8] {'gy'}, dimensions={0}, use_global_device_ids=true | all-gather | bytes 663552 | tf_op jit(solution)/shard_map/all_gather | solution.py:118
  214.9 10.7 all_gather.45
  229.0 19.4 %maximum_maximum_fusion = bf16[4096,512]{0,1:T(8,128)(2,1)} fusion(bf16[1024,256]{0,1:T(8,128)(2,1)S(1)} %copy-done.35, bf16[1024,128]{0,1:T(8,128)(2,1)S(1)} %copy-done.29, bf16[1024,128]{0,1:T(8,128)(2,1)S(1)} %copy-done.27, bf16[1024,512]{0,1:T(8,128)(2,1)} %collective-permute-done.2, bf16[1024,512]{0,1:T(8,128)(2,1)} %collective-permute-done.1, ...), kind=kLoop, calls=%fused_computation.57 | loop fusion | flops 25165824 | bytes 8388608 | tf_op jit(solution)/shard_map/concatenate | solution.py:176
  271.4 167.6 %all-reduce.30.cloned.1.call-done = f32[1024,1152]{1,0:T(8,128)} async-done(((f32[1024,1152]{1,0:T(8,128)}), f32[1024,1152]{1,0:T(8,128)}) %all-reduce.30.cloned.1.call-update) | async-done | bytes 4718608 | tf_op jit(solution)/shard_map/psum | solution.py:208
  446.7 9.9 fusion.109
  456.6 12.3 multiply_convert_fusion.1
  468.9 10.4 fusion.110
  480.0 170.4 %all-reduce.32.cloned.1.call-done = f32[1024,1152]{1,0:T(8,128)} async-done(((f32[1024,1152]{1,0:T(8,128)}), f32[1024,1152]{1,0:T(8,128)}) %all-reduce.32.cloned.1.call-update) | async-done | bytes 4718608 | tf_op jit(solution)/shard_map/psum | solution.py:214
  659.3 15.8 %multiply_convert_fusion = (bf16[1024,1728]{0,1:T(8,128)(2,1)}, bf16[1024,1728]{0,1:T(8,128)(2,1)}) fusion(f32[1024,1728]{0,1:T(8,128)} %fusion.109, f32[1024,1728]{0,1:T(8,128)} %get-tuple-element.87, bf16[1024,1152]{1,0:T(8,128)(2,1)S(1)} %get-tuple-element.60, bf16[1728,1152]{0,1:T(8,128)(2,1)S(1)} %copy-done.72), kind=kOutput, calls=%fused_computation.26 | convolution fusion | flops 4119330816 | bytes 27574272 | tf_op jit(solution)/shard_map/dot_general | solution.py:67
  689.4 171.1 %all-reduce.34.cloned.1.call-done = f32[1024,1152]{1,0:T(8,128)} async-done(((f32[1024,1152]{1,0:T(8,128)}), f32[1024,1152]{1,0:T(8,128)}) %all-reduce.34.cloned.1.call-update) | async-done | bytes 4718608 | tf_op jit(solution)/shard_map/psum | solution.py:228
  888.0 13.4 %scatter_fusion = f32[16,256,512]{2,1,0:T(8,128)} fusion(f32[16,256,512]{2,1,0:T(8,128)} %broadcast_in_dim.67, s32[12]{0:T(128)S(1)} %fusion.97, f32[12,256,512]{2,1,0:T(8,128)} %bitcast.132), kind=kCustom, calls=%fused_computation.8 | custom fusion | flops 1572864 | bytes 18874416 | tf_op jit(solution)/shard_map/scatter-add | solution.py:260
  924.1 77.9 %collective-permute-done.4 = f32[1024,512]{0,1:T(8,128)} collective-permute-done((f32[1024,512]{0,1:T(8,128)}, f32[1024,512]{0,1:T(8,128)}, u32[]{:S(2)}, u32[]{:S(2)}) %collective-permute-start.4) | collective-permute-done | bytes 2097184 | tf_op jit(solution)/shard_map/ppermute | solution.py:17
  1024.9 9.1 convolution_convert_fusion.2
  1034.5 9.1 convolution_convert_fusion.1
  1043.8 9.3 convolution_convert_fusion
  1060.2 60.2 %all-reduce.36.cloned.1.call-done = f32[1024,512]{0,1:T(8,128)} async-done(((f32[1024,512]{0,1:T(8,128)}), f32[1024,512]{0,1:T(8,128)}) %all-reduce.36.cloned.1.call-update) | async-done | bytes 2097168 | tf_op jit(solution)/shard_map/psum | solution.py:265
  1160.1 18.1 %fusion.102 = (bf16[40,256]{1,0:T(8,128)(2,1)S(1)}, bf16[40,256]{1,0:T(8,128)(2,1)S(1)}) fusion(bf16[288,256]{1,0:T(8,128)(2,1)S(1)} %get-tuple-element.71, bf16[288,256]{1,0:T(8,128)(2,1)S(1)} %get-tuple-element.70), kind=kCustom, calls=%all-reduce-scatter.2 | all-reduce-scatter fusion | flops 163841 | bytes 336384
  1188.2 37.5 %reduce-scatter.16.cloned.1.call-done = bf16[144,1728]{1,0:T(8,128)(2,1)} async-done(((bf16[1152,1728]{1,0:T(8,128)(2,1)}), bf16[144,1728]{1,0:T(8,128)(2,1)}) %reduce-scatter.16.cloned.1.call-update) | async-done | bytes 497680 | tf_op jit(solution)/shard_map/reduce_scatter | solution.py:315
  1227.8 52.5 %reduce-scatter.18.cloned.1.call-done = bf16[1728,144]{0,1:T(8,128)(2,1)} async-done(((bf16[1728,1152]{0,1:T(8,128)(2,1)}), bf16[1728,144]{0,1:T(8,128)(2,1)}) %reduce-scatter.18.cloned.1.call-update) | async-done | bytes 497680 | tf_op jit(solution)/shard_map/reduce_scatter | solution.py:318
  1287.6 23.0 %all-reduce.20 = (bf16[1152]{0:T(1024)(128)(2,1)S(1)}, bf16[1152]{0:T(1024)(128)(2,1)S(1)}, bf16[1152]{0:T(1024)(128)(2,1)S(1)}, bf16[1152]{0:T(1024)(128)(2,1)S...) all-reduce(bf16[1152]{0:T(1024)(128)(2,1)S(1)} %get-tuple-element.1, ...), channel_id=2, replica_groups=mesh['gx'=4,'gy'=8] {'gy'}, use_global_device_ids=true, to_apply=%region_22.24.clone | all-reduce | flops 5120 | bytes 20480
  1311.6 11.6 all-reduce.22
  (376 shorter events, 244.2 us)
Async XLA Ops:
  8.0 431.0 %all-reduce.30.cloned.1.call-start = ((), (), s32[]{:S(2)}) async-start(), calls=%async_computation.5 | async-start | bytes 9437184 | tf_op jit(solution)/shard_map/psum | solution.py:208
  145.0 83.9 %collective-permute-start.2 = (bf16[1024,512]{0,1:T(8,128)(2,1)}, bf16[1024,512]{0,1:T(8,128)(2,1)}, u32[]{:S(2)}, u32[]{:S(2)}) collective-permute-start(bf16[1024,512]{0,1:T(8,128)(2,1)} %pad_maximum_fusion.1), channel_id=1, source_target_pairs={{0,1},{1,2},{2,3},{3,4},{4,5},{5,6},{6,7},{8,9},{9,10},{10,11},{11... | collective-permute-start | bytes 3145736 | tf_op jit(solution)/shard_map/ppermute | solution.py:17
  148.4 80.6 %collective-permute-start.1 = (bf16[1024,512]{0,1:T(8,128)(2,1)}, bf16[1024,512]{0,1:T(8,128)(2,1)}, u32[]{:S(2)}, u32[]{:S(2)}) collective-permute-start(bf16[1024,512]{0,1:T(8,128)(2,1)} %pad_maximum_fusion.1), channel_id=1, source_target_pairs={{0,2},{1,3},{2,4},{3,5},{4,6},{5,7},{8,10},{9,11},{10,12},{11,13},... | collective-permute-start | bytes 3145736 | tf_op jit(solution)/shard_map/ppermute | solution.py:17
  152.0 77.0 %collective-permute-start = (bf16[1024,512]{0,1:T(8,128)(2,1)}, bf16[1024,512]{0,1:T(8,128)(2,1)}, u32[]{:S(2)}, u32[]{:S(2)}) collective-permute-start(bf16[1024,512]{0,1:T(8,128)(2,1)} %pad_maximum_fusion.1), channel_id=1, source_target_pairs={{0,3},{1,4},{2,5},{3,6},{4,7},{8,11},{9,12},{10,13},{11,14},{12,15... | collective-permute-start | bytes 3145736 | tf_op jit(solution)/shard_map/ppermute | solution.py:17
  269.6 177.1 %all-gather.6.cloned.1.call-start = ((), (), s32[]{:S(2)}) async-start(), calls=%async_computation.6 | async-start | bytes 4644864 | tf_op jit(solution)/shard_map/all_gather | solution.py:120
  270.2 186.4 %all-gather.8.cloned.1.call-start = ((), (), s32[]{:S(2)}) async-start(), calls=%async_computation.7 | async-start | bytes 4644864 | tf_op jit(solution)/shard_map/all_gather | solution.py:121
  270.8 198.1 %all-gather.10.cloned.1.call-start = ((), (), s32[]{:S(2)}) async-start(), calls=%async_computation.8 | async-start | bytes 4644864 | tf_op jit(solution)/shard_map/all_gather | solution.py:122
  271.3 379.1 %all-reduce.32.cloned.1.call-start = ((), (), s32[]{:S(2)}) async-start(), calls=%async_computation.9 | async-start | bytes 9437184 | tf_op jit(solution)/shard_map/psum | solution.py:214
  479.3 171.1 %copy-start.8 = (bf16[1024,1152]{1,0:T(8,128)(2,1)S(1)}, bf16[1024,1152]{1,0:T(8,128)(2,1)}, u32[]{:S(2)}) copy-start(bf16[1024,1152]{1,0:T(8,128)(2,1)} %param.33) | copy-start | bytes 7077892
  479.3 381.1 %all-reduce.34.cloned.1.call-start = ((), (), s32[]{:S(2)}) async-start(), calls=%async_computation.10 | async-start | bytes 9437184 | tf_op jit(solution)/shard_map/psum | solution.py:228
  689.3 431.0 %all-reduce.36.cloned.1.call-start = ((), (), s32[]{:S(2)}) async-start(), calls=%async_computation.11 | async-start | bytes 4194304 | tf_op jit(solution)/shard_map/psum | solution.py:265
  911.3 12.8 collective-permute-start.5
  915.5 86.5 %collective-permute-start.4 = (f32[1024,512]{0,1:T(8,128)}, f32[1024,512]{0,1:T(8,128)}, u32[]{:S(2)}, u32[]{:S(2)}) collective-permute-start(f32[1024,512]{0,1:T(8,128)} %copy.102), channel_id=1, source_target_pairs={{2,0},{3,1},{4,2},{5,3},{6,4},{7,5},{10,8},{11,9},{12,10},{13,11},... | collective-permute-start | bytes 6291464 | tf_op jit(solution)/shard_map/ppermute | solution.py:17
  919.7 87.0 %collective-permute-start.3 = (f32[1024,512]{0,1:T(8,128)}, f32[1024,512]{0,1:T(8,128)}, u32[]{:S(2)}, u32[]{:S(2)}) collective-permute-start(f32[1024,512]{0,1:T(8,128)} %copy.101), channel_id=1, source_target_pairs={{3,0},{4,1},{5,2},{6,3},{7,4},{11,8},{12,9},{13,10},{14,11},{15,12... | collective-permute-start | bytes 6291464 | tf_op jit(solution)/shard_map/ppermute | solution.py:17
  1012.6 170.2 %reduce-scatter.10.cloned.1.call-start = ((), (), s32[]{:S(2)}) async-start(), calls=%async_computation.13 | async-start | bytes 663552 | tf_op jit(solution)/shard_map/reduce_scatter | solution.py:306
  1021.3 163.2 %reduce-scatter.12.cloned.1.call-start = ((), (), s32[]{:S(2)}) async-start(), calls=%async_computation.14 | async-start | bytes 663552 | tf_op jit(solution)/shard_map/reduce_scatter | solution.py:309
  1024.9 161.2 %reduce-scatter.14.cloned.1.call-start = ((), (), s32[]{:S(2)}) async-start(), calls=%async_computation.15 | async-start | bytes 4644864 | tf_op jit(solution)/shard_map/reduce_scatter | solution.py:312
  1034.1 191.7 %reduce-scatter.16.cloned.1.call-start = ((), (), s32[]{:S(2)}) async-start(), calls=%async_computation.16 | async-start | bytes 4644864 | tf_op jit(solution)/shard_map/reduce_scatter | solution.py:315
  1043.7 236.7 %reduce-scatter.18.cloned.1.call-start = ((), (), s32[]{:S(2)}) async-start(), calls=%async_computation.17 | async-start | bytes 4644864 | tf_op jit(solution)/shard_map/reduce_scatter | solution.py:318
  1053.1 230.9 %all-reduce.38.cloned.1.call-start = ((), (), s32[]{:S(2)}) async-start(), calls=%async_computation.12 | async-start | bytes 4718592 | tf_op jit(solution)/shard_map/psum | solution.py:292
  1160.1 123.9 %copy-start.4 = (bf16[1024,1152]{1,0:T(8,128)(2,1)S(1)}, bf16[1024,1152]{1,0:T(8,128)(2,1)}, u32[]{:S(2)}) copy-start(bf16[1024,1152]{1,0:T(8,128)(2,1)} %param.18) | copy-start | bytes 7077892
  1160.1 123.9 %copy-start.45 = (f32[1152]{0:T(1024)S(1)}, f32[1152]{0:T(1024)}, u32[]{:S(2)}) copy-start(f32[1152]{0:T(1024)} %copy-done.44) | copy-start | bytes 13828
  1178.3 104.2 %collective-permute-start.6 = (bf16[28,256]{1,0:T(8,128)(2,1)S(1)}, bf16[28,256]{1,0:T(8,128)(2,1)S(1)}, u32[]{:S(2)}, u32[]{:S(2)}) collective-permute-start(bf16[28,256]{1,0:T(8,128)(2,1)S(1)} %slice.91), channel_id=1, source_target_pairs={{0,1},{1,2},{2,3},{3,4},{4,5},{5,6},{6,7},{8,9},{9,10},{10,11},{11... | collective-permute-start | bytes 43016
  1179.6 103.0 %collective-permute-start.7 = (bf16[28,256]{1,0:T(8,128)(2,1)S(1)}, bf16[28,256]{1,0:T(8,128)(2,1)S(1)}, u32[]{:S(2)}, u32[]{:S(2)}) collective-permute-start(bf16[28,256]{1,0:T(8,128)(2,1)S(1)} %slice.92), channel_id=1, source_target_pairs={{0,1},{1,2},{2,3},{3,4},{4,5},{5,6},{6,7},{8,9},{9,10},{10,11},{11... | collective-permute-start | bytes 43016
  (75 other events, 1644.2 us)
Sparse Core Ops, SparseCore 0:
  269.7 169.2 all-reduce.29
  479.4 170.9 all-reduce.31
  689.4 170.9 all-reduce.33
  1012.8 107.5 all-reduce.35
  1145.1 95.7 all-reduce.37
Sparse Core Ops, SparseCore 1:
  272.0 33.5 all-gather.5
  307.3 36.2 all-gather.7
  345.3 36.2 all-gather.9
  1021.4 55.4 reduce-scatter.9
  1080.2 34.4 reduce-scatter.11
  1118.5 51.7 reduce-scatter.13
  1174.0 51.8 reduce-scatter.15
  1229.5 50.9 reduce-scatter.17
where the time goes:
time: 1350 us; the launch traced here: 1340 us
  waiting for transfers between devices  744 us (55%)
  blocking collectives  228 us (17%)
  other arithmetic  133 us (10%)
  matrix products  120 us (9%)
  local copies, waits for them, and re-layouts  77.1 us (6%)
  between operations  20 us (1%)
  starting transfers between devices  16.7 us (1%)
    psum x1, waiting for transfers between devices, body(): d_normed_ffn = lax.psum(ffn_back_part, 'gx')  171 us
    psum x1, waiting for transfers between devices, body(): lax.psum(jnp.dot(hidden, down_full, preferred_element_type=jnp.float32),...  170 us
    psum x1, waiting for transfers between devices, body(): attn_total = lax.psum(attn_part, 'gx')  168 us
    ppermute x6, waiting for transfers between devices, from_behind(): return lax.ppermute(block, axis, route)  82.6 us
    unnamed x3, blocking collectives  67.2 us
    psum x1, waiting for transfers between devices, body(): d_own = lax.psum(d_own, 'gx')  60.2 us
    all_gather x1, blocking collectives, body(): lax.all_gather(w_query, 'gy', axis=0, tiled=True)  57.1 us
    reduce_scatter x1, waiting for transfers between devices, body(): lax.psum_scatter(grad_down.astype(jnp.bfloat16), 'gy', scatter_dimension=...  52.5 us
  transfers between devices with their start and end apart: 21, of which 8 were waited for; matrix products, arithmetic and copies ran while one was open for 12% of the time, Pallas kernels for 0%

commit v1 on v0

v1 whole, which is shorter than its diff:
```python
import math

import jax
import jax.numpy as jnp
from jax import lax
from jax.experimental import pallas as pl
from jax.experimental.pallas import tpu as pltpu
from jax.sharding import Mesh
from jax.sharding import PartitionSpec as P

SEG = 256
EPSILON = 1e-06
MASKED = -1e30
PLANE = ("gb", "ga", "gc")
SWAP = [(0, 1), (1, 0)]
F32 = jnp.float32
BF16 = jnp.bfloat16


def rms_norm(values, gain):
    return values * lax.rsqrt(jnp.mean(values * values, axis=-1, keepdims=True) + EPSILON) * gain


def norm_back(values, gain, incoming):
    r = lax.rsqrt(jnp.mean(values * values, axis=-1, keepdims=True) + EPSILON)
    scaled = gain * incoming
    inner = jnp.mean(values * scaled, axis=-1, keepdims=True)
    return r * scaled - values * (r * r * r) * inner, incoming * values * r


def rotate(values, cos_table, sin_table):
    half_width = values.shape[-1] // 2
    a, b = values[..., :half_width], values[..., half_width:]
    return jnp.concatenate([a * cos_table - b * sin_table, b * cos_table + a * sin_table], axis=-1)


def dot(a, b, dims=(1, 0)):
    return lax.dot_general(
        a, b, (((dims[0],), (dims[1],)), ((), ())), preferred_element_type=F32
    )


def swap(x, axis):
    return lax.ppermute(x, axis, SWAP)


def across(x, distance):
    return lax.ppermute(x, "gx", [(i, i ^ distance) for i in range(4)])


def place(pieces, slots, count):
    rows, width = pieces[0].shape[-2:]
    shape = jax.ShapeDtypeStruct((count, rows, width), pieces[0].dtype)

    def kernel(slot_ref, *refs):
        ins, (out, held, sems) = refs[: len(pieces)], refs[len(pieces) :]
        loads = [
            pltpu.make_async_copy(ref, held.at[i], sems.at[0, i]) for i, ref in enumerate(ins)
        ]
        stores = [
            pltpu.make_async_copy(held.at[i], out.at[slot_ref[i]], sems.at[1, i])
            for i in range(len(pieces))
        ]
        for load in loads:
            load.start()
        for load, store in zip(loads, stores):
            load.wait()
            store.start()
        for store in stores:
            store.wait()

    return pl.pallas_call(
        kernel,
        out_shape=shape,
        in_specs=[pl.BlockSpec(memory_space=pltpu.SMEM)]
        + [pl.BlockSpec(memory_space=pl.ANY)] * len(pieces),
        out_specs=pl.BlockSpec(memory_space=pl.ANY),
        scratch_shapes=[
            pltpu.VMEM((len(pieces), rows, width), pieces[0].dtype),
            pltpu.SemaphoreType.DMA((2, len(pieces))),
        ],
        compiler_params=pltpu.CompilerParams(vmem_limit_bytes=32 * 2**20),
    )(slots, *pieces)


def plane_gather(x):
    if lax.axis_size("ga") != 2:
        return lax.all_gather(x, PLANE, axis=0)
    half = x.shape[0] // 32 * 16
    from_x, from_y = swap(x, "ga"), swap(x, "gb")
    diagonal = jnp.concatenate([swap(from_y[:half], "ga"), swap(from_x[half:], "gb")], axis=0)
    mine = [x, from_x, from_y, diagonal]
    theirs = [swap(piece, "gc") for piece in mine]
    here = lax.axis_index(PLANE)
    slots = jnp.array([0, 2, 4, 6, 1, 3, 5, 7], jnp.int32) ^ here
    return place(mine + theirs, slots, 8)


def plane_scatter(g):
    if lax.axis_size("ga") != 2:
        return lax.psum_scatter(g, PLANE, scatter_dimension=0).astype(F32)
    y, x, c = [lax.axis_index(name) for name in PLANE]
    g = g.reshape((4, 2) + g.shape[1:])

    def pick(values, index, axis):
        return lax.dynamic_index_in_dim(values, index, axis, keepdims=False)

    received = swap(pick(g, 1 - c, 1), "gc")

    def chip(number):
        return pick(pick(g, c, 1), number, 0).astype(F32) + pick(received, number, 0).astype(F32)

    here, by_x, by_y, far = [
        chip(n) for n in (2 * y + x, 2 * y + 1 - x, 2 * (1 - y) + x, 2 * (1 - y) + 1 - x)
    ]
    far = far.astype(BF16)
    half = g.shape[2] // 32 * 16
    got_first = swap(far[:half], "ga")
    got_second = swap(far[half:], "gb")
    send_x = jnp.concatenate([by_x[:half], by_x[half:] + got_second.astype(F32)], axis=0)
    send_y = jnp.concatenate([by_y[:half] + got_first.astype(F32), by_y[half:]], axis=0)
    return here + swap(send_x.astype(BF16), "ga").astype(F32) + swap(
        send_y.astype(BF16), "gb"
    ).astype(F32)


def glu(gate, up):
    return jax.nn.gelu(gate, approximate=True) * up


def body(
    tokens,
    parents,
    w_query,
    w_key,
    w_value,
    w_out,
    w_gate,
    w_up,
    w_down,
    g_attn_in,
    g_attn_out,
    g_ffn_in,
    g_ffn_out,
    g_query,
    g_key,
    cotangent,
):
    column = lax.axis_index(PLANE)
    columns = lax.axis_size(PLANE)
    plane = lax.axis_index("gx")
    planes = lax.axis_size("gx")
    width = tokens.shape[1]
    head_width = w_key.shape[1]
    heads = planes * w_query.shape[1] // head_width
    block, small = w_query.shape[0], w_key.shape[0]
    gains_len = 4 * block + 2 * g_query.shape[0]
    gain_rows = -(-gains_len // (2 * head_width))
    used = block + small + gain_rows
    pack_rows = -(-used // 16) * 16
    pack_width = 2 * head_width

    ffn_mine = jnp.concatenate([w_gate, w_up, w_down.T], axis=0)
    ffn_theirs = across(ffn_mine, 2)
    gains = jnp.concatenate([g_attn_in, g_attn_out, g_ffn_in, g_ffn_out, g_query, g_key])
    gains = jnp.pad(gains, (0, gain_rows * pack_width - gains_len)).reshape(gain_rows, pack_width)
    pack = jnp.concatenate(
        [
            jnp.concatenate([w_query, w_out.T], axis=1),
            jnp.concatenate([w_key, w_value], axis=1),
            gains,
            jnp.zeros((pack_rows - used, pack_width), BF16),
        ],
        axis=0,
    )
    pack = lax.all_gather(pack, "gx", axis=0, tiled=True)
    pack = plane_gather(pack).reshape(columns, planes, pack_rows, pack_width)

    def from_blocks(blocks):
        return blocks.transpose(0, 2, 1, 3).reshape(columns * block, -1)

    wq = from_blocks(pack[:, :, :block, :head_width])
    wo_t = from_blocks(pack[:, :, :block, head_width:])
    wkv = pack[:, :, block : block + small].transpose(1, 0, 2, 3).reshape(width, pack_width)
    gains = pack[:, 0, block + small : used].reshape(columns, -1)[:, :gains_len].astype(F32)
    gain_in, gain_post, gain_ffn, gain_last = [
        gains[:, i * block : (i + 1) * block].reshape(-1) for i in range(4)
    ]
    gain_query, gain_key = [
        gains[:, 4 * block + i * g_query.shape[0] :][:, : g_query.shape[0]].reshape(-1)
        for i in range(2)
    ]

    def ffn_weights(mine):
        stacked = plane_gather(mine).reshape(columns, 3, block, -1)
        return [stacked[:, i].reshape(width, -1) for i in range(3)]

    quarters = [ffn_weights(ffn_mine), ffn_weights(ffn_theirs)]

    def parent_of(segment):
        found = lax.dynamic_index_in_dim(parents, jnp.maximum(segment, 0), 0, keepdims=False)
        return jnp.where(segment >= 0, found, -1)

    def level_of(segment):
        level = jnp.int32(0)
        for _ in range(5):
            segment = parent_of(segment)
            level = level + (segment >= 0).astype(jnp.int32)
        return level

    first = 4 * column
    role = column % 4
    own = first + plane
    own_a = parent_of(own)
    own_b = parent_of(own_a)

    def later(distance):
        return jnp.minimum(own + 4 * distance, parents.shape[0] - 1)

    a1, a2 = parent_of(later(1)), parent_of(later(2))
    b1, b2 = parent_of(a1), parent_of(a2)

    def local(segment):
        return jnp.clip(segment - first, 0, 3)

    pick_1 = local(a1)
    pick_2 = local(jnp.where(role == 0, b2, a2))
    pick_3 = local(b1)
    pick_a, pick_b = local(own_a), local(own_b)
    trees = range(columns // 4)
    route_1 = [(4 * t + i, 4 * t + i + 1) for t in trees for i in (0, 1)]
    route_2 = [(4 * t + i, 4 * t + i + 2) for t in trees for i in (0, 1)]
    route_3 = [(4 * t + i, 4 * t + i + 1) for t in trees for i in (0, 2)]

    def send(x, route):
        return lax.ppermute(x, PLANE, route)

    def send_back(x, route):
        return lax.ppermute(x, PLANE, [(b, a) for a, b in route])

    levels = jnp.stack([level_of(first + i) for i in range(4)])
    depth = (levels[:, None] * SEG + jnp.arange(SEG, dtype=jnp.int32)[None, :]).reshape(-1)
    half_width = head_width // 2
    rates = 10000.0 ** (-jnp.arange(half_width, dtype=F32) / half_width)
    turned = depth.astype(F32)[:, None] * rates[None, :]
    cos_table, sin_table = jnp.cos(turned), jnp.sin(turned)

    def own_rows(x):
        return lax.dynamic_slice_in_dim(x, plane * SEG, SEG, 0)

    def pair_rows(x):
        other = lax.dynamic_slice_in_dim(x, (plane ^ 1) * SEG, SEG, 0)
        return jnp.concatenate([own_rows(x), other], axis=0)

    residual = tokens.astype(F32)
    normed = rms_norm(residual, gain_in).astype(BF16)
    normed_own = own_rows(normed)
    kv_raw = dot(normed, wkv)
    key_raw = kv_raw[:, :head_width]
    key_used = rotate(rms_norm(key_raw, gain_key), cos_table, sin_table).astype(BF16)
    pairs = jnp.concatenate([key_used, kv_raw[:, head_width:].astype(BF16)], axis=1)

    def segment_of(x, number):
        return lax.dynamic_slice_in_dim(x, number * SEG, SEG, 0)

    got_1 = send(segment_of(pairs, pick_1), route_1)
    got_2 = send(segment_of(pairs, pick_2), route_2)
    got_3 = send(jnp.where(role == 2, got_2, segment_of(pairs, pick_3)), route_3)
    slot_a = jnp.where(
        role == 0, segment_of(pairs, pick_a), jnp.where(role == 3, got_2, got_1)
    )
    slot_b = jnp.where(
        role == 0, segment_of(pairs, pick_b), jnp.where(role == 2, got_2, got_3)
    )
    slots = jnp.concatenate([own_rows(pairs), slot_a, slot_b], axis=0)
    keys, values = slots[:, :head_width], slots[:, head_width:]
    cos_own, sin_own = own_rows(cos_table)[:, None], own_rows(sin_table)[:, None]
    query_raw = dot(normed_own, wq).reshape(SEG, heads, head_width)
    queries = rotate(rms_norm(query_raw, gain_query), cos_own, sin_own).astype(BF16)
    offset = jnp.arange(SEG, dtype=jnp.int32)
    at_query, at_key = offset[:, None], offset[None, :]
    visible = jnp.concatenate(
        [
            at_key <= at_query,
            jnp.broadcast_to(own_a >= 0, (SEG, SEG)),
            (at_key > at_query) & (own_b >= 0),
        ],
        axis=1,
    )
    score_scale = head_width ** (-0.5)
    scores = jnp.einsum("qhd,kd->hqk", queries, keys, preferred_element_type=F32) * score_scale
    scores = jnp.where(visible[None], scores, MASKED)
    weights = jnp.exp(scores - jnp.max(scores, axis=-1, keepdims=True))
    probs = weights / jnp.sum(weights, axis=-1, keepdims=True)
    probs_low = probs.astype(BF16)
    heads_low = jnp.einsum("hqk,kd->qhd", probs_low, values, preferred_element_type=F32)
    heads_low = heads_low.reshape(SEG, -1).astype(BF16)

    heads_pair = jnp.concatenate([heads_low, across(heads_low, 1)], axis=0)
    attn = dot(heads_pair, wo_t, (1, 1))
    upstream = pair_rows(cotangent).astype(F32)
    mid = pair_rows(residual) + rms_norm(attn, gain_post)
    normed_ffn = rms_norm(mid, gain_ffn).astype(BF16)
    parts = []
    ffn_part = 0.0
    for gate_w, up_w, down_w in quarters:
        gate, up = dot(normed_ffn, gate_w), dot(normed_ffn, up_w)
        hidden = glu(gate, up).astype(BF16)
        parts.append((gate, up, hidden))
        ffn_part = ffn_part + dot(hidden, down_w, (1, 1))
    ffn_own = ffn_part[:SEG] + across(ffn_part[SEG:].astype(BF16), 1).astype(F32)
    ffn = jnp.concatenate([ffn_own, across(ffn_own.astype(BF16), 1).astype(F32)], axis=0)
    output = (mid[:SEG] + rms_norm(ffn_own, gain_last)).astype(BF16)
    output = lax.all_gather(output, "gx", axis=0, tiled=True)

    d_ffn, d_gain_last = norm_back(ffn, gain_last, upstream)
    d_ffn_low = d_ffn.astype(BF16)
    back = 0.0
    ffn_grads = []
    for (gate, up, hidden), (gate_w, up_w, down_w) in zip(parts, quarters):
        d_hidden = dot(d_ffn_low, down_w)
        d_gate, d_up = jax.vjp(glu, gate, up)[1](d_hidden)
        d_gate, d_up = d_gate.astype(BF16), d_up.astype(BF16)
        back = back + dot(d_gate, gate_w, (1, 1)) + dot(d_up, up_w, (1, 1))
        made = [
            dot(normed_ffn, d_gate, (0, 0)),
            dot(normed_ffn, d_up, (0, 0)),
            dot(d_ffn_low, hidden, (0, 0)),
        ]
        made = [m.astype(BF16).reshape(columns, block, -1) for m in made]
        ffn_grads.append(jnp.concatenate(made, axis=1))
    d_normed_ffn = back[:SEG] + across(back[SEG:].astype(BF16), 1).astype(F32)
    grads_theirs = plane_scatter(ffn_grads[1])
    grads_mine = plane_scatter(ffn_grads[0])
    ffn_grad = grads_mine + across(grads_theirs.astype(BF16), 2).astype(F32)

    d_mid_add, d_gain_ffn = norm_back(mid[:SEG], gain_ffn, d_normed_ffn)
    d_mid = upstream[:SEG] + d_mid_add
    d_attn, d_gain_post = norm_back(attn[:SEG], gain_post, d_mid)
    d_attn_low = d_attn.astype(BF16)
    grad_out_t = dot(d_attn_low, heads_low, (0, 0))
    d_heads = dot(d_attn_low, wo_t).astype(BF16).reshape(SEG, heads, head_width)
    d_probs = jnp.einsum("qhd,kd->hqk", d_heads, values, preferred_element_type=F32)
    d_scores = probs * (d_probs - jnp.sum(d_probs * probs, axis=-1, keepdims=True))
    d_scores = d_scores.astype(BF16)
    d_keys = jnp.einsum("hqk,qhd->kd", d_scores, queries, preferred_element_type=F32)
    d_values = jnp.einsum("hqk,qhd->kd", probs_low, d_heads, preferred_element_type=F32)
    d_slots = jnp.concatenate([d_keys * score_scale, d_values], axis=1)
    d_self, d_a, d_b = d_slots[:SEG], d_slots[SEG : 2 * SEG], d_slots[2 * SEG :]
    back_1 = send_back(d_a.astype(BF16), route_1)
    back_3 = send_back(d_b.astype(BF16), route_3)
    d_b_far = jnp.where(role == 2, d_b + back_3.astype(F32), 0.0)
    back_2 = send_back(jnp.where(role == 3, d_a, d_b_far).astype(BF16), route_2)
    near = role == 0
    terms = [
        (plane, d_self),
        (jnp.where(near & (own_a >= 0), pick_a, -1), d_a),
        (jnp.where(near & (own_b >= 0), pick_b, -1), d_b),
        (jnp.where(role <= 1, pick_1, -1), back_1.astype(F32)),
        (jnp.where(role <= 1, pick_2, -1), back_2.astype(F32)),
        (jnp.where(near, pick_3, -1), back_3.astype(F32)),
    ]
    d_window = jnp.concatenate(
        [sum(jnp.where(at == i, term, 0.0) for at, term in terms) for i in range(4)], axis=0
    )
    d_own = lax.psum_scatter(
        d_window.astype(BF16), "gx", scatter_dimension=0, tiled=True
    ).astype(F32)
    d_queries = jnp.einsum("hqk,kd->qhd", d_scores, keys, preferred_element_type=F32)
    d_query_raw, d_gain_query = norm_back(
        query_raw, gain_query, rotate(d_queries * score_scale, cos_own, -sin_own)
    )
    d_key_raw, d_gain_key = norm_back(
        own_rows(key_raw),
        gain_key,
        rotate(d_own[:, :head_width], cos_own[:, 0], -sin_own[:, 0]),
    )
    d_query_low = d_query_raw.reshape(SEG, -1).astype(BF16)
    d_kv_low = jnp.concatenate([d_key_raw, d_own[:, head_width:]], axis=1).astype(BF16)
    d_normed = dot(d_query_low, wq, (1, 1)) + dot(d_kv_low, wkv, (1, 1))
    d_res_add, d_gain_in = norm_back(own_rows(residual), gain_in, d_normed)
    grad_tokens = lax.all_gather(
        (d_mid + d_res_add).astype(BF16), "gx", axis=0, tiled=True
    ).astype(F32)

    def to_blocks(grad):
        return grad.astype(BF16).reshape(columns, block, planes, -1).transpose(0, 2, 1, 3)

    grad_query = to_blocks(dot(normed_own, d_query_low, (0, 0)))
    grad_out = to_blocks(grad_out_t)
    grad_kv = dot(normed_own, d_kv_low, (0, 0)).astype(BF16)
    grad_kv = grad_kv.reshape(planes, columns, small, -1).transpose(1, 0, 2, 3)
    gain_sums = [
        d_gain_in.sum(0),
        d_gain_post.sum(0),
        d_gain_ffn.sum(0),
        d_gain_last[:SEG].sum(0),
        d_gain_query.sum((0, 1)),
        d_gain_key.sum(0),
    ]
    gain_sums = jnp.concatenate([g.reshape(columns, -1) for g in gain_sums], axis=1).astype(BF16)
    gain_sums = jnp.pad(gain_sums, ((0, 0), (0, gain_rows * pack_width - gains_len)))
    gain_sums = jnp.broadcast_to(
        gain_sums.reshape(columns, 1, gain_rows, pack_width),
        (columns, planes, gain_rows, pack_width),
    )
    grads = jnp.concatenate(
        [
            jnp.concatenate([grad_query, grad_out], axis=3),
            grad_kv,
            gain_sums,
            jnp.zeros((columns, planes, pack_rows - used, pack_width), BF16),
        ],
        axis=2,
    )
    grads = plane_scatter(grads.reshape(columns, planes * pack_rows, pack_width))
    gain_grads = lax.all_gather(
        grads[block + small : used].astype(BF16), "gx", axis=0
    ).astype(F32).sum(0).reshape(-1)
    grads = lax.psum_scatter(
        grads.astype(BF16), "gx", scatter_dimension=0, tiled=True
    ).astype(F32)
    return (
        output,
        grad_tokens,
        gain_grads[:block],
        gain_grads[block : 2 * block],
        gain_grads[2 * block : 3 * block],
        gain_grads[3 * block : 4 * block],
        gain_grads[4 * block : 4 * block + g_query.shape[0]],
        gain_grads[4 * block + g_query.shape[0] : gains_len],
        grads[:block, :head_width],
        grads[block : block + small, :head_width],
        grads[block : block + small, head_width:],
        grads[:block, head_width:].T,
        ffn_grad[:block],
        ffn_grad[block : 2 * block],
        ffn_grad[2 * block :].T,
    )


def solution(mesh):
    side = math.isqrt(mesh.shape["gy"] // 2)
    split = Mesh(mesh.devices.reshape(mesh.shape["gx"], side, side, 2), ("gx",) + PLANE)
    whole = ("gx",) + PLANE
    return jax.shard_map(
        body,
        mesh=split,
        in_specs=(
            P(PLANE, None),
            P(),
            P(PLANE, "gx"),
            P(whole, None),
            P(whole, None),
            P("gx", PLANE),
            P(PLANE, "gx"),
            P(PLANE, "gx"),
            P("gx", PLANE),
            P(PLANE),
            P(PLANE),
            P(PLANE),
            P(PLANE),
            P(PLANE),
            P(PLANE),
            P(PLANE, None),
        ),
        out_specs=(
            P(PLANE, None),
            P(PLANE, None),
            P(PLANE),
            P(PLANE),
            P(PLANE),
            P(PLANE),
            P(PLANE),
            P(PLANE),
            P(PLANE, "gx"),
            P(whole, None),
            P(whole, None),
            P("gx", PLANE),
            P(PLANE, "gx"),
            P(PLANE, "gx"),
            P("gx", PLANE),
        ),
        check_vma=False,
    )
```

time: 1350 us -> 817 us (0.61)
  waiting for transfers between devices: 744 us -> 227 us
  blocking collectives: 228 us -> 103 us
  local copies, waits for them, and re-layouts: 77.1 us -> 160 us
  starting transfers between devices: 16.7 us -> 48.4 us
  matrix products: 120 us -> 99.9 us
  Pallas kernels: 0 us -> 17.5 us
  other arithmetic: 133 us -> 117 us
    psum x5 -> x0, waiting for transfers between devices: 569 us -> none  [the longest x1 171 us: body(): d_normed_ffn = lax.psum(ffn_back_part, 'gx')]
    ppermute x6 -> x51, waiting for transfers between devices: 82.6 us -> 222 us  [the longest x39 169 us: swap(): return lax.ppermute(x, axis, SWAP)]
    reduce_scatter x5 -> x2, waiting for transfers between devices: 90.1 us -> 4.76 us  [the longest x1 4.75 us: body(): lax.psum_scatter(d_window.astype(BF16), 'gx', scatter_dimension=0, tiled=...]
    unnamed x3 -> x0, blocking collectives: 67.2 us -> none
    all_gather x4 -> x2, blocking collectives: 149 us -> 103 us  [the longest x1 80.9 us: body(): lax.all_gather(grads[block + small:used].astype(BF16), 'gx', axis=0)]
    convert_element_type x0 -> x6, local copies, waits for them, and re-layouts: none -> 38.6 us  [body(): made = [m.astype(BF16).reshape(columns, block, -1) for m in made]]
    ppermute x6 -> x51, starting transfers between devices: 13 us -> 47.7 us  [the longest x39 31.9 us: swap(): return lax.ppermute(x, axis, SWAP)]
    slice x3 -> x31, local copies, waits for them, and re-layouts: 8.32 us -> 30.9 us  [the longest x2 10.7 us: ffn_weights(): return [stacked[:, i].reshape(width, -1) for i in range(3)]]
  transfers between devices with their start and end apart: 21 -> 55, of which waited for: 8 -> 17; matrix products, arithmetic and copies ran while one was open for 12% -> 33% of each run, Pallas kernels for 0% -> 1%
where the time goes in v1:
time: 817 us; the launch traced here: 805 us
  waiting for transfers between devices  227 us (28%)
  local copies, waits for them, and re-layouts  160 us (20%)
  other arithmetic  117 us (14%)
  blocking collectives  103 us (13%)
  matrix products  99.9 us (12%)
  starting transfers between devices  48.4 us (6%)
  between operations  33.1 us (4%)
  Pallas kernels  17.5 us (2%)
    ppermute x39, waiting for transfers between devices, swap(): return lax.ppermute(x, axis, SWAP)  169 us
    dot_general x27, matrix products, dot(): lax.dot_general(a, b, (((dims[0],), (dims[1],)), ((), ())), preferred_ele...  93.4 us
    all_gather x1, blocking collectives, body(): lax.all_gather(grads[block + small:used].astype(BF16), 'gx', axis=0)  80.9 us
    unnamed x229, local copies, waits for them, and re-layouts  40.2 us
    convert_element_type x6, local copies, waits for them, and re-layouts, body(): made = [m.astype(BF16).reshape(columns, block, -1) for m in made]  38.6 us
    ppermute x39, starting transfers between devices, swap(): return lax.ppermute(x, axis, SWAP)  31.9 us
    ppermute x6, waiting for transfers between devices, across(): return lax.ppermute(x, 'gx', [(i, i ^ distance) for i in range(4)])  29.3 us
    all_gather x1, blocking collectives, body(): pack = lax.all_gather(pack, 'gx', axis=0, tiled=True)  21.7 us
  transfers between devices with their start and end apart: 55, of which 17 were waited for; matrix products, arithmetic and copies ran while one was open for 33% of the time, Pallas kernels for 1%

profile of v1, /device:TPU:0, one launch (start us, length us, event | category | flops | bytes accessed | tf_op | source)
XLA Modules:
  0.0 805.5 jit_solution(5786902483345868505)
XLA Ops:
  12.5 21.7 %all_gather.15.refs_0_ = bf16[768,512]{1,0:T(8,128)(2,1)} all-gather(bf16[192,512]{1,0:T(8,128)(2,1)S(1)} %maximum_maximum_fusion.1), channel_id=1, replica_groups=mesh['gx'=4,'gb'=2,'ga'=2,'gc'=2] {'gx'}, dimensions={0}, use_global_device_ids=true | all-gather | bytes 983040 | tf_op jit(solution)/shard_map/all_gather | solution.py:176
  81.1 11.7 %collective-permute-done.2 = bf16[384,512]{1,0:T(8,128)(2,1)} collective-permute-done((bf16[384,512]{1,0:T(8,128)(2,1)}, bf16[384,512]{1,0:T(8,128)(2,1)}, u32[]{:S(2)}, u32[]{:S(2)}) %collective-permute-start.2) | collective-permute-done | bytes 393248 | tf_op jit(solution)/shard_map/ppermute | solution.py:44
  146.2 12.3 %collective-permute-done.8 = bf16[256,512]{0,1:T(8,128)(2,1)S(1)} collective-permute-done((bf16[256,512]{0,1:T(8,128)(2,1)}, bf16[256,512]{0,1:T(8,128)(2,1)S(1)}, u32[]{:S(2)}, u32[]{:S(2)}) %collective-permute-start.8) | collective-permute-done | bytes 262176 | tf_op jit(solution)/shard_map/ppermute | solution.py:236
  184.9 17.7 %collective-permute-done.22.refs_2_ = bf16[432,1728]{1,0:T(8,128)(2,1)} collective-permute-done((bf16[432,1728]{1,0:T(8,128)(2,1)}, bf16[432,1728]{1,0:T(8,128)(2,1)}, u32[]{:S(2)}, u32[]{:S(2)}) %collective-permute-start.22) | collective-permute-done | bytes 1493024 | tf_op jit(solution)/shard_map/ppermute | solution.py:44
  210.2 14.0 %collective-permute-done.23 = bf16[208,1728]{1,0:T(8,128)(2,1)S(1)} collective-permute-done((bf16[208,1728]{1,0:T(8,128)(2,1)S(1)}, bf16[208,1728]{1,0:T(8,128)(2,1)S(1)}, u32[]{:S(2)}, u32[]{:S(2)}) %collective-permute-start.23) | collective-permute-done | bytes 718880 | tf_op jit(solution)/shard_map/ppermute | solution.py:44
  226.1 17.1 %collective-permute-done.24 = bf16[224,1728]{1,0:T(8,128)(2,1)S(1)} collective-permute-done((bf16[224,1728]{1,0:T(8,128)(2,1)S(1)}, bf16[224,1728]{1,0:T(8,128)(2,1)S(1)}, u32[]{:S(2)}, u32[]{:S(2)}) %collective-permute-start.24) | collective-permute-done | bytes 774176 | tf_op jit(solution)/shard_map/ppermute | solution.py:44
  244.3 7.8 shard_map.299
  269.3 7.1 shard_map.300
  296.9 12.9 %collective-permute-done.29 = bf16[256,1152]{1,0:T(8,128)(2,1)S(1)} collective-permute-done((bf16[256,1152]{1,0:T(8,128)(2,1)}, bf16[256,1152]{1,0:T(8,128)(2,1)S(1)}, u32[]{:S(2)}, u32[]{:S(2)}) %collective-permute-start.29) | collective-permute-done | bytes 589856 | tf_op jit(solution)/shard_map/ppermute | solution.py:48
  311.9 14.2 %collective-permute-done.30 = bf16[256,1152]{1,0:T(8,128)(2,1)S(1)} collective-permute-done((bf16[256,1152]{1,0:T(8,128)(2,1)S(1)}, bf16[256,1152]{1,0:T(8,128)(2,1)S(1)}, u32[]{:S(2)}, u32[]{:S(2)}) %collective-permute-start.30) | collective-permute-done | bytes 589856 | tf_op jit(solution)/shard_map/ppermute | solution.py:48
  383.1 6.3 copy.92
  389.4 6.5 copy.91
  395.9 6.4 copy.90
  402.3 7.3 pad_maximum_fusion.1
  416.0 6.3 copy.89
  422.3 6.4 copy.88
  428.7 6.6 copy.87
  435.4 7.3 pad_maximum_fusion
  473.4 9.9 %collective-permute-done.34 = bf16[256,512]{0,1:T(8,128)(2,1)S(1)} collective-permute-done((bf16[256,512]{0,1:T(8,128)(2,1)S(1)}, bf16[256,512]{0,1:T(8,128)(2,1)S(1)}, u32[]{:S(2)}, u32[]{:S(2)}) %collective-permute-start.34) | collective-permute-done | bytes 262176 | tf_op jit(solution)/shard_map/ppermute | solution.py:239
  528.8 12.5 %maximum_maximum_fusion = bf16[8,4,192,512]{3,1,2,0:T(4,128)(2,1)S(1)} fusion(bf16[8,4,2,512]{3,1,2,0:T(4,128)(2,1)S(1)} %broadcast_in_dim.92, bf16[8,4,36,512]{3,1,2,0:T(4,128)(2,1)S(1)} %copy.85, bf16[8,4,144,256]{3,1,2,0:T(4,128)(2,1)S(1)} %bitcast.281, bf16[8,4,144,256]{3,1,2,0:T(4,128)(2,1)S(1)} %bitcast.282, bf16[192]{0:T(256)(128)(2,1)S(1)} %copy-done.92), kind=kLoop, calls=%fused_computation.9 | loop fusion | flops 31457280 | bytes 12255616 | tf_op jit(solution)/shard_map/concatenate | solution.py:407
  576.8 13.1 %collective-permute-done.43 = bf16[208,1728]{1,0:T(8,128)(2,1)S(1)} collective-permute-done((bf16[208,1728]{1,0:T(8,128)(2,1)S(1)}, bf16[208,1728]{1,0:T(8,128)(2,1)S(1)}, u32[]{:S(2)}, u32[]{:S(2)}) %collective-permute-start.43) | collective-permute-done | bytes 718880 | tf_op jit(solution)/shard_map/ppermute | solution.py:44
  599.6 7.8 collective-permute-done.36
  611.3 78.9 %collective-permute-done.39 = bf16[768,512]{1,0:T(8,128)(2,1)S(1)} collective-permute-done((bf16[768,512]{1,0:T(8,128)(2,1)S(1)}, bf16[768,512]{1,0:T(8,128)(2,1)S(1)}, u32[]{:S(2)}, u32[]{:S(2)}) %collective-permute-start.39) | collective-permute-done | bytes 786464 | tf_op jit(solution)/shard_map/ppermute | solution.py:44
  702.5 80.9 %all-gather.1 = bf16[4,2,512]{2,1,0:T(2,128)(2,1)S(1)} all-gather(bf16[1,2,512]{2,1,0:T(2,128)(2,1)S(1)} %slice_bitcast_fusion.9), channel_id=2, replica_groups=mesh['gx'=4,'gb'=2,'ga'=2,'gc'=2] {'gx'}, dimensions={0}, use_global_device_ids=true | all-gather | bytes 10240 | tf_op jit(solution)/shard_map/all_gather | solution.py:417
  (540 shorter events, 379.7 us)
Async XLA Ops:
  7.2 504.7 %reduce-scatter.3.cloned.1.call-start = ((), (), s32[]{:S(2)}) async-start(), calls=%async_computation.3 | async-start | bytes 1310720 | tf_op jit(solution)/shard_map/reduce_scatter | solution.py:366
  38.7 55.7 %collective-permute-start.12 = (bf16[432,1728]{1,0:T(8,128)(2,1)S(1)}, bf16[432,1728]{1,0:T(8,128)(2,1)S(1)}, u32[]{:S(2)}, u32[]{:S(2)}) collective-permute-start(bf16[432,1728]{1,0:T(8,128)(2,1)S(1)} %pad_maximum_fusion.3.refs_0_), channel_id=1, source_target_pairs={{0,2},{2,0},{1,3},{3,1},{4,6},{6,4},{5,7},{7,5},{8,10},{10,8},{9,1... | collective-permute-start | bytes 4478984 | tf_op jit(solution)/shard_map/ppermute | solution.py:44
  39.3 55.2 %collective-permute-start.13 = (bf16[432,1728]{1,0:T(8,128)(2,1)S(1)}, bf16[432,1728]{1,0:T(8,128)(2,1)}, u32[]{:S(2)}, u32[]{:S(2)}) collective-permute-start(bf16[432,1728]{1,0:T(8,128)(2,1)S(1)} %pad_maximum_fusion.3.refs_0_), channel_id=1, source_target_pairs={{0,4},{4,0},{1,5},{5,1},{2,6},{6,2},{3,7},{7,3},{8,12},{12,8},{9,1... | collective-permute-start | bytes 4478984 | tf_op jit(solution)/shard_map/ppermute | solution.py:44
  39.8 65.6 %collective-permute-start.20 = (bf16[432,1728]{1,0:T(8,128)(2,1)S(1)}, bf16[432,1728]{1,0:T(8,128)(2,1)}, u32[]{:S(2)}, u32[]{:S(2)}) collective-permute-start(bf16[432,1728]{1,0:T(8,128)(2,1)S(1)} %pad_maximum_fusion.3.refs_0_), channel_id=1, source_target_pairs={{0,16},{8,24},{16,0},{24,8},{1,17},{9,25},{17,1},{25,9},{2,18},{10... | collective-permute-start | bytes 4478984 | tf_op jit(solution)/shard_map/ppermute | solution.py:48
  101.7 80.0 %collective-permute-start.14 = (bf16[208,1728]{1,0:T(8,128)(2,1)}, bf16[208,1728]{1,0:T(8,128)(2,1)}, u32[]{:S(2)}, u32[]{:S(2)}) collective-permute-start(bf16[208,1728]{1,0:T(8,128)(2,1)} %slice.354), channel_id=1, source_target_pairs={{0,2},{2,0},{1,3},{3,1},{4,6},{6,4},{5,7},{7,5},{8,10},{10,8},{9,1... | collective-permute-start | bytes 2156552 | tf_op jit(solution)/shard_map/ppermute | solution.py:44
  105.4 77.6 %collective-permute-start.15 = (bf16[224,1728]{1,0:T(8,128)(2,1)}, bf16[224,1728]{1,0:T(8,128)(2,1)}, u32[]{:S(2)}, u32[]{:S(2)}) collective-permute-start(bf16[224,1728]{1,0:T(8,128)(2,1)} %slice.355), channel_id=1, source_target_pairs={{0,4},{4,0},{1,5},{5,1},{2,6},{6,2},{3,7},{7,3},{8,12},{12,8},{9,1... | collective-permute-start | bytes 2322440 | tf_op jit(solution)/shard_map/ppermute | solution.py:44
  106.9 96.8 %collective-permute-start.21 = (bf16[432,1728]{1,0:T(8,128)(2,1)}, bf16[432,1728]{1,0:T(8,128)(2,1)}, u32[]{:S(2)}, u32[]{:S(2)}) collective-permute-start(bf16[432,1728]{1,0:T(8,128)(2,1)} %collective-permute-done.20.refs_0_), channel_id=1, source_target_pairs={{0,2},{2,0},{1,3},{3,1},{4,6},{6,4},{5,7},{7,5},{8,10},{10,8},{9,1... | collective-permute-start | bytes 4478984 | tf_op jit(solution)/shard_map/ppermute | solution.py:44
  181.8 61.4 %collective-permute-start.16 = (bf16[432,1728]{1,0:T(8,128)(2,1)S(1)}, bf16[432,1728]{1,0:T(8,128)(2,1)S(1)}, u32[]{:S(2)}, u32[]{:S(2)}) collective-permute-start(bf16[432,1728]{1,0:T(8,128)(2,1)S(1)} %pad_maximum_fusion.3.refs_0_), channel_id=1, source_target_pairs={{0,1},{1,0},{2,3},{3,2},{4,5},{5,4},{6,7},{7,6},{8,9},{9,8},{10,11... | collective-permute-start | bytes 4478984 | tf_op jit(solution)/shard_map/ppermute | solution.py:44
  183.0 60.8 %collective-permute-start.17 = (bf16[432,1728]{1,0:T(8,128)(2,1)S(1)}, bf16[432,1728]{1,0:T(8,128)(2,1)S(1)}, u32[]{:S(2)}, u32[]{:S(2)}) collective-permute-start(bf16[432,1728]{1,0:T(8,128)(2,1)S(1)} %collective-permute-done.12.refs_1_), channel_id=1, source_target_pairs={{0,1},{1,0},{2,3},{3,2},{4,5},{5,4},{6,7},{7,6},{8,9},{9,8},{10,11... | collective-permute-start | bytes 4478984 | tf_op jit(solution)/shard_map/ppermute | solution.py:44
  202.6 41.3 %collective-permute-start.18 = (bf16[432,1728]{1,0:T(8,128)(2,1)}, bf16[432,1728]{1,0:T(8,128)(2,1)S(1)}, u32[]{:S(2)}, u32[]{:S(2)}) collective-permute-start(bf16[432,1728]{1,0:T(8,128)(2,1)} %collective-permute-done.13.refs_2_), channel_id=1, source_target_pairs={{0,1},{1,0},{2,3},{3,2},{4,5},{5,4},{6,7},{7,6},{8,9},{9,8},{10,11... | collective-permute-start | bytes 4478984 | tf_op jit(solution)/shard_map/ppermute | solution.py:44
  382.5 67.6 %collective-permute-start.31 = (bf16[256,1152]{1,0:T(8,128)(2,1)}, bf16[256,1152]{1,0:T(8,128)(2,1)S(1)}, u32[]{:S(2)}, u32[]{:S(2)}) collective-permute-start(bf16[256,1152]{1,0:T(8,128)(2,1)} %slice.513), channel_id=1, source_target_pairs={{0,8},{8,0},{16,24},{24,16},{1,9},{9,1},{17,25},{25,17},{2,10},{10... | collective-permute-start | bytes 1769480 | tf_op jit(solution)/shard_map/ppermute | solution.py:48
  416.0 133.6 %collective-permute-start.45 = (bf16[4,432,1728]{2,1,0:T(8,128)(2,1)}, bf16[4,432,1728]{2,1,0:T(8,128)(2,1)}, u32[]{:S(2)}, u32[]{:S(2)}) collective-permute-start(bf16[4,432,1728]{2,1,0:T(8,128)(2,1)} %dynamic-slice_bitcast_fusion), channel_id=1, source_target_pairs={{0,1},{1,0},{2,3},{3,2},{4,5},{5,4},{6,7},{7,6},{8,9},{9,8},{10,11... | collective-permute-start | bytes 17915912 | tf_op jit(solution)/shard_map/ppermute | solution.py:44
  449.5 106.4 %collective-permute-start.40 = (bf16[4,432,1728]{2,1,0:T(8,128)(2,1)}, bf16[4,432,1728]{2,1,0:T(8,128)(2,1)}, u32[]{:S(2)}, u32[]{:S(2)}) collective-permute-start(bf16[4,432,1728]{2,1,0:T(8,128)(2,1)} %dynamic-slice_bitcast_fusion.1), channel_id=1, source_target_pairs={{0,1},{1,0},{2,3},{3,2},{4,5},{5,4},{6,7},{7,6},{8,9},{9,8},{10,11... | collective-permute-start | bytes 17915912 | tf_op jit(solution)/shard_map/ppermute | solution.py:44
  485.5 212.2 %all-gather.5.cloned.1.call-start = ((), (), s32[]{:S(2)}) async-start(), calls=%async_computation.2 | async-start | bytes 2949120 | tf_op jit(solution)/shard_map/all_gather | solution.py:314
  506.7 191.0 %all-gather.7.cloned.1.call-start = ((), (), s32[]{:S(2)}) async-start(), calls=%async_computation.4 | async-start | bytes 2949120 | tf_op jit(solution)/shard_map/all_gather | solution.py:382
  549.3 235.4 %reduce-scatter.5.cloned.1.call-start = ((), (), s32[]{:S(2)}) async-start(), calls=%async_computation.5 | async-start | bytes 983040 | tf_op jit(solution)/shard_map/reduce_scatter | solution.py:420
  563.4 45.7 %collective-permute-start.41 = (bf16[224,1728]{1,0:T(8,128)(2,1)S(1)}, bf16[224,1728]{1,0:T(8,128)(2,1)S(1)}, u32[]{:S(2)}, u32[]{:S(2)}) collective-permute-start(bf16[224,1728]{1,0:T(8,128)(2,1)S(1)} %slice.397), channel_id=1, source_target_pairs={{0,4},{4,0},{1,5},{5,1},{2,6},{6,2},{3,7},{7,3},{8,12},{12,8},{9,1... | collective-permute-start | bytes 2322440 | tf_op jit(solution)/shard_map/ppermute | solution.py:44
  589.9 103.0 %collective-permute-start.49 = (bf16[432,1728]{1,0:T(8,128)(2,1)}, bf16[432,1728]{1,0:T(8,128)(2,1)}, u32[]{:S(2)}, u32[]{:S(2)}) collective-permute-start(bf16[432,1728]{1,0:T(8,128)(2,1)} %pad_maximum_fusion.7), channel_id=1, source_target_pairs={{0,4},{4,0},{1,5},{5,1},{2,6},{6,2},{3,7},{7,3},{8,12},{12,8},{9,1... | collective-permute-start | bytes 4478984 | tf_op jit(solution)/shard_map/ppermute | solution.py:44
  592.8 196.5 %collective-permute-start.44 = (bf16[432,1728]{1,0:T(8,128)(2,1)}, bf16[432,1728]{1,0:T(8,128)(2,1)}, u32[]{:S(2)}, u32[]{:S(2)}) collective-permute-start(bf16[432,1728]{1,0:T(8,128)(2,1)} %pad_maximum_fusion.5), channel_id=1, source_target_pairs={{0,4},{4,0},{1,5},{5,1},{2,6},{6,2},{3,7},{7,3},{8,12},{12,8},{9,1... | collective-permute-start | bytes 4478984 | tf_op jit(solution)/shard_map/ppermute | solution.py:44
  597.9 95.0 %collective-permute-start.47 = (bf16[432,1728]{1,0:T(8,128)(2,1)}, bf16[432,1728]{1,0:T(8,128)(2,1)}, u32[]{:S(2)}, u32[]{:S(2)}) collective-permute-start(bf16[432,1728]{1,0:T(8,128)(2,1)} %pad_maximum_fusion.6), channel_id=1, source_target_pairs={{0,2},{2,0},{1,3},{3,1},{4,6},{6,4},{5,7},{7,5},{8,10},{10,8},{9,1... | collective-permute-start | bytes 4478984 | tf_op jit(solution)/shard_map/ppermute | solution.py:44
  607.4 82.8 %collective-permute-start.39 = (bf16[768,512]{1,0:T(8,128)(2,1)S(1)}, bf16[768,512]{1,0:T(8,128)(2,1)S(1)}, u32[]{:S(2)}, u32[]{:S(2)}) collective-permute-start(bf16[768,512]{1,0:T(8,128)(2,1)S(1)} %pad_maximum_fusion.13), channel_id=1, source_target_pairs={{0,4},{4,0},{1,5},{5,1},{2,6},{6,2},{3,7},{7,3},{8,12},{12,8},{9,1... | collective-permute-start | bytes 2359304 | tf_op jit(solution)/shard_map/ppermute | solution.py:44
  609.1 81.4 %collective-permute-start.37 = (bf16[768,512]{1,0:T(8,128)(2,1)S(1)}, bf16[768,512]{1,0:T(8,128)(2,1)S(1)}, u32[]{:S(2)}, u32[]{:S(2)}) collective-permute-start(bf16[768,512]{1,0:T(8,128)(2,1)S(1)} %pad_maximum_fusion.12), channel_id=1, source_target_pairs={{0,2},{2,0},{1,3},{3,1},{4,6},{6,4},{5,7},{7,5},{8,10},{10,8},{9,1... | collective-permute-start | bytes 2359304 | tf_op jit(solution)/shard_map/ppermute | solution.py:44
  690.2 99.0 %collective-permute-start.42 = (bf16[432,1728]{1,0:T(8,128)(2,1)}, bf16[432,1728]{1,0:T(8,128)(2,1)S(1)}, u32[]{:S(2)}, u32[]{:S(2)}) collective-permute-start(bf16[432,1728]{1,0:T(8,128)(2,1)} %pad_maximum_fusion.4), channel_id=1, source_target_pairs={{0,2},{2,0},{1,3},{3,1},{4,6},{6,4},{5,7},{7,5},{8,10},{10,8},{9,1... | collective-permute-start | bytes 4478984 | tf_op jit(solution)/shard_map/ppermute | solution.py:44
  696.5 93.9 %collective-permute-start.50 = (bf16[432,1728]{1,0:T(8,128)(2,1)S(1)}, bf16[432,1728]{1,0:T(8,128)(2,1)}, u32[]{:S(2)}, u32[]{:S(2)}) collective-permute-start(bf16[432,1728]{1,0:T(8,128)(2,1)S(1)} %fusion.21), channel_id=1, source_target_pairs={{0,16},{8,24},{16,0},{24,8},{1,17},{9,25},{17,1},{25,9},{2,18},{10... | collective-permute-start | bytes 4478984 | tf_op jit(solution)/shard_map/ppermute | solution.py:48
  (139 other events, 1396.0 us)
Sparse Core Ops, SparseCore 0:
  485.6 26.2 reduce-scatter.2
  514.1 49.1 all-gather.4
  565.5 49.2 all-gather.6
  693.1 57.5 reduce-scatter.4

commit v2 on v1

v2 whole, which is shorter than its diff:
```python
import math

import jax
import jax.numpy as jnp
from jax import lax
from jax.experimental import pallas as pl
from jax.experimental.pallas import tpu as pltpu
from jax.sharding import Mesh
from jax.sharding import PartitionSpec as P

SEG = 256
EPSILON = 1e-06
MASKED = -1e30
PLANE = ("gb", "ga", "gc")
SWAP = [(0, 1), (1, 0)]
F32 = jnp.float32
BF16 = jnp.bfloat16


def rms_norm(values, gain):
    return values * lax.rsqrt(jnp.mean(values * values, axis=-1, keepdims=True) + EPSILON) * gain


def norm_back(values, gain, incoming):
    r = lax.rsqrt(jnp.mean(values * values, axis=-1, keepdims=True) + EPSILON)
    scaled = gain * incoming
    inner = jnp.mean(values * scaled, axis=-1, keepdims=True)
    return r * scaled - values * (r * r * r) * inner, incoming * values * r


def rotate(values, cos_table, sin_table):
    half_width = values.shape[-1] // 2
    a, b = values[..., :half_width], values[..., half_width:]
    return jnp.concatenate([a * cos_table - b * sin_table, b * cos_table + a * sin_table], axis=-1)


def dot(a, b, dims=(1, 0)):
    return lax.dot_general(
        a, b, (((dims[0],), (dims[1],)), ((), ())), preferred_element_type=F32
    )


def swap(x, axis):
    return lax.ppermute(x, axis, SWAP)


def across(x, distance):
    return lax.ppermute(x, "gx", [(i, i ^ distance) for i in range(4)])


def tie(*values):
    return lax.optimization_barrier(values)


def cost(microseconds):
    flops = int(microseconds * 0.6 * 1.15e9)
    return pl.CostEstimate(flops=flops, bytes_accessed=0, transcendentals=0)


def whole(array_or_space):
    return pl.BlockSpec(memory_space=array_or_space)


def params(mib):
    return pltpu.CompilerParams(vmem_limit_bytes=mib * 2**20)


def square():
    return lax.axis_size("ga") == 2


def halves(x):
    half = x.shape[0] // 32 * 16 or x.shape[0] // 2
    return x[:half], x[half:]


def send_near(x):
    return swap(x, "ga"), swap(x, "gb")


def send_far(from_x, from_y):
    return swap(halves(from_y)[0], "ga"), swap(halves(from_x)[1], "gb")


def collect(pieces, rows):
    count = len(pieces)
    starts = [0, rows, 2 * rows, 3 * rows, 3 * rows + pieces[3].shape[0]]
    shape = (4 * rows,) + pieces[0].shape[1:]

    def kernel(*refs):
        ins, (out, held, sems) = refs[:count], refs[count:]
        spots = [pl.ds(start, piece.shape[0]) for start, piece in zip(starts, pieces)]
        loads = [
            pltpu.make_async_copy(ref, held.at[spot], sems.at[0, i])
            for i, (ref, spot) in enumerate(zip(ins, spots))
        ]
        stores = [
            pltpu.make_async_copy(held.at[spot], out.at[spot], sems.at[1, i])
            for i, spot in enumerate(spots)
        ]
        for load in loads:
            load.start()
        for load, store in zip(loads, stores):
            load.wait()
            store.start()
        for store in stores:
            store.wait()

    return pl.pallas_call(
        kernel,
        out_shape=jax.ShapeDtypeStruct(shape, pieces[0].dtype),
        in_specs=[whole(pl.ANY)] * count,
        out_specs=whole(pl.ANY),
        scratch_shapes=[pltpu.VMEM(shape, pieces[0].dtype), pltpu.SemaphoreType.DMA((2, count))],
        compiler_params=params(24),
        cost_estimate=cost(4),
    )(*pieces)


def chip_slots():
    here = lax.axis_index(PLANE)
    return jnp.array([0, 2, 4, 6, 1, 3, 5, 7], jnp.int32) ^ here


def unpack(pieces, block, head_width, gain_spot, gain_rows):
    four, rows, width = pieces[0].shape
    planes = four // 4
    rest = rows - block
    small = block // planes
    count = len(pieces)
    jobs = [(i, 4 * chip + h, 4 * i + chip, h) for i in range(2) for chip in range(4) for h in range(planes)]

    def kernel(slot_ref, *refs):
        ins, (wq, wo, wkv, gains, other, sems) = refs[:count], refs[count:]
        copies = []
        for n, (i, j, at_slot, h) in enumerate(jobs):
            slot = slot_ref[at_slot]
            at = pl.ds(pl.multiple_of(slot * block, 16), block)
            to = pl.ds(h * head_width, head_width)
            parts = [
                (ins[i].at[j, pl.ds(0, block), pl.ds(0, head_width)], wq.at[at, to]),
                (ins[i].at[j, pl.ds(0, block), pl.ds(head_width, head_width)], wo.at[at, to]),
                (ins[i].at[j, pl.ds(block, rest), :], other.at[slot, h]),
            ]
            copies += [
                pltpu.make_async_copy(a, b, sems.at[n, m]) for m, (a, b) in enumerate(parts)
            ]
        for copy in copies:
            copy.start()
        for copy in copies:
            copy.wait()
        for c in range(8):
            gains[c] = other[c, 0, gain_spot : gain_spot + gain_rows, :]
        for h in range(planes):
            wkv[h * 8 * small : (h + 1) * 8 * small] = jnp.concatenate(
                [other[c, h, :small, :].astype(F32) for c in range(8)], axis=0
            ).astype(BF16)

    matrix = jax.ShapeDtypeStruct((8 * block, planes * head_width), BF16)
    return pl.pallas_call(
        kernel,
        out_shape=[
            matrix,
            matrix,
            jax.ShapeDtypeStruct((8 * block, width), BF16),
            jax.ShapeDtypeStruct((8, gain_rows, width), BF16),
        ],
        in_specs=[whole(pltpu.SMEM)] + [whole(pl.ANY)] * count,
        out_specs=[whole(pltpu.VMEM)] * 4,
        scratch_shapes=[
            pltpu.VMEM((8, planes, rest, width), BF16),
            pltpu.SemaphoreType.DMA((len(jobs), 3)),
        ],
        compiler_params=params(24),
        cost_estimate=cost(4.3),
    )(chip_slots(), *pieces)


def core_rows(ref, core, block):
    return jnp.concatenate(
        [ref[pl.ds(pl.multiple_of((2 * k + core) * block, 16), block), :] for k in range(4)],
        axis=0,
    )


def ffn_weight_grads(core, normed_t, d_ffn_t, d_gate, d_up, hidden, block):
    units = d_gate.shape[1]

    def kernel(core_ref, normed_ref, d_ffn_ref, gate_ref, up_ref, hidden_ref, out):
        m = pl.program_id(0)

        def run(left, right):
            rows = core_rows(left, core_ref[0], block)
            for n in range(0, units, 256):
                w = min(256, units - n)
                made = dot(rows, right[:, n : n + w]).astype(BF16)
                out[:, :, n : n + w] = made.reshape(4, block, w)

        for number, (left, right) in enumerate(
            ((normed_ref, gate_ref), (normed_ref, up_ref), (d_ffn_ref, hidden_ref))
        ):
            pl.when(m == number)(lambda left=left, right=right: run(left, right))

    def full(x):
        return pl.BlockSpec(x.shape, lambda m, c: (0, 0))

    ins = (normed_t, d_ffn_t, d_gate, d_up, hidden)
    return pl.pallas_call(
        kernel,
        grid_spec=pltpu.PrefetchScalarGridSpec(
            num_scalar_prefetch=1,
            grid=(3,),
            in_specs=[full(x) for x in ins],
            out_specs=pl.BlockSpec((4, block, units), lambda m, c: (0, m, 0)),
        ),
        out_shape=jax.ShapeDtypeStruct((4, 3 * block, units), BF16),
        compiler_params=params(48),
        cost_estimate=cost(6.7),
    )(core.reshape(1), *ins)


def attention_weight_grads(core, normed_t, d_query, d_attn_t, heads_low, other, block, planes):
    head_width = d_query.shape[1] // planes
    more = other.shape[1] // planes
    rows_all = block + more

    def kernel(core_ref, normed_ref, query_ref, d_attn_ref, heads_ref, other_ref, out):
        for half, (left, right) in enumerate(((normed_ref, query_ref), (d_attn_ref, heads_ref))):
            rows = core_rows(left, core_ref[0], block)
            for h in range(planes):
                made = dot(rows, right[:, h * head_width : (h + 1) * head_width]).astype(BF16)
                out[:, h * rows_all : h * rows_all + block, half * head_width : (half + 1) * head_width] = (
                    made.reshape(4, block, head_width)
                )
        for chip in range(4):
            for h in range(planes):
                out[chip, h * rows_all + block : (h + 1) * rows_all] = other_ref[
                    2 * chip + core_ref[0], h * more : (h + 1) * more
                ]

    return pl.pallas_call(
        kernel,
        out_shape=jax.ShapeDtypeStruct((4, planes * rows_all, 2 * head_width), BF16),
        in_specs=[whole(pltpu.SMEM)] + [whole(pltpu.VMEM)] * 5,
        out_specs=whole(pltpu.VMEM),
        compiler_params=params(32),
        cost_estimate=cost(2.5),
    )(core.reshape(1), normed_t, d_query, d_attn_t, heads_low, other)


class Scatter:
    def __init__(self, keep, received):
        y, x = lax.axis_index("gb"), lax.axis_index("ga")
        self.pick = lambda n: lax.dynamic_index_in_dim(keep, n, 0, keepdims=False).astype(
            F32
        ) + lax.dynamic_index_in_dim(received, n, 0, keepdims=False).astype(F32)
        self.here, self.x, self.y = 2 * y + x, 2 * y + 1 - x, 2 * (1 - y) + x
        self.far = 2 * (1 - y) + 1 - x

    def send_far(self):
        first, second = halves(self.pick(self.far).astype(BF16))
        return swap(first, "ga"), swap(second, "gb")

    def near_blocks(self, got_first, got_second):
        (x0, x1), (y0, y1) = halves(self.pick(self.x)), halves(self.pick(self.y))
        to_x = jnp.concatenate([x0, x1 + got_second.astype(F32)], axis=0)
        to_y = jnp.concatenate([y0 + got_first.astype(F32), y1], axis=0)
        return to_x.astype(BF16), to_y.astype(BF16)

    def send_near(self, got_first, got_second):
        to_x, to_y = self.near_blocks(got_first, got_second)
        return swap(to_x, "ga"), swap(to_y, "gb")

    def total(self, got_x, got_y):
        return self.pick(self.here) + got_x.astype(F32) + got_y.astype(F32)


def plane_scatter(g):
    if not square():
        return lax.psum_scatter(g, PLANE, scatter_dimension=0).astype(F32)
    c = lax.axis_index("gc")
    g = g.reshape((4, 2) + g.shape[1:])
    keep = lax.dynamic_index_in_dim(g, c, 1, keepdims=False)
    received = swap(lax.dynamic_index_in_dim(g, 1 - c, 1, keepdims=False), "gc")
    work = Scatter(keep, received)
    return work.total(*work.send_near(*work.send_far()))


GELU_A = 0.7978845608028654
GELU_B = 0.044715


def row_scale(values):
    return lax.rsqrt(jnp.mean(values * values, axis=-1, keepdims=True) + EPSILON)


def full(x):
    return pl.BlockSpec(x.shape, lambda *_: (0,) * len(x.shape))


def like(shape, dtype=F32):
    return jax.ShapeDtypeStruct(shape, dtype)


def prefetch_call(kernel, scalars, grid, ins, in_specs, outs, out_specs, scratch=(), mib=48, us=3):
    return pl.pallas_call(
        kernel,
        grid_spec=pltpu.PrefetchScalarGridSpec(
            num_scalar_prefetch=1,
            grid=grid,
            in_specs=in_specs,
            out_specs=out_specs,
            scratch_shapes=scratch,
        ),
        out_shape=outs,
        compiler_params=params(mib),
        cost_estimate=cost(us),
    )(scalars, *ins)


def flags_kernel(parents, spot):
    segments = parents.shape[0]

    def kernel(parents_ref, spot_ref, out):
        def parent_of(segment):
            found = parents_ref[jnp.maximum(segment, 0)]
            return jnp.where(segment >= 0, found, -1)

        column, plane = spot_ref[0], spot_ref[1]
        first = 4 * column
        own = first + plane

        def later(distance):
            return parent_of(jnp.minimum(own + 4 * distance, segments - 1))

        def local(segment):
            return jnp.clip(segment - first, 0, 3)

        role = lax.rem(column, 4)
        a, a1, a2 = parent_of(own), later(1), later(2)
        b, b1, b2 = parent_of(a), parent_of(a1), parent_of(a2)
        made = [
            role,
            plane,
            local(a),
            local(b),
            (a >= 0).astype(jnp.int32),
            (b >= 0).astype(jnp.int32),
            local(a1),
            local(jnp.where(role == 0, b2, a2)),
            local(b1),
        ]
        for i in range(4):
            segment, level = first + i, jnp.int32(0)
            for _ in range(5):
                segment = parent_of(segment)
                level = level + (segment >= 0).astype(jnp.int32)
            made.append(level)
        for i, value in enumerate(made):
            out[i] = value

    return pl.pallas_call(
        kernel,
        out_shape=like((13,), jnp.int32),
        in_specs=[whole(pltpu.SMEM)] * 2,
        out_specs=whole(pltpu.SMEM),
    )(parents, spot)


def key_value_kernel(flags, tokens, gain_in, wkv, gain_key, cos_table, sin_table):
    rows, width = tokens.shape
    head = wkv.shape[1] // 2
    half = head // 2

    def kernel(f, t_ref, gain_ref, w_ref, key_gain_ref, c_ref, s_ref, pairs, normed, raw, *sends):
        values = t_ref[...].astype(F32)
        low = (values * row_scale(values) * gain_ref[...]).astype(BF16)
        made = dot(low, w_ref[...])
        key = made[:, :head]
        scaled = key * row_scale(key) * key_gain_ref[...]
        pair = jnp.concatenate(
            [rotate(scaled, c_ref[...], s_ref[...]), made[:, head:]], axis=1
        ).astype(BF16)
        pairs[...] = pair
        for n in range(3):

            @pl.when(pl.program_id(0) == f[6 + n])
            def _(n=n):
                sends[n][...] = pair

        @pl.when(pl.program_id(0) == f[1])
        def _():
            normed[...] = low
            raw[...] = key

    def rows_of(x):
        return pl.BlockSpec((SEG, x), lambda i, p: (i, 0))

    return prefetch_call(
        kernel,
        flags,
        (rows // SEG,),
        (tokens, gain_in, wkv, gain_key, cos_table, sin_table),
        [rows_of(width), full(gain_in), full(wkv), full(gain_key), rows_of(half), rows_of(half)],
        [like((rows, 2 * head), BF16), like((SEG, width), BF16), like((SEG, head))]
        + [like((SEG, 2 * head), BF16)] * 3,
        [
            rows_of(2 * head),
            pl.BlockSpec((SEG, width), lambda i, p: (0, 0)),
            pl.BlockSpec((SEG, head), lambda i, p: (0, 0)),
        ]
        + [pl.BlockSpec((SEG, 2 * head), lambda i, p: (0, 0))] * 3,
        us=6,
    )


def query_kernel(plane, normed, wq, gain_query, cos_table, sin_table, head):
    width, total = wq.shape
    half = head // 2

    def kernel(plane_ref, n_ref, w_ref, gain_ref, c_ref, s_ref, query, raw):
        made = dot(n_ref[...], w_ref[...])
        raw[...] = made
        scaled = made * row_scale(made) * gain_ref[...]
        query[...] = rotate(scaled, c_ref[...], s_ref[...]).astype(BF16)

    by_head = pl.BlockSpec((SEG, head), lambda h, p: (0, h))
    table = pl.BlockSpec((SEG, half), lambda h, p: (p[0], 0))
    return prefetch_call(
        kernel,
        plane.reshape(1),
        (total // head,),
        (normed, wq, gain_query, cos_table, sin_table),
        [full(normed), pl.BlockSpec((width, head), lambda h, p: (0, h)), full(gain_query), table, table],
        [like((SEG, total), BF16), like((SEG, total))],
        [by_head, by_head],
        us=2.3,
    )


def visible_pairs(alive_a, alive_b):
    at_query = lax.broadcasted_iota(jnp.int32, (SEG, 3 * SEG), 0)
    spot = lax.broadcasted_iota(jnp.int32, (SEG, 3 * SEG), 1)
    own = (spot < SEG) & (spot <= at_query)
    above = (spot >= SEG) & (spot < 2 * SEG) & (alive_a > 0)
    top = (spot - 2 * SEG > at_query) & (alive_b > 0)
    return own | above | top


def softmax_of(query, keys, scale, alive_a, alive_b):
    scores = dot(query, keys, (1, 1)) * scale
    scores = jnp.where(visible_pairs(alive_a, alive_b), scores, MASKED)
    weights = jnp.exp(scores - jnp.max(scores, axis=-1, keepdims=True))
    return weights / jnp.sum(weights, axis=-1, keepdims=True)


def attention_kernel(flags, query, pairs, got_1, got_2, got_3):
    total = query.shape[1]
    head = pairs.shape[1] // 2

    def kernel(f, q_ref, pairs_ref, g1, g2, g3, heads, slots):
        @pl.when(pl.program_id(0) == 0)
        def _():
            role = f[0]

            def near(n):
                return pairs_ref[pl.ds(pl.multiple_of(n * SEG, SEG), SEG), :]

            slots[:SEG] = near(f[1])

            @pl.when(role == 0)
            def _():
                slots[SEG : 2 * SEG] = near(f[2])
                slots[2 * SEG :] = near(f[3])

            @pl.when(role == 1)
            def _():
                slots[SEG : 2 * SEG] = g1[...]
                slots[2 * SEG :] = g3[...]

            @pl.when(role == 2)
            def _():
                slots[SEG : 2 * SEG] = g1[...]
                slots[2 * SEG :] = g2[...]

            @pl.when(role == 3)
            def _():
                slots[SEG : 2 * SEG] = g2[...]
                slots[2 * SEG :] = g3[...]

        probs = softmax_of(q_ref[...], slots[:, :head], head**-0.5, f[4], f[5])
        heads[...] = dot(probs.astype(BF16), slots[:, head:]).astype(BF16)

    by_head = pl.BlockSpec((SEG, head), lambda h, f: (0, h))
    ins = (query, pairs, got_1, got_2, got_3)
    return prefetch_call(
        kernel,
        flags,
        (total // head,),
        ins,
        [by_head] + [full(x) for x in ins[1:]],
        [like((SEG, total), BF16), like((3 * SEG, 2 * head), BF16)],
        [by_head, pl.BlockSpec((3 * SEG, 2 * head), lambda h, f: (0, 0))],
        us=5.4,
    )


def middle_kernel(plane, heads_own, heads_got, wo_t, tokens, gain_post, gain_ffn):
    width, total = wo_t.shape

    def kernel(p, own, got, w_ref, t_ref, post_ref, gain_ref, attn, mid, normed):
        i = pl.program_id(0)

        def run(heads):
            made = dot(heads[...], w_ref[...], (1, 1))

            @pl.when(i == 0)
            def _():
                attn[...] = made

            middle = t_ref[...].astype(F32) + made * row_scale(made) * post_ref[...]
            mid[...] = middle
            normed[...] = (middle * row_scale(middle) * gain_ref[...]).astype(BF16)

        pl.when(i == 0)(lambda: run(own))
        pl.when(i == 1)(lambda: run(got))

    rows = pl.BlockSpec((SEG, width), lambda i, p: (i, 0))
    return prefetch_call(
        kernel,
        plane.reshape(1),
        (2,),
        (heads_own, heads_got, wo_t, tokens, gain_post, gain_ffn),
        [
            full(heads_own),
            full(heads_got),
            full(wo_t),
            pl.BlockSpec((SEG, width), lambda i, p: (p[0] ^ i, 0)),
            full(gain_post),
            full(gain_ffn),
        ],
        [like((SEG, width)), like((2 * SEG, width)), like((2 * SEG, width), BF16)],
        [pl.BlockSpec((SEG, width), lambda i, p: (0, 0)), rows, rows],
        us=4.5,
    )


def both_cores(pieces):
    return pieces + [(swap(piece, "gc"), row, slot + 1) for piece, row, slot in pieces]


class Blocks:
    def __init__(self, pieces, block):
        self.jobs = []
        if block is None:
            self.pieces = tuple(pieces)
            self.width, self.units = pieces[0].shape
            self.slots = jnp.zeros((1,), jnp.int32)
            self.jobs = [(m, 0, m, 0, self.width, None) for m in range(3)]
            return
        self.pieces = tuple(piece for piece, _, _ in pieces)
        self.units = self.pieces[0].shape[1]
        self.width = 8 * block
        here = lax.axis_index(PLANE)
        self.slots = jnp.array([slot for _, _, slot in pieces], jnp.int32)
        self.slots = (self.slots ^ here) * block
        for i, (piece, start, _) in enumerate(pieces):
            for m in range(3):
                low, high = max(start, m * block), min(start + piece.shape[0], (m + 1) * block)
                if low < high:
                    self.jobs.append((i, low - start, m, low - m * block, high - low, i))

    @classmethod
    def collected(cls, own, other, block):
        made = cls([(own, 0, 0), (other, 0, 1)], block)
        here = lax.axis_index(PLANE)
        made.slots = chip_slots() * block
        made.jobs = [
            (i, (3 * chip + m) * block, m, 0, block, 4 * i + chip)
            for i in range(2)
            for chip in range(4)
            for m in range(3)
        ]
        return made

    def scratch(self):
        return [
            pltpu.VMEM((3, self.width, self.units), BF16),
            pltpu.SemaphoreType.DMA((len(self.jobs),)),
        ]

    def copies(self, slots, refs, held, sems, matrix):
        made = []
        for n, (i, source, m, to, rows, slot) in enumerate(self.jobs):
            if m == matrix:
                base = 0 if slot is None else pl.multiple_of(slots[slot], 16)
                made.append(
                    pltpu.make_async_copy(
                        refs[i].at[pl.ds(source, rows)],
                        held.at[m, pl.ds(base + to, rows)],
                        sems.at[n],
                    )
                )
        return made


def ffn_forward_kernel(blocks, normed, part):
    rows, width = normed.shape
    units = blocks.units
    count = len(blocks.pieces)
    first = part is None

    def kernel(slots, n_ref, *refs):
        if not first:
            part_ref, refs = refs[0], refs[1:]
        pieces, (act, slope, hidden, out, held, sems) = refs[:count], refs[count:]
        start = pl.program_id(0) == 0

        def wait(m):
            @pl.when(start)
            def _():
                for copy in blocks.copies(slots, pieces, held, sems, m):
                    copy.wait()

        @pl.when(start)
        def _():
            for m in range(3):
                for copy in blocks.copies(slots, pieces, held, sems, m):
                    copy.start()

        left = n_ref[...]
        wait(0)
        gate = dot(left, held[0])
        wait(1)
        up = dot(left, held[1])
        square_gate = gate * gate
        turn = jnp.tanh(GELU_A * (gate + GELU_B * gate * square_gate))
        spread = 0.5 * (1.0 + turn)
        gelu = gate * spread
        bend = spread + 0.5 * gate * (1.0 - turn * turn) * (
            GELU_A * (1.0 + 3.0 * GELU_B * square_gate)
        )
        act[...] = gelu.astype(BF16)
        slope[...] = (up * bend).astype(BF16)
        low = (gelu * up).astype(BF16)
        hidden[...] = low
        wait(2)
        made = dot(low, held[2], (1, 1))
        out[...] = made if first else part_ref[...] + made

    by_rows = pl.BlockSpec((SEG, width), lambda i, s: (i, 0))
    by_units = pl.BlockSpec((SEG, units), lambda i, s: (i, 0))
    return prefetch_call(
        kernel,
        blocks.slots,
        (rows // SEG,),
        (normed,) + (() if first else (part,)) + blocks.pieces,
        [by_rows] + ([] if first else [by_rows]) + [whole(pl.ANY)] * count,
        [like((rows, units), BF16)] * 3 + [like((rows, width))],
        [by_units] * 3 + [by_rows],
        blocks.scratch(),
        mib=58,
        us=16,
    )


def ffn_backward_kernel(blocks, d_ffn, act, slope, back):
    rows, width = d_ffn.shape
    units = blocks.units
    count = len(blocks.pieces)
    first = back is None

    def kernel(slots, d_ref, act_ref, slope_ref, *refs):
        if not first:
            back_ref, refs = refs[0], refs[1:]
        pieces, (d_gate, d_up, out, held, sems) = refs[:count], refs[count:]
        start = pl.program_id(0) == 0

        def wait(m):
            @pl.when(start)
            def _():
                for copy in blocks.copies(slots, pieces, held, sems, m):
                    copy.wait()

        @pl.when(start)
        def _():
            for m in (2, 0, 1):
                for copy in blocks.copies(slots, pieces, held, sems, m):
                    copy.start()

        wait(2)
        d_hidden = dot(d_ref[...], held[2])
        to_gate = (d_hidden * slope_ref[...].astype(F32)).astype(BF16)
        to_up = (d_hidden * act_ref[...].astype(F32)).astype(BF16)
        d_gate[...] = to_gate
        d_up[...] = to_up
        wait(0)
        wait(1)
        made = dot(to_gate, held[0], (1, 1)) + dot(to_up, held[1], (1, 1))
        out[...] = made if first else back_ref[...] + made

    by_rows = pl.BlockSpec((SEG, width), lambda i, s: (i, 0))
    by_units = pl.BlockSpec((SEG, units), lambda i, s: (i, 0))
    return prefetch_call(
        kernel,
        blocks.slots,
        (rows // SEG,),
        (d_ffn, act, slope) + (() if first else (back,)) + blocks.pieces,
        [by_rows, by_units, by_units] + ([] if first else [by_rows]) + [whole(pl.ANY)] * count,
        [like((rows, units), BF16)] * 2 + [like((rows, width))],
        [by_units] * 2 + [by_rows],
        blocks.scratch(),
        mib=58,
        us=16,
    )


def ffn_end_kernel(plane, ffn_own, ffn_other, mid, cotangent, gain):
    rows, width = mid.shape

    def kernel(p, own_ref, other_ref, mid_ref, up_ref, gain_ref, d_out, d_turned, out, share):
        i = pl.program_id(0)
        g = gain_ref[...]

        def run(ref, own):
            ffn = ref[...].astype(F32)
            r = row_scale(ffn)
            incoming = up_ref[...].astype(F32)
            out[...] = (mid_ref[...] + ffn * r * g).astype(BF16)
            if own:
                share[...] = jnp.sum(incoming * ffn * r, axis=0, keepdims=True)
            scaled = g * incoming
            inner = jnp.mean(ffn * scaled, axis=-1, keepdims=True)
            made = (r * scaled - ffn * (r * r * r) * inner).astype(BF16)
            d_out[...] = made
            d_turned[...] = made.T

        pl.when(i == 0)(lambda: run(own_ref, True))
        pl.when(i == 1)(lambda: run(other_ref, False))

    once = pl.BlockSpec((SEG, width), lambda i, p: (0, 0))
    by_rows = pl.BlockSpec((SEG, width), lambda i, p: (i, 0))
    return prefetch_call(
        kernel,
        plane.reshape(1),
        (2,),
        (ffn_own, ffn_other, mid, cotangent, gain),
        [once, once, by_rows, pl.BlockSpec((SEG, width), lambda i, p: (p[0] ^ i, 0)), full(gain)],
        [like((rows, width), BF16), like((width, rows), BF16), like((rows, width), BF16), like((1, width))],
        [
            by_rows,
            pl.BlockSpec((width, SEG), lambda i, p: (0, i)),
            by_rows,
            pl.BlockSpec((1, width), lambda i, p: (0, 0)),
        ],
        us=3.4,
    )


def spread_kernel(plane, blocks, order, dtype):
    width = blocks[0].shape[1]
    count = len(blocks)
    spots = [(n, r) for n, x in enumerate(blocks) for r in range(x.shape[0] // SEG)]

    def kernel(p, *refs):
        ins, out = refs[:count], refs[count]
        for i, (n, r) in enumerate(spots):

            @pl.when(pl.program_id(0) == p[0] ^ order[i])
            def _(n=n, r=r):
                out[...] = ins[n][r * SEG : (r + 1) * SEG].astype(dtype)

    return prefetch_call(
        kernel,
        plane.reshape(1),
        (4,),
        tuple(blocks),
        [full(x) for x in blocks],
        like((4 * SEG, width), dtype),
        pl.BlockSpec((SEG, width), lambda i, p: (i, 0)),
        us=3,
    )


def attention_back_kernel(
    flags, back, got, mid, cotangent, gain_ffn, attn, gain_post, wo_t, query, query_raw, gain_query,
    slots, cos_table, sin_table, head,
):
    width, total = wo_t.shape
    heads = total // head
    half = head // 2
    scale = head**-0.5

    def kernel(
        f, back_ref, got_ref, mid_ref, up_ref, gain_ffn_ref, attn_ref, gain_post_ref, w_ref, q_ref,
        raw_ref, gain_query_ref, slots_ref, c_ref, s_ref,
        d_mid, d_attn, d_attn_turned, shares, d_query, query_share, d_self, d_a, d_b, sums,
    ):
        h = pl.program_id(0)

        @pl.when(h == 0)
        def _():
            incoming = back_ref[...] + got_ref[...].astype(F32)
            add, share = norm_back(mid_ref[...], gain_ffn_ref[...], incoming)
            made = up_ref[...].astype(F32) + add
            d_mid[...] = made
            d_a_low, share_post = norm_back(attn_ref[...], gain_post_ref[...], made)
            low = d_a_low.astype(BF16)
            d_attn[...] = low
            d_attn_turned[...] = low.T
            shares[0:1, :] = jnp.sum(share, axis=0, keepdims=True)
            shares[1:2, :] = jnp.sum(share_post, axis=0, keepdims=True)
            sums[...] = jnp.zeros_like(sums)
            query_share[...] = jnp.zeros_like(query_share)

        keys, values = slots_ref[:, :head], slots_ref[:, head:]
        q = q_ref[...]
        d_heads = dot(d_attn[...], w_ref[...]).astype(BF16)
        probs = softmax_of(q, keys, scale, f[4], f[5])
        d_probs = dot(d_heads, values, (1, 1))
        d_scores = probs * (d_probs - jnp.sum(d_probs * probs, axis=-1, keepdims=True))
        d_scores = d_scores.astype(BF16)
        sums[:, :head] += dot(d_scores, q, (0, 0))
        sums[:, head:] += dot(probs.astype(BF16), d_heads, (0, 0))
        turned = rotate(dot(d_scores, keys) * scale, c_ref[...], -s_ref[...])
        made, share = norm_back(raw_ref[...], gain_query_ref[...], turned)
        d_query[...] = made.astype(BF16)
        query_share[...] += jnp.sum(share, axis=0, keepdims=True)

        @pl.when(h == heads - 1)
        def _():
            sums[:, :head] = sums[:, :head] * scale
            d_self[...] = sums[:SEG]
            d_a[...] = sums[SEG : 2 * SEG].astype(BF16)
            d_b[...] = sums[2 * SEG :].astype(BF16)

    def once(shape):
        return pl.BlockSpec(shape, lambda h, f: (0,) * len(shape))

    by_head = pl.BlockSpec((SEG, head), lambda h, f: (0, h))
    table = pl.BlockSpec((SEG, half), lambda h, f: (f[1], 0))
    rows = once((SEG, width))
    return prefetch_call(
        kernel,
        flags,
        (heads,),
        (back, got, mid, cotangent, gain_ffn, attn, gain_post, wo_t, query, query_raw, gain_query,
         slots, cos_table, sin_table),
        [
            rows,
            rows,
            rows,
            pl.BlockSpec((SEG, width), lambda h, f: (f[1], 0)),
            full(gain_ffn),
            rows,
            full(gain_post),
            pl.BlockSpec((width, head), lambda h, f: (0, h)),
            by_head,
            by_head,
            full(gain_query),
            full(slots),
            table,
            table,
        ],
        [
            like((SEG, width)),
            like((SEG, width), BF16),
            like((width, SEG), BF16),
            like((2, width)),
            like((SEG, total), BF16),
            like((1, head)),
            like((SEG, 2 * head)),
            like((SEG, 2 * head), BF16),
            like((SEG, 2 * head), BF16),
        ],
        [
            rows,
            rows,
            once((width, SEG)),
            once((2, width)),
            by_head,
            once((1, head)),
            once((SEG, 2 * head)),
            once((SEG, 2 * head)),
            once((SEG, 2 * head)),
        ],
        [pltpu.VMEM((3 * SEG, 2 * head), F32)],
        us=12,
    )


def tokens_back_kernel(
    plane, terms, key_raw, gain_key, cos_table, sin_table, wkv, d_normed, d_mid, tokens, gain_in
):
    width = d_mid.shape[1]
    head = key_raw.shape[1]
    half = head // 2
    count = len(terms)

    def kernel(p, *refs):
        terms_in, refs = refs[:count], refs[count:]
        (raw_ref, gain_ref, c_ref, s_ref, w_ref, dn_ref, mid_ref, t_ref, gain_in_ref) = refs[:9]
        d_kv, rows_out, share_key, share_in = refs[9:]
        total = terms_in[0][...].astype(F32)
        for term in terms_in[1:]:
            total = total + term[...].astype(F32)
        turned = rotate(total[:, :head], c_ref[...], -s_ref[...])
        made, share = norm_back(raw_ref[...], gain_ref[...], turned)
        share_key[...] = jnp.sum(share, axis=0, keepdims=True)
        low = jnp.concatenate([made, total[:, head:]], axis=1).astype(BF16)
        d_kv[...] = low
        incoming = dn_ref[...] + dot(low, w_ref[...], (1, 1))
        add, share = norm_back(t_ref[...].astype(F32), gain_in_ref[...], incoming)
        share_in[...] = jnp.sum(share, axis=0, keepdims=True)
        rows_out[...] = (mid_ref[...] + add).astype(BF16)

    table = pl.BlockSpec((SEG, half), lambda i, p: (p[0], 0))
    ins = (*terms, key_raw, gain_key, cos_table, sin_table, wkv, d_normed, d_mid, tokens, gain_in)
    specs = [full(x) for x in ins]
    specs[count + 2] = specs[count + 3] = table
    specs[count + 7] = pl.BlockSpec((SEG, width), lambda i, p: (p[0], 0))
    outs = [like((SEG, 2 * head), BF16), like((SEG, width), BF16), like((1, head)), like((1, width))]
    return prefetch_call(
        kernel, plane.reshape(1), (1,), ins, specs, outs, [full(o) for o in outs], us=3
    )


def window_kernel(flags, d_self, d_a, d_b, back_1, back_2, back_3):
    shape = (2,) + d_self.shape

    def kernel(f, own_ref, a_ref, b_ref, b1, b2, b3, sent, kept):
        role, plane = f[0], f[1]
        near = role == 0
        ats = [
            plane,
            jnp.where(near & (f[4] > 0), f[2], -1),
            jnp.where(near & (f[5] > 0), f[3], -1),
            jnp.where(role <= 1, f[6], -1),
            jnp.where(role <= 1, f[7], -1),
            jnp.where(near, f[8], -1),
        ]
        refs = (own_ref, a_ref, b_ref, b1, b2, b3)
        for out, k, other in ((sent, 0, 1), (sent, 1, 3), (kept, 0, 0), (kept, 1, 2)):
            number = plane ^ other
            total = jnp.zeros(out.shape[1:], F32)
            for at, ref in zip(ats, refs):
                total = total + jnp.where(at == number, ref[...].astype(F32), 0.0)
            out[k] = total.astype(BF16)

    return pl.pallas_call(
        kernel,
        out_shape=[like(shape, BF16)] * 2,
        in_specs=[whole(pltpu.SMEM)] + [whole(pltpu.VMEM)] * 6,
        out_specs=[whole(pltpu.VMEM)] * 2,
        compiler_params=params(32),
        cost_estimate=cost(2.4),
    )(flags, d_self, d_a, d_b, back_1, back_2, back_3)


def z_first(sent, kept, kept_far):
    got = across(sent, 1).astype(F32)
    return tie((kept.astype(F32) + got[0]).astype(BF16), (kept_far.astype(F32) + got[1]).astype(BF16))


def z_halve(x):
    here = lax.axis_index("gx")

    def at(n):
        return lax.dynamic_index_in_dim(x, n, 0, keepdims=False)

    return z_first(jnp.stack([at(here ^ 1), at(here ^ 3)]), at(here), at(here ^ 2))


def body(
    tokens,
    parents,
    w_query,
    w_key,
    w_value,
    w_out,
    w_gate,
    w_up,
    w_down,
    g_attn_in,
    g_attn_out,
    g_ffn_in,
    g_ffn_out,
    g_query,
    g_key,
    cotangent,
):
    column = lax.axis_index(PLANE)
    columns = lax.axis_size(PLANE)
    plane = lax.axis_index("gx")
    planes = lax.axis_size("gx")
    width = tokens.shape[1]
    head_width = w_key.shape[1]
    heads = planes * w_query.shape[1] // head_width
    block, small = w_query.shape[0], w_key.shape[0]
    gains_len = 4 * block + 2 * g_query.shape[0]
    pack_width = 2 * head_width
    gain_rows = -(-gains_len // pack_width)
    used = small + gain_rows
    gain_spot = -(-small // 8) * 8
    pack_rows = -(-(block + gain_spot + gain_rows) // 16) * 16

    core = lax.axis_index("gc")
    down_t = w_down.T
    ffn_mine = jnp.concatenate([w_gate, w_up, down_t], axis=0)
    gains = jnp.concatenate([g_attn_in, g_attn_out, g_ffn_in, g_ffn_out, g_query, g_key])
    gains = jnp.pad(gains, (0, gain_rows * pack_width - gains_len)).reshape(gain_rows, pack_width)
    pack = jnp.concatenate(
        [
            jnp.concatenate([w_query, w_out.T], axis=1),
            jnp.concatenate([w_key, w_value], axis=1),
            jnp.zeros((gain_spot - small, pack_width), BF16),
            gains,
            jnp.zeros((pack_rows - block - gain_spot - gain_rows, pack_width), BF16),
        ],
        axis=0,
    )
    flags = flags_kernel(parents, jnp.stack([column, plane]).astype(jnp.int32))
    depth = flags[9:13, None] * SEG + jnp.arange(SEG, dtype=jnp.int32)[None, :]
    half_width = head_width // 2
    rates = 10000.0 ** (-jnp.arange(half_width, dtype=F32) / half_width)
    turned = depth.reshape(-1).astype(F32)[:, None] * rates[None, :]
    cos_table, sin_table = jnp.cos(turned), jnp.sin(turned)
    if square():
        ffn_x, ffn_y = send_near(ffn_mine)
        pack = lax.all_gather(pack, "gx", axis=0)
        pack, other_gate = tie(pack, w_gate)
        their_gate = across(other_gate, 2)
        pack_x, pack_y = send_near(pack)
        ffn_x, ffn_y, pack, pack_x, pack_y, cos_table, sin_table = tie(
            ffn_x, ffn_y, pack, pack_x, pack_y, cos_table, sin_table
        )
        pack_far = send_far(pack_x, pack_y)
        ffn_far = send_far(ffn_x, ffn_y)
        *pack_far, their_gate, other_up, other_down = tie(*pack_far, their_gate, w_up, down_t)
        their_up, their_down = across(other_up, 2), across(other_down, 2)
        pack_all = collect((pack, pack_x, pack_y, *pack_far), planes)
        pack_other = swap(pack_all, "gc")
        wq, wo_t, wkv, gains = unpack(
            [pack_all, pack_other], block, head_width, gain_spot, gain_rows
        )
    else:
        pack = lax.all_gather(pack, "gx", axis=0, tiled=True)
        pack = lax.all_gather(pack, PLANE, axis=0).reshape(columns, planes, pack_rows, pack_width)

        def from_blocks(blocks):
            return blocks.transpose(0, 2, 1, 3).reshape(columns * block, -1)

        wq = from_blocks(pack[:, :, :block, :head_width])
        wo_t = from_blocks(pack[:, :, :block, head_width:])
        wkv = pack[:, :, block : block + small].transpose(1, 0, 2, 3).reshape(width, pack_width)
        gains = pack[:, 0, block + gain_spot : block + gain_spot + gain_rows]

        def ffn_weights(mine):
            stacked = lax.all_gather(mine, PLANE, axis=0).reshape(columns, 3, block, -1)
            return Blocks([stacked[:, i].reshape(width, -1) for i in range(3)], None)

        quarter_mine = ffn_weights(ffn_mine)
        quarter_theirs = ffn_weights(across(ffn_mine, 2))

    gains = gains.reshape(columns, -1)[:, :gains_len].astype(F32)
    gain_in, gain_post, gain_ffn, gain_last = [
        gains[:, i * block : (i + 1) * block].reshape(1, -1) for i in range(4)
    ]
    gain_query, gain_key = [
        gains[:, 4 * block + i * g_query.shape[0] :][:, : g_query.shape[0]].reshape(1, -1)
        for i in range(2)
    ]

    role = column % 4
    trees = range(columns // 4)
    route_1 = [(4 * t + i, 4 * t + i + 1) for t in trees for i in (0, 1)]
    route_2 = [(4 * t + i, 4 * t + i + 2) for t in trees for i in (0, 1)]
    route_3 = [(4 * t + i, 4 * t + i + 1) for t in trees for i in (0, 2)]

    def send(x, route):
        return lax.ppermute(x, PLANE, route)

    def send_back(x, route):
        return lax.ppermute(x, PLANE, [(b, a) for a, b in route])

    pairs, normed_own, key_raw, send_1, send_2, send_3 = key_value_kernel(
        flags, tokens, gain_in, wkv, gain_key, cos_table, sin_table
    )
    if square():
        send_1, send_2, *ffn_far = tie(send_1, send_2, *ffn_far)
    got_1 = send(send_1, route_1)
    got_2 = send(send_2, route_2)
    query, query_raw = query_kernel(
        plane, normed_own, wq, gain_query, cos_table, sin_table, head_width
    )
    if square():
        query, ffn_x, ffn_y, *ffn_far = tie(query, ffn_x, ffn_y, *ffn_far)
        mine_all = collect((ffn_mine, ffn_x, ffn_y, *ffn_far), 3 * block)
        got_1, got_2, mine_all, their_up, their_down = tie(
            got_1, got_2, mine_all, their_up, their_down
        )
        mine_other = swap(mine_all, "gc")
        theirs = jnp.concatenate([their_gate, their_up, their_down], axis=0)
        their_x, their_y = send_near(theirs)
    got_3 = send(jnp.where(role == 2, got_2, send_3), route_3)
    heads_low, slots = attention_kernel(flags, query, pairs, got_1, got_2, got_3)

    if square():
        heads_low, mine_other = tie(heads_low, mine_other)
        heads_got = across(heads_low, 1)
        quarter_mine = Blocks.collected(mine_all, mine_other, block)
    else:
        heads_got = across(heads_low, 1)
    attn, mid, normed_ffn = middle_kernel(
        plane, heads_low, heads_got, wo_t, tokens, gain_post, gain_ffn
    )
    if square():
        normed_ffn, their_x, their_y = tie(normed_ffn, their_x, their_y)
        their_far = send_far(their_x, their_y)
        quarter_theirs = Blocks(
            both_cores(
                [
                    (theirs, 0, 0),
                    (their_x, 0, 2),
                    (their_y, 0, 4),
                    (their_far[0], 0, 6),
                    (their_far[1], their_far[0].shape[0], 6),
                ]
            ),
            block,
        )
    act_m, slope_m, hidden_m, ffn_part = ffn_forward_kernel(quarter_mine, normed_ffn, None)
    act_t, slope_t, hidden_t, ffn_part = ffn_forward_kernel(quarter_theirs, normed_ffn, ffn_part)
    ffn_got = across(ffn_part[SEG:].astype(BF16), 1)
    ffn_own = (ffn_part[:SEG] + ffn_got.astype(F32)).astype(BF16)
    ffn_other = across(ffn_own, 1)
    d_ffn_low, d_ffn_t, output, d_gain_last = ffn_end_kernel(
        plane, ffn_own, ffn_other, mid, cotangent, gain_last
    )

    output_far = [across(output[:SEG], 2)]
    d_gate_t, d_up_t, back = ffn_backward_kernel(quarter_theirs, d_ffn_low, act_t, slope_t, None)
    if square():
        lefts = (normed_ffn.T, d_ffn_t)
        send_theirs = ffn_weight_grads(1 - core, *lefts, d_gate_t, d_up_t, hidden_t, block)
        back, send_theirs, output_far[0] = tie(back, send_theirs, output_far[0])
        recv_theirs = swap(send_theirs, "gc")
    d_gate_m, d_up_m, back = ffn_backward_kernel(quarter_mine, d_ffn_low, act_m, slope_m, back)
    back, d_gate_t = tie(back, d_gate_t)
    back_got = across(back[SEG:].astype(BF16), 1)
    if square():
        keep_theirs = ffn_weight_grads(core, *lefts, d_gate_t, d_up_t, hidden_t, block)
        back_got, recv_theirs, keep_theirs, output = tie(
            back_got, recv_theirs, keep_theirs, output
        )
        theirs_far = Scatter(keep_theirs, recv_theirs).send_far()
    else:
        grads = []
        for d_gate, d_up, hidden in ((d_gate_m, d_up_m, hidden_m), (d_gate_t, d_up_t, hidden_t)):
            blocks = [
                dot(normed_ffn, d_gate, (0, 0)),
                dot(normed_ffn, d_up, (0, 0)),
                dot(d_ffn_low, hidden, (0, 0)),
            ]
            blocks = [m.astype(BF16).reshape(columns, block, -1) for m in blocks]
            grads.append(plane_scatter(jnp.concatenate(blocks, axis=1)))
        ffn_grad = grads[0] + across(grads[1].astype(BF16), 2).astype(F32)

    output_far.append(across(output[SEG : SEG + SEG // 2], 2))

    (
        d_mid, d_attn_low, d_attn_t, d_gains_mid, d_query_low, d_gain_query, d_self, d_a, d_b,
    ) = attention_back_kernel(
        flags, back, back_got, mid, cotangent, gain_ffn, attn, gain_post, wo_t, query, query_raw,
        gain_query, slots, cos_table, sin_table, head_width,
    )
    if square():
        d_a, d_b, output_far[1], output = tie(d_a, d_b, output_far[1], output)
    output_far.append(across(output[SEG + SEG // 2 :], 2))
    back_1 = send_back(d_a, route_1)
    back_3 = send_back(d_b, route_3)
    if square():
        d_a, d_b, back_1, back_3, *theirs_far = tie(d_a, d_b, back_1, back_3, *theirs_far)
    d_b_far = jnp.where(role == 2, d_b.astype(F32) + back_3.astype(F32), 0.0).astype(BF16)
    to_back_2 = jnp.where(role == 3, d_a, d_b_far)
    if square():
        to_back_2, keep_theirs, recv_theirs, d_gate_m, *theirs_far = tie(
            to_back_2, keep_theirs, recv_theirs, d_gate_m, *theirs_far
        )
    back_2 = send_back(to_back_2, route_2)
    if square():
        to_near = Scatter(keep_theirs, recv_theirs).near_blocks(*theirs_far)
        made = (*lefts, d_gate_m, d_up_m, hidden_m)
        send_mine = ffn_weight_grads(1 - core, *made, block)
        back_2, output_far[2], send_mine, *to_near = tie(
            back_2, output_far[2], send_mine, *to_near
        )
        recv_mine = swap(send_mine, "gc")
        half = to_near[0].shape[0] // 32 * 16

        near_first = swap(to_near[0][:half], "ga"), swap(to_near[1][:half], "gb")
    sent, kept = window_kernel(flags, d_self, d_a, d_b, back_1, back_2, back_3)
    kept, passed = z_first(sent, kept[0], kept[1])
    if square():
        keep_mine = ffn_weight_grads(core, *made, block)
        passed, keep_mine, recv_mine, *near = tie(passed, keep_mine, recv_mine, *near_first, *to_near)
        near_first = near[:2]
        near_second = swap(near[2][half:], "ga"), swap(near[3][half:], "gb")
    d_normed_query = dot(d_query_low, wq, (1, 1))
    own_terms = [kept, across(passed, 2)]
    if square():
        own_terms[1], keep_theirs, recv_theirs, *near = tie(
            own_terms[1], keep_theirs, recv_theirs, *near_first, *near_second
        )
        theirs_near = [jnp.concatenate([near[i], near[i + 2]], axis=0) for i in range(2)]
        theirs_sum = Scatter(keep_theirs, recv_theirs).total(*theirs_near).astype(BF16)
        gate_sum = across(theirs_sum[:block], 2)
        mine_far = Scatter(keep_mine, recv_mine).send_far()
        theirs_sum = Scatter(keep_theirs, recv_theirs).total(*theirs_near).astype(BF16)
        gate_sum = across(theirs_sum[:block], 2)
    d_kv_low, token_rows, d_gain_key, d_gain_in = tokens_back_kernel(
        plane, own_terms, key_raw, gain_key, cos_table, sin_table, wkv, d_normed_query, d_mid,
        tokens, gain_in,
    )
    tokens_far = across(token_rows, 2)

    grad_kv = dot(normed_own, d_kv_low, (0, 0)).astype(BF16)
    grad_kv = grad_kv.reshape(planes, columns, small, -1).transpose(1, 0, 2, 3)
    gain_sums = [
        d_gain_in,
        d_gains_mid[1:],
        d_gains_mid[:1],
        d_gain_last,
        d_gain_query,
        d_gain_key,
    ]
    gain_sums = jnp.concatenate([g.reshape(columns, -1) for g in gain_sums], axis=1).astype(BF16)
    gain_sums = jnp.pad(gain_sums, ((0, 0), (0, gain_rows * pack_width - gains_len)))
    gain_sums = jnp.broadcast_to(
        gain_sums.reshape(columns, 1, gain_rows, pack_width),
        (columns, planes, gain_rows, pack_width),
    )
    rest_rows = pack_rows - block
    rest = jnp.concatenate(
        [grad_kv, gain_sums, jnp.zeros((columns, planes, pack_rows - block - used, pack_width), BF16)],
        axis=2,
    ).reshape(columns, planes * rest_rows, pack_width)
    if square():
        attn_lefts = (normed_own.T, d_query_low, d_attn_t, heads_low, rest)
        attn_send = attention_weight_grads(1 - core, *attn_lefts, block, planes)
        attn_keep = attention_weight_grads(core, *attn_lefts, block, planes)
        attn_received = swap(attn_send, "gc")
        gate_sum, other_up, attn_keep, attn_received, keep_mine, recv_mine, *mine_far = tie(
            gate_sum, theirs_sum[block : 2 * block], attn_keep, attn_received, keep_mine, recv_mine,
            *mine_far,
        )
        attn_far = Scatter(attn_keep, attn_received).send_far()
        tokens_far, other_down, attn_keep, attn_received, *attn_far = tie(
            tokens_far, theirs_sum[2 * block :], attn_keep, attn_received, *attn_far
        )
        attn_work = Scatter(attn_keep, attn_received)
        attn_near = attn_work.send_near(*attn_far)
        up_sum = across(other_up, 2)
        tokens_near = across(jnp.concatenate([token_rows, tokens_far], axis=0), 1)
        up_sum, keep_mine, recv_mine, *attn_near = tie(up_sum, keep_mine, recv_mine, *attn_near)
        mine = Scatter(keep_mine, recv_mine)
        mine_near = mine.send_near(*mine_far)
        down_sum = across(other_down, 2)
        grads = attn_work.total(*attn_near)
    else:

        def to_blocks(grad):
            return grad.astype(BF16).reshape(columns, block, planes, -1).transpose(0, 2, 1, 3)

        grads = jnp.concatenate(
            [
                to_blocks(dot(normed_own, d_query_low, (0, 0))),
                to_blocks(dot(d_attn_low, heads_low, (0, 0))),
            ],
            axis=3,
        ).reshape(columns, planes * block, pack_width)
        grads = jnp.concatenate(
            [grads.reshape(columns, planes, block, -1), rest.reshape(columns, planes, rest_rows, -1)],
            axis=2,
        ).reshape(columns, planes * pack_rows, pack_width)
        grads = plane_scatter(grads)
    grads = grads.reshape(planes, pack_rows, pack_width)
    rest = jnp.broadcast_to(
        grads[:1, block + small :], (planes, pack_rows - block - small, pack_width)
    )
    grads = jnp.concatenate([grads[:, : block + small], rest], axis=1).astype(BF16)
    kept, passed = z_halve(grads)
    if square():
        passed, down_sum = tie(passed, down_sum)
    else:
        tokens_near = across(jnp.concatenate([token_rows, tokens_far], axis=0), 1)
    grads = kept.astype(F32) + across(passed, 2).astype(F32)
    if square():
        ffn_grad = mine.total(*mine_near) + jnp.concatenate(
            [gate_sum, up_sum, down_sum], axis=0
        ).astype(F32)
    grad_tokens = spread_kernel(plane, (token_rows, tokens_far, tokens_near), (0, 2, 1, 3), F32)
    output_far[1:] = [jnp.concatenate(output_far[1:], axis=0)]
    output = spread_kernel(plane, (output, *output_far), (0, 1, 2, 3), BF16)
    gain_grads = grads[block + small : block + used].reshape(-1)
    return (
        output,
        grad_tokens,
        gain_grads[:block],
        gain_grads[block : 2 * block],
        gain_grads[2 * block : 3 * block],
        gain_grads[3 * block : 4 * block],
        gain_grads[4 * block : 4 * block + g_query.shape[0]],
        gain_grads[4 * block + g_query.shape[0] : gains_len],
        grads[:block, :head_width],
        grads[block : block + small, :head_width],
        grads[block : block + small, head_width:],
        grads[:block, head_width:].T,
        ffn_grad[:block],
        ffn_grad[block : 2 * block],
        ffn_grad[2 * block :].T,
    )


def solution(mesh):
    side = math.isqrt(mesh.shape["gy"] // 2)
    split = Mesh(mesh.devices.reshape(mesh.shape["gx"], side, side, 2), ("gx",) + PLANE)
    whole = ("gx",) + PLANE
    return jax.shard_map(
        body,
        mesh=split,
        in_specs=(
            P(PLANE, None),
            P(),
            P(PLANE, "gx"),
            P(whole, None),
            P(whole, None),
            P("gx", PLANE),
            P(PLANE, "gx"),
            P(PLANE, "gx"),
            P("gx", PLANE),
            P(PLANE),
            P(PLANE),
            P(PLANE),
            P(PLANE),
            P(PLANE),
            P(PLANE),
            P(PLANE, None),
        ),
        out_specs=(
            P(PLANE, None),
            P(PLANE, None),
            P(PLANE),
            P(PLANE),
            P(PLANE),
            P(PLANE),
            P(PLANE),
            P(PLANE),
            P(PLANE, "gx"),
            P(whole, None),
            P(whole, None),
            P("gx", PLANE),
            P(PLANE, "gx"),
            P(PLANE, "gx"),
            P("gx", PLANE),
        ),
        check_vma=False,
    )
```

time: 817 us -> 604 us (0.74)
  Pallas kernels: 17.5 us -> 147 us
  matrix products: 99.9 us -> 2.39 us
  local copies, waits for them, and re-layouts: 160 us -> 70 us
  blocking collectives: 103 us -> 20.1 us
  other arithmetic: 117 us -> 40 us
  between operations: 33.1 us -> 2.57 us
  waiting for transfers between devices: 227 us -> 251 us
  starting transfers between devices: 48.4 us -> 63.8 us
    pallas_call x3 -> x24, Pallas kernels: 17.5 us -> 147 us  [the longest x13 103 us: prefetch_call(): pl.pallas_call(kernel, grid_spec=pltpu.PrefetchScalarGridSpec(num_scalar_...]
    ppermute x6 -> x19, waiting for transfers between devices: 29.3 us -> 154 us  [across(): return lax.ppermute(x, 'gx', [(i, i ^ distance) for i in range(4)])]
    dot_general x27 -> x2, matrix products: 93.4 us -> 2.39 us  [dot(): lax.dot_general(a, b, (((dims[0],), (dims[1],)), ((), ())), preferred_ele...]
    all_gather x2 -> x1, blocking collectives: 103 us -> 20.1 us  [body(): pack = lax.all_gather(pack, 'gx', axis=0)]
    ppermute x39 -> x36, waiting for transfers between devices: 169 us -> 92.9 us  [swap(): return lax.ppermute(x, axis, SWAP)]
    convert_element_type x6 -> x0, local copies, waits for them, and re-layouts: 38.6 us -> none  [body(): made = [m.astype(BF16).reshape(columns, block, -1) for m in made]]
    concatenate x15 -> x12, other arithmetic: 37.8 us -> 4.08 us  [the longest x1 1.55 us: body(): ffn_mine = jnp.concatenate([w_gate, w_up, down_t], axis=0)]
    ppermute x6 -> x19, starting transfers between devices: 2.87 us -> 22.9 us  [across(): return lax.ppermute(x, 'gx', [(i, i ^ distance) for i in range(4)])]
  transfers between devices with their start and end apart: 55 -> 61, of which waited for: 17 -> 32; matrix products, arithmetic and copies ran while one was open for 33% -> 9% of each run, Pallas kernels for 1% -> 20%
where the time goes in v2:
time: 604 us; the launch traced here: 597 us
  waiting for transfers between devices  251 us (42%)
  Pallas kernels  147 us (24%)
  local copies, waits for them, and re-layouts  70 us (12%)
  starting transfers between devices  63.8 us (11%)
  other arithmetic  40 us (7%)
  blocking collectives  20.1 us (3%)
    ppermute x19, waiting for transfers between devices, across(): return lax.ppermute(x, 'gx', [(i, i ^ distance) for i in range(4)])  154 us
    pallas_call x13, Pallas kernels, prefetch_call(): pl.pallas_call(kernel, grid_spec=pltpu.PrefetchScalarGridSpec(num_scalar_...  103 us
    ppermute x36, waiting for transfers between devices, swap(): return lax.ppermute(x, axis, SWAP)  92.9 us
    unnamed x214, local copies, waits for them, and re-layouts  41.3 us
    ppermute x36, starting transfers between devices, swap(): return lax.ppermute(x, axis, SWAP)  30.4 us
    pallas_call x4, Pallas kernels, ffn_weight_grads(): pl.pallas_call(kernel, grid_spec=pltpu.PrefetchScalarGridSpec(num_scalar_...  26.9 us
    ppermute x19, starting transfers between devices, across(): return lax.ppermute(x, 'gx', [(i, i ^ distance) for i in range(4)])  22.9 us
    all_gather x1, blocking collectives, body(): pack = lax.all_gather(pack, 'gx', axis=0)  20.1 us
  transfers between devices with their start and end apart: 61, of which 32 were waited for; matrix products, arithmetic and copies ran while one was open for 9% of the time, Pallas kernels for 20%

profile of v2, /device:TPU:0, one launch (start us, length us, event | category | flops | bytes accessed | tf_op | source)
XLA Modules:
  0.0 596.9 jit_solution(11062957097005215053)
XLA Ops:
  7.2 20.1 %all-gather = bf16[768,512]{1,0:T(8,128)(2,1)} all-gather(bf16[192,512]{1,0:T(8,128)(2,1)S(1)} %concatenate.72), channel_id=2, replica_groups=mesh['gx'=4,'gb'=2,'ga'=2,'gc'=2] {'gx'}, dimensions={0}, use_global_device_ids=true | all-gather | bytes 983040 | tf_op jit(solution)/shard_map/all_gather | solution.py:1030
  34.9 21.2 %collective-permute-done.2.refs_1_ = bf16[4,192,512]{2,1,0:T(8,128)(2,1)} collective-permute-done((bf16[4,192,512]{2,1,0:T(8,128)(2,1)}, bf16[4,192,512]{2,1,0:T(8,128)(2,1)}, u32[]{:S(2)}, u32[]{:S(2)}) %collective-permute-start.2) | collective-permute-done | bytes 786464 | tf_op jit(solution)/shard_map/ppermute | solution.py:44
  61.8 6.5 %collective-permute-done.4.refs_3_ = bf16[2,192,512]{2,1,0:T(8,128)(2,1)S(1)} collective-permute-done((bf16[2,192,512]{2,1,0:T(8,128)(2,1)S(1)}, bf16[2,192,512]{2,1,0:T(8,128)(2,1)S(1)}, u32[]{:S(2)}, u32[]{:S(2)}) %collective-permute-start.4) | collective-permute-done | bytes 393248 | tf_op jit(solution)/shard_map/ppermute | solution.py:44
  118.2 8.2 %collective-permute-done.13 = bf16[144,1728]{1,0:T(8,128)(2,1)} collective-permute-done((bf16[144,1728]{1,0:T(8,128)(2,1)}, bf16[144,1728]{1,0:T(8,128)(2,1)}, u32[]{:S(2)}, u32[]{:S(2)}) %collective-permute-start.13) | collective-permute-done | bytes 497696 | tf_op jit(solution)/shard_map/ppermute | solution.py:48
  144.2 13.3 %collective-permute-done.16.got = bf16[256,1024]{1,0:T(8,128)(2,1)S(1)} collective-permute-done((bf16[256,1024]{1,0:T(8,128)(2,1)S(1)}, bf16[256,1024]{1,0:T(8,128)(2,1)S(1)}, u32[]{:S(2)}, u32[]{:S(2)}) %collective-permute-start.16) | collective-permute-done | bytes 524320 | tf_op jit(solution)/shard_map/ppermute | solution.py:48
  174.1 15.5 %collective-permute-done.19.refs_4_.refs_3_ = bf16[208,1728]{1,0:T(8,128)(2,1)} collective-permute-done((bf16[208,1728]{1,0:T(8,128)(2,1)S(1)}, bf16[208,1728]{1,0:T(8,128)(2,1)}, u32[]{:S(2)}, u32[]{:S(2)}) %collective-permute-start.19) | collective-permute-done | bytes 718880 | tf_op jit(solution)/shard_map/ppermute | solution.py:44
  190.1 15.4 %shard_map.306 = (bf16[512,1728]{1,0:T(8,128)(2,1)}, bf16[512,1728]{1,0:T(8,128)(2,1)}, bf16[512,1728]{1,0:T(8,128)(2,1)}, f32[512,1152]{1,0:T(8,128)}) custom-call(s32[8]{0:T(128)} %get-tuple-element.358.slots, bf16[512,1152]{1,0:T(8,128)(2,1)} %copy-done.22, bf16[1728,1728]{1,0:T(8,128)(2,1)} %shard_map.303.refs_0_.refs_1_, ...), custom_call_target="tpu_custom_call" | custom-call | flops 11040000000 | tf_op jit(solution)/shard_map/pallas_call | solution.py:306
  207.2 16.0 %shard_map.307 = (bf16[512,1728]{1,0:T(8,128)(2,1)}, bf16[512,1728]{1,0:T(8,128)(2,1)}, bf16[512,1728]{1,0:T(8,128)(2,1)}, f32[512,1152]{1,0:T(8,128)}) custom-call(s32[10]{0:T(128)} %xor_multiply_fusion.slots, bf16[512,1152]{1,0:T(8,128)(2,1)} %copy-done.22, f32[512,1152]{1,0:T(8,128)} %get-tuple-element.209.refs_0_, ...), custom_call_target="tpu_custom_call" | custom-call | flops 11040000000 | tf_op jit(solution)/shard_map/pallas_call | solution.py:306
  225.4 14.6 %collective-permute-done.26 = bf16[256,1152]{1,0:T(8,128)(2,1)S(1)} collective-permute-done((bf16[256,1152]{1,0:T(8,128)(2,1)S(1)}, bf16[256,1152]{1,0:T(8,128)(2,1)S(1)}, u32[]{:S(2)}, u32[]{:S(2)}) %collective-permute-start.26) | collective-permute-done | bytes 589856 | tf_op jit(solution)/shard_map/ppermute | solution.py:48
  242.9 13.2 %collective-permute-done.27.other_ref = bf16[256,1152]{1,0:T(8,128)(2,1)} collective-permute-done((bf16[256,1152]{1,0:T(8,128)(2,1)S(1)}, bf16[256,1152]{1,0:T(8,128)(2,1)}, u32[]{:S(2)}, u32[]{:S(2)}) %collective-permute-start.27) | collective-permute-done | bytes 589856 | tf_op jit(solution)/shard_map/ppermute | solution.py:48
  263.2 16.1 %shard_map.309 = (bf16[512,1728]{1,0:T(8,128)(2,1)}, bf16[512,1728]{1,0:T(8,128)(2,1)}, f32[512,1152]{1,0:T(8,128)}) custom-call(s32[10]{0:T(128)} %xor_multiply_fusion.slots, bf16[512,1152]{1,0:T(8,128)(2,1)} %copy-done.55, bf16[512,1728]{1,0:T(8,128)(2,1)} %get-tuple-element.217.act_ref, bf16[512,1728]{1,0:T(8,128)(2,1)} %get-tuple-element.218.slope_ref, ...), custom_call_target="tpu_custom_call" | custom-call | flops 11040000000 | tf_op jit(solution)/shard_map/pallas_call | solution.py:306
  282.3 6.6 %shard_map.310 = bf16[4,432,1728]{2,1,0:T(8,128)(2,1)} custom-call(s32[1]{0:T(128)} %bitcast.5.core_ref, bf16[1152,512]{1,0:T(8,128)(2,1)S(1)} %bitcast.119, bf16[1152,512]{1,0:T(8,128)(2,1)S(1)} %get-tuple-element.220.d_ffn_ref, bf16[512,1728]{1,0:T(8,128)(2,1)S(1)} %copy-done.48, bf16[512,1728]{1,0:T(8,128)(2,1)S(1)} %copy-done.50, ...), custom_call_target="tpu_custom_call" | custom-call | flops 4623000064 | tf_op jit(solution)/shard_map/pallas_call | solution.py:208
  288.9 15.9 %shard_map.311 = (bf16[512,1728]{1,0:T(8,128)(2,1)}, bf16[512,1728]{1,0:T(8,128)(2,1)}, f32[512,1152]{1,0:T(8,128)}) custom-call(s32[8]{0:T(128)} %get-tuple-element.358.slots, bf16[512,1152]{1,0:T(8,128)(2,1)} %copy-done.55, bf16[512,1728]{1,0:T(8,128)(2,1)} %get-tuple-element.215.act_ref, bf16[512,1728]{1,0:T(8,128)(2,1)} %get-tuple-element.216.slope_ref, ...), custom_call_target="tpu_custom_call" | custom-call | flops 11040000000 | tf_op jit(solution)/shard_map/pallas_call | solution.py:306
  312.7 6.6 %shard_map.312 = bf16[4,432,1728]{2,1,0:T(8,128)(2,1)} custom-call(s32[1]{0:T(128)} %bitcast.7.core_ref, bf16[1152,512]{1,0:T(8,128)(2,1)S(1)} %bitcast.120, bf16[1152,512]{1,0:T(8,128)(2,1)S(1)} %copy-done.53, bf16[512,1728]{1,0:T(8,128)(2,1)S(1)} %copy-done.49, bf16[512,1728]{1,0:T(8,128)(2,1)S(1)} %copy-done.51, ...), custom_call_target="tpu_custom_call" | custom-call | flops 4623000064 | tf_op jit(solution)/shard_map/pallas_call | solution.py:208
  331.2 11.7 %shard_map.313 = (f32[256,1152]{1,0:T(8,128)}, bf16[256,1152]{1,0:T(8,128)(2,1)}, bf16[1152,256]{1,0:T(8,128)(2,1)S(1)}, f32[2,1152]{1,0:T(2,128)S(1)}, bf16[256...) custom-call(s32[13]{0:T(128)S(1)} %copy-done.43, ...), custom_call_target="tpu_custom_call" | custom-call | flops 8280000000 | tf_op jit(solution)/shard_map/pallas_call | solution.py:306
  361.5 7.0 %shard_map.314 = bf16[4,432,1728]{2,1,0:T(8,128)(2,1)} custom-call(s32[1]{0:T(128)} %bitcast.5.core_ref, bf16[1152,512]{1,0:T(8,128)(2,1)S(1)} %bitcast.121, bf16[1152,512]{1,0:T(8,128)(2,1)S(1)} %copy-done.54, bf16[512,1728]{1,0:T(8,128)(2,1)S(1)} %copy-done.46, bf16[512,1728]{1,0:T(8,128)(2,1)S(1)} %copy-done.47, ...), custom_call_target="tpu_custom_call" | custom-call | flops 4623000064 | tf_op jit(solution)/shard_map/pallas_call | solution.py:208
  377.0 6.6 %shard_map.317 = bf16[4,432,1728]{2,1,0:T(8,128)(2,1)} custom-call(s32[1]{0:T(128)} %bitcast.7.core_ref, bf16[1152,512]{1,0:T(8,128)(2,1)S(1)} %bitcast.122, bf16[1152,512]{1,0:T(8,128)(2,1)S(1)} %copy-done.54, bf16[512,1728]{1,0:T(8,128)(2,1)S(1)} %copy-done.46, bf16[512,1728]{1,0:T(8,128)(2,1)S(1)} %copy-done.47, ...), custom_call_target="tpu_custom_call" | custom-call | flops 4623000064 | tf_op jit(solution)/shard_map/pallas_call | solution.py:208
  404.4 10.3 %collective-permute-done.42.refs_1_ = bf16[256,512]{1,0:T(8,128)(2,1)S(1)} collective-permute-done((bf16[256,512]{1,0:T(8,128)(2,1)}, bf16[256,512]{1,0:T(8,128)(2,1)S(1)}, u32[]{:S(2)}, u32[]{:S(2)}) %collective-permute-start.42) | collective-permute-done | bytes 262176 | tf_op jit(solution)/shard_map/ppermute | solution.py:48
  441.5 9.7 %collective-permute-done.48 = bf16[208,1728]{1,0:T(8,128)(2,1)S(1)} collective-permute-done((bf16[208,1728]{1,0:T(8,128)(2,1)S(1)}, bf16[208,1728]{1,0:T(8,128)(2,1)S(1)}, u32[]{:S(2)}, u32[]{:S(2)}) %collective-permute-start.48) | collective-permute-done | bytes 718880 | tf_op jit(solution)/shard_map/ppermute | solution.py:44
  452.1 24.8 %collective-permute-done.46 = bf16[144,1728]{1,0:T(8,128)(2,1)S(1)} collective-permute-done((bf16[144,1728]{1,0:T(8,128)(2,1)S(1)}, bf16[144,1728]{1,0:T(8,128)(2,1)S(1)}, u32[]{:S(2)}, u32[]{:S(2)}) %collective-permute-start.46) | collective-permute-done | bytes 497696 | tf_op jit(solution)/shard_map/ppermute | solution.py:48
  480.9 8.2 %collective-permute-done.45.refs_1_ = bf16[256,1152]{1,0:T(8,128)(2,1)S(1)} collective-permute-done((bf16[256,1152]{1,0:T(8,128)(2,1)S(1)}, bf16[256,1152]{1,0:T(8,128)(2,1)S(1)}, u32[]{:S(2)}, u32[]{:S(2)}) %collective-permute-start.45) | collective-permute-done | bytes 589856 | tf_op jit(solution)/shard_map/ppermute | solution.py:48
  501.0 29.1 %collective-permute-done.53 = bf16[144,1728]{1,0:T(8,128)(2,1)S(1)} collective-permute-done((bf16[144,1728]{1,0:T(8,128)(2,1)}, bf16[144,1728]{1,0:T(8,128)(2,1)S(1)}, u32[]{:S(2)}, u32[]{:S(2)}) %collective-permute-start.53) | collective-permute-done | bytes 497696 | tf_op jit(solution)/shard_map/ppermute | solution.py:48
  539.0 18.7 %collective-permute-done.56 = bf16[2,192,512]{2,1,0:T(8,128)(2,1)S(1)} collective-permute-done((bf16[2,192,512]{2,1,0:T(8,128)(2,1)S(1)}, bf16[2,192,512]{2,1,0:T(8,128)(2,1)S(1)}, u32[]{:S(2)}, u32[]{:S(2)}) %collective-permute-start.56) | collective-permute-done | bytes 393248 | tf_op jit(solution)/shard_map/ppermute | solution.py:48
  572.5 19.7 %collective-permute-done.60 = bf16[432,1728]{1,0:T(8,128)(2,1)S(1)} collective-permute-done((bf16[432,1728]{1,0:T(8,128)(2,1)S(1)}, bf16[432,1728]{1,0:T(8,128)(2,1)S(1)}, u32[]{:S(2)}, u32[]{:S(2)}) %collective-permute-start.60) | collective-permute-done | bytes 1493024 | tf_op jit(solution)/shard_map/ppermute | solution.py:44
  (456 shorter events, 259.1 us)
Async XLA Ops:
  2.3 55.3 %collective-permute-start = (bf16[432,1728]{1,0:T(8,128)(2,1)S(1)}, bf16[432,1728]{1,0:T(8,128)(2,1)S(1)}, u32[]{:S(2)}, u32[]{:S(2)}) collective-permute-start(bf16[432,1728]{1,0:T(8,128)(2,1)S(1)} %pad_maximum_fusion.refs_0_), channel_id=1, source_target_pairs={{0,2},{2,0},{1,3},{3,1},{4,6},{6,4},{5,7},{7,5},{8,10},{10,8},{9,1... | collective-permute-start | bytes 4478984 | tf_op jit(solution)/shard_map/ppermute | solution.py:44
  5.3 52.3 %collective-permute-start.1 = (bf16[432,1728]{1,0:T(8,128)(2,1)S(1)}, bf16[432,1728]{1,0:T(8,128)(2,1)}, u32[]{:S(2)}, u32[]{:S(2)}) collective-permute-start(bf16[432,1728]{1,0:T(8,128)(2,1)S(1)} %pad_maximum_fusion.refs_0_), channel_id=1, source_target_pairs={{0,4},{4,0},{1,5},{5,1},{2,6},{6,2},{3,7},{7,3},{8,12},{12,8},{9,1... | collective-permute-start | bytes 4478984 | tf_op jit(solution)/shard_map/ppermute | solution.py:44
  27.3 28.8 %collective-permute-start.2 = (bf16[4,192,512]{2,1,0:T(8,128)(2,1)}, bf16[4,192,512]{2,1,0:T(8,128)(2,1)}, u32[]{:S(2)}, u32[]{:S(2)}) collective-permute-start(bf16[4,192,512]{2,1,0:T(8,128)(2,1)} %bitcast.4.refs_0_), channel_id=1, source_target_pairs={{0,2},{2,0},{1,3},{3,1},{4,6},{6,4},{5,7},{7,5},{8,10},{10,8},{9,1... | collective-permute-start | bytes 2359304 | tf_op jit(solution)/shard_map/ppermute | solution.py:44
  27.9 29.7 %collective-permute-start.3 = (bf16[4,192,512]{2,1,0:T(8,128)(2,1)}, bf16[4,192,512]{2,1,0:T(8,128)(2,1)}, u32[]{:S(2)}, u32[]{:S(2)}) collective-permute-start(bf16[4,192,512]{2,1,0:T(8,128)(2,1)} %bitcast.4.refs_0_), channel_id=1, source_target_pairs={{0,4},{4,0},{1,5},{5,1},{2,6},{6,2},{3,7},{7,3},{8,12},{12,8},{9,1... | collective-permute-start | bytes 2359304 | tf_op jit(solution)/shard_map/ppermute | solution.py:44
  28.4 33.5 %collective-permute-start.6 = (bf16[144,1728]{1,0:T(8,128)(2,1)}, bf16[144,1728]{1,0:T(8,128)(2,1)}, u32[]{:S(2)}, u32[]{:S(2)}) collective-permute-start(bf16[144,1728]{1,0:T(8,128)(2,1)} %param.25), channel_id=1, source_target_pairs={{0,16},{8,24},{16,0},{24,8},{1,17},{9,25},{17,1},{25,9},{2,18},{10... | collective-permute-start | bytes 1493000 | tf_op jit(solution)/shard_map/ppermute | solution.py:48
  78.4 39.8 %collective-permute-start.12 = (bf16[144,1728]{1,0:T(8,128)(2,1)}, bf16[144,1728]{1,0:T(8,128)(2,1)}, u32[]{:S(2)}, u32[]{:S(2)}) collective-permute-start(bf16[144,1728]{1,0:T(8,128)(2,1)} %param.26), channel_id=1, source_target_pairs={{0,16},{8,24},{16,0},{24,8},{1,17},{9,25},{17,1},{25,9},{2,18},{10... | collective-permute-start | bytes 1493000 | tf_op jit(solution)/shard_map/ppermute | solution.py:48
  81.0 45.4 %collective-permute-start.13 = (bf16[144,1728]{1,0:T(8,128)(2,1)}, bf16[144,1728]{1,0:T(8,128)(2,1)}, u32[]{:S(2)}, u32[]{:S(2)}) collective-permute-start(bf16[144,1728]{1,0:T(8,128)(2,1)} %bitcast.2), channel_id=1, source_target_pairs={{0,16},{8,24},{16,0},{24,8},{1,17},{9,25},{17,1},{25,9},{2,18},{10... | collective-permute-start | bytes 1493000 | tf_op jit(solution)/shard_map/ppermute | solution.py:48
  132.9 36.5 %collective-permute-start.17 = (bf16[432,1728]{1,0:T(8,128)(2,1)}, bf16[432,1728]{1,0:T(8,128)(2,1)S(1)}, u32[]{:S(2)}, u32[]{:S(2)}) collective-permute-start(bf16[432,1728]{1,0:T(8,128)(2,1)} %constant_dynamic-update-slice_fusion.refs_1_.refs_0_), channel_id=1, source_target_pairs={{0,2},{2,0},{1,3},{3,1},{4,6},{6,4},{5,7},{7,5},{8,10},{10,8},{9,1... | collective-permute-start | bytes 4478984 | tf_op jit(solution)/shard_map/ppermute | solution.py:44
  133.5 36.3 %collective-permute-start.18 = (bf16[432,1728]{1,0:T(8,128)(2,1)}, bf16[432,1728]{1,0:T(8,128)(2,1)}, u32[]{:S(2)}, u32[]{:S(2)}) collective-permute-start(bf16[432,1728]{1,0:T(8,128)(2,1)} %constant_dynamic-update-slice_fusion.refs_1_.refs_0_), channel_id=1, source_target_pairs={{0,4},{4,0},{1,5},{5,1},{2,6},{6,2},{3,7},{7,3},{8,12},{12,8},{9,1... | collective-permute-start | bytes 4478984 | tf_op jit(solution)/shard_map/ppermute | solution.py:44
  173.1 32.5 %collective-permute-start.21 = (bf16[432,1728]{1,0:T(8,128)(2,1)}, bf16[432,1728]{1,0:T(8,128)(2,1)S(1)}, u32[]{:S(2)}, u32[]{:S(2)}) collective-permute-start(bf16[432,1728]{1,0:T(8,128)(2,1)} %constant_dynamic-update-slice_fusion.refs_1_.refs_0_), channel_id=1, source_target_pairs={{0,1},{1,0},{2,3},{3,2},{4,5},{5,4},{6,7},{7,6},{8,9},{9,8},{10,11... | collective-permute-start | bytes 4478984 | tf_op jit(solution)/shard_map/ppermute | solution.py:44
  173.1 32.5 %collective-permute-start.22 = (bf16[432,1728]{1,0:T(8,128)(2,1)S(1)}, bf16[432,1728]{1,0:T(8,128)(2,1)S(1)}, u32[]{:S(2)}, u32[]{:S(2)}) collective-permute-start(bf16[432,1728]{1,0:T(8,128)(2,1)S(1)} %collective-permute-done.17.refs_2_.refs_1_), channel_id=1, source_target_pairs={{0,1},{1,0},{2,3},{3,2},{4,5},{5,4},{6,7},{7,6},{8,9},{9,8},{10,11... | collective-permute-start | bytes 4478984 | tf_op jit(solution)/shard_map/ppermute | solution.py:44
  173.6 32.0 %collective-permute-start.23 = (bf16[432,1728]{1,0:T(8,128)(2,1)}, bf16[432,1728]{1,0:T(8,128)(2,1)}, u32[]{:S(2)}, u32[]{:S(2)}) collective-permute-start(bf16[432,1728]{1,0:T(8,128)(2,1)} %collective-permute-done.18.refs_3_.refs_2_), channel_id=1, source_target_pairs={{0,1},{1,0},{2,3},{3,2},{4,5},{5,4},{6,7},{7,6},{8,9},{9,8},{10,11... | collective-permute-start | bytes 4478984 | tf_op jit(solution)/shard_map/ppermute | solution.py:44
  260.5 28.4 %collective-permute-start.28 = (bf16[256,1152]{1,0:T(8,128)(2,1)S(1)}, bf16[256,1152]{1,0:T(8,128)(2,1)S(1)}, u32[]{:S(2)}, u32[]{:S(2)}) collective-permute-start(bf16[256,1152]{1,0:T(8,128)(2,1)S(1)} %slice.290), channel_id=1, source_target_pairs={{0,16},{8,24},{16,0},{24,8},{1,17},{9,25},{17,1},{25,9},{2,18},{10... | collective-permute-start | bytes 1769480 | tf_op jit(solution)/shard_map/ppermute | solution.py:48
  288.9 34.0 %collective-permute-start.30 = (bf16[4,432,1728]{2,1,0:T(8,128)(2,1)}, bf16[4,432,1728]{2,1,0:T(8,128)(2,1)}, u32[]{:S(2)}, u32[]{:S(2)}) collective-permute-start(bf16[4,432,1728]{2,1,0:T(8,128)(2,1)} %shard_map.310), channel_id=1, source_target_pairs={{0,1},{1,0},{2,3},{3,2},{4,5},{5,4},{6,7},{7,6},{8,9},{9,8},{10,11... | collective-permute-start | bytes 17915912 | tf_op jit(solution)/shard_map/ppermute | solution.py:44
  429.4 47.5 %collective-permute-start.47 = (bf16[4,768,512]{2,1,0:T(8,128)(2,1)}, bf16[4,768,512]{2,1,0:T(8,128)(2,1)}, u32[]{:S(2)}, u32[]{:S(2)}) collective-permute-start(bf16[4,768,512]{2,1,0:T(8,128)(2,1)} %shard_map.320), channel_id=1, source_target_pairs={{0,1},{1,0},{2,3},{3,2},{4,5},{5,4},{6,7},{7,6},{8,9},{9,8},{10,11... | collective-permute-start | bytes 9437192 | tf_op jit(solution)/shard_map/ppermute | solution.py:44
  437.4 39.4 %collective-permute-start.46 = (bf16[144,1728]{1,0:T(8,128)(2,1)S(1)}, bf16[144,1728]{1,0:T(8,128)(2,1)S(1)}, u32[]{:S(2)}, u32[]{:S(2)}) collective-permute-start(bf16[144,1728]{1,0:T(8,128)(2,1)S(1)} %get-tuple-element.333), channel_id=1, source_target_pairs={{0,16},{8,24},{16,0},{24,8},{1,17},{9,25},{17,1},{25,9},{2,18},{10... | collective-permute-start | bytes 1493000 | tf_op jit(solution)/shard_map/ppermute | solution.py:48
  440.6 48.6 %collective-permute-start.45 = (bf16[256,1152]{1,0:T(8,128)(2,1)S(1)}, bf16[256,1152]{1,0:T(8,128)(2,1)S(1)}, u32[]{:S(2)}, u32[]{:S(2)}) collective-permute-start(bf16[256,1152]{1,0:T(8,128)(2,1)S(1)} %copy-done.29), channel_id=1, source_target_pairs={{0,16},{8,24},{16,0},{24,8},{1,17},{9,25},{17,1},{25,9},{2,18},{10... | collective-permute-start | bytes 1769480 | tf_op jit(solution)/shard_map/ppermute | solution.py:48
  491.7 38.4 %collective-permute-start.55 = (bf16[768,512]{1,0:T(8,128)(2,1)S(1)}, bf16[768,512]{1,0:T(8,128)(2,1)}, u32[]{:S(2)}, u32[]{:S(2)}) collective-permute-start(bf16[768,512]{1,0:T(8,128)(2,1)S(1)} %pad_maximum_fusion.7), channel_id=1, source_target_pairs={{0,4},{4,0},{1,5},{5,1},{2,6},{6,2},{3,7},{7,3},{8,12},{12,8},{9,1... | collective-permute-start | bytes 2359304 | tf_op jit(solution)/shard_map/ppermute | solution.py:44
  493.7 36.5 %collective-permute-start.54 = (bf16[768,512]{1,0:T(8,128)(2,1)S(1)}, bf16[768,512]{1,0:T(8,128)(2,1)}, u32[]{:S(2)}, u32[]{:S(2)}) collective-permute-start(bf16[768,512]{1,0:T(8,128)(2,1)S(1)} %pad_maximum_fusion.6), channel_id=1, source_target_pairs={{0,2},{2,0},{1,3},{3,1},{4,6},{6,4},{5,7},{7,5},{8,10},{10,8},{9,1... | collective-permute-start | bytes 2359304 | tf_op jit(solution)/shard_map/ppermute | solution.py:44
  494.5 35.6 %collective-permute-start.53 = (bf16[144,1728]{1,0:T(8,128)(2,1)}, bf16[144,1728]{1,0:T(8,128)(2,1)S(1)}, u32[]{:S(2)}, u32[]{:S(2)}) collective-permute-start(bf16[144,1728]{1,0:T(8,128)(2,1)} %get-tuple-element.299), channel_id=1, source_target_pairs={{0,16},{8,24},{16,0},{24,8},{1,17},{9,25},{17,1},{25,9},{2,18},{10... | collective-permute-start | bytes 1493000 | tf_op jit(solution)/shard_map/ppermute | solution.py:48
  497.7 60.2 %collective-permute-start.57 = (bf16[144,1728]{1,0:T(8,128)(2,1)S(1)}, bf16[144,1728]{1,0:T(8,128)(2,1)S(1)}, u32[]{:S(2)}, u32[]{:S(2)}) collective-permute-start(bf16[144,1728]{1,0:T(8,128)(2,1)S(1)} %copy-done.83), channel_id=1, source_target_pairs={{0,16},{8,24},{16,0},{24,8},{1,17},{9,25},{17,1},{25,9},{2,18},{10... | collective-permute-start | bytes 1493000 | tf_op jit(solution)/shard_map/ppermute | solution.py:48
  500.7 58.7 %collective-permute-start.52 = (bf16[512,1152]{1,0:T(8,128)(2,1)S(1)}, bf16[512,1152]{1,0:T(8,128)(2,1)S(1)}, u32[]{:S(2)}, u32[]{:S(2)}) collective-permute-start(bf16[512,1152]{1,0:T(8,128)(2,1)S(1)} %pad_maximum_fusion.5), channel_id=1, source_target_pairs={{0,8},{8,0},{16,24},{24,16},{1,9},{9,1},{17,25},{25,17},{2,10},{10... | collective-permute-start | bytes 3538952 | tf_op jit(solution)/shard_map/ppermute | solution.py:48
  536.8 35.7 %collective-permute-start.59 = (bf16[432,1728]{1,0:T(8,128)(2,1)S(1)}, bf16[432,1728]{1,0:T(8,128)(2,1)S(1)}, u32[]{:S(2)}, u32[]{:S(2)}) collective-permute-start(bf16[432,1728]{1,0:T(8,128)(2,1)S(1)} %pad_maximum_fusion.3), channel_id=1, source_target_pairs={{0,2},{2,0},{1,3},{3,1},{4,6},{6,4},{5,7},{7,5},{8,10},{10,8},{9,1... | collective-permute-start | bytes 4478984 | tf_op jit(solution)/shard_map/ppermute | solution.py:44
  558.9 33.3 %collective-permute-start.60 = (bf16[432,1728]{1,0:T(8,128)(2,1)S(1)}, bf16[432,1728]{1,0:T(8,128)(2,1)S(1)}, u32[]{:S(2)}, u32[]{:S(2)}) collective-permute-start(bf16[432,1728]{1,0:T(8,128)(2,1)S(1)} %pad_maximum_fusion.4), channel_id=1, source_target_pairs={{0,4},{4,0},{1,5},{5,1},{2,6},{6,2},{3,7},{7,3},{8,12},{12,8},{9,1... | collective-permute-start | bytes 4478984 | tf_op jit(solution)/shard_map/ppermute | solution.py:44
  (141 other events, 1447.0 us)

commit v3 on v2

--- a/solution.py
+++ b/solution.py
@@ -53,7 +53,7 @@
 
 
 def cost(microseconds):
-    flops = int(microseconds * 0.6 * 1.15e9)
+    flops = int(microseconds * 1.0 * 1.15e9)
     return pl.CostEstimate(flops=flops, bytes_accessed=0, transcendentals=0)
 
 
@@ -251,28 +251,46 @@
 class Scatter:
     def __init__(self, keep, received):
         y, x = lax.axis_index("gb"), lax.axis_index("ga")
-        self.pick = lambda n: lax.dynamic_index_in_dim(keep, n, 0, keepdims=False).astype(
-            F32
-        ) + lax.dynamic_index_in_dim(received, n, 0, keepdims=False).astype(F32)
+        self.keep, self.received = keep, received
         self.here, self.x, self.y = 2 * y + x, 2 * y + 1 - x, 2 * (1 - y) + x
         self.far = 2 * (1 - y) + 1 - x
-
-    def send_far(self):
-        first, second = halves(self.pick(self.far).astype(BF16))
-        return swap(first, "ga"), swap(second, "gb")
+        self.half = keep.shape[1] // 32 * 16
+
+    def part(self, chip, second=None):
+        made = 0.0
+        for values in (self.keep, self.received):
+            block = lax.dynamic_index_in_dim(values, chip, 0, keepdims=False)
+            if second is not None:
+                block = block[self.half :] if second else block[: self.half]
+            made = made + block.astype(F32)
+        return made
+
+    def far_blocks(self):
+        return self.part(self.far, False).astype(BF16), self.part(self.far, True).astype(BF16)
+
+    def first_blocks(self):
+        return self.part(self.x, False).astype(BF16), self.part(self.y, True).astype(BF16)
+
+    def second_blocks(self, got_first, got_second):
+        to_x = self.part(self.x, True) + got_second.astype(F32)
+        to_y = self.part(self.y, False) + got_first.astype(F32)
+        return to_x.astype(BF16), to_y.astype(BF16)
 
     def near_blocks(self, got_first, got_second):
-        (x0, x1), (y0, y1) = halves(self.pick(self.x)), halves(self.pick(self.y))
-        to_x = jnp.concatenate([x0, x1 + got_second.astype(F32)], axis=0)
-        to_y = jnp.concatenate([y0 + got_first.astype(F32), y1], axis=0)
-        return to_x.astype(BF16), to_y.astype(BF16)
-
-    def send_near(self, got_first, got_second):
-        to_x, to_y = self.near_blocks(got_first, got_second)
-        return swap(to_x, "ga"), swap(to_y, "gb")
-
-    def total(self, got_x, got_y):
-        return self.pick(self.here) + got_x.astype(F32) + got_y.astype(F32)
+        first, second = self.first_blocks(), self.second_blocks(got_first, got_second)
+        return jnp.concatenate([first[0], second[0]]), jnp.concatenate([second[1], first[1]])
+
+    def near_total(self, got_x, got_y):
+        return self.part(self.here) + got_x.astype(F32) + got_y.astype(F32)
+
+    def total(self, first, second):
+        upper = self.part(self.here, False) + first[0].astype(F32) + second[1].astype(F32)
+        lower = self.part(self.here, True) + second[0].astype(F32) + first[1].astype(F32)
+        return jnp.concatenate([upper, lower], axis=0)
+
+
+def send_xy(blocks):
+    return swap(blocks[0], "ga"), swap(blocks[1], "gb")
 
 
 def plane_scatter(g):
@@ -283,7 +301,8 @@
     keep = lax.dynamic_index_in_dim(g, c, 1, keepdims=False)
     received = swap(lax.dynamic_index_in_dim(g, 1 - c, 1, keepdims=False), "gc")
     work = Scatter(keep, received)
-    return work.total(*work.send_near(*work.send_far()))
+    second = work.second_blocks(*send_xy(work.far_blocks()))
+    return work.total(send_xy(work.first_blocks()), send_xy(second))
 
 
 GELU_A = 0.7978845608028654
@@ -1028,16 +1047,16 @@
     if square():
         ffn_x, ffn_y = send_near(ffn_mine)
         pack = lax.all_gather(pack, "gx", axis=0)
-        pack, other_gate = tie(pack, w_gate)
-        their_gate = across(other_gate, 2)
+        pack, other_gu = tie(pack, ffn_mine[: 2 * block])
+        their_gu = across(other_gu, 2)
         pack_x, pack_y = send_near(pack)
         ffn_x, ffn_y, pack, pack_x, pack_y, cos_table, sin_table = tie(
             ffn_x, ffn_y, pack, pack_x, pack_y, cos_table, sin_table
         )
         pack_far = send_far(pack_x, pack_y)
         ffn_far = send_far(ffn_x, ffn_y)
-        *pack_far, their_gate, other_up, other_down = tie(*pack_far, their_gate, w_up, down_t)
-        their_up, their_down = across(other_up, 2), across(other_down, 2)
+        *pack_far, their_gu, other_down = tie(*pack_far, their_gu, down_t)
+        their_down = across(other_down, 2)
         pack_all = collect((pack, pack_x, pack_y, *pack_far), planes)
         pack_other = swap(pack_all, "gc")
         wq, wo_t, wkv, gains = unpack(
@@ -1087,20 +1106,18 @@
         flags, tokens, gain_in, wkv, gain_key, cos_table, sin_table
     )
     if square():
-        send_1, send_2, *ffn_far = tie(send_1, send_2, *ffn_far)
+        send_1, send_2 = tie(send_1, send_2)
     got_1 = send(send_1, route_1)
     got_2 = send(send_2, route_2)
     query, query_raw = query_kernel(
         plane, normed_own, wq, gain_query, cos_table, sin_table, head_width
     )
     if square():
-        query, ffn_x, ffn_y, *ffn_far = tie(query, ffn_x, ffn_y, *ffn_far)
+        query, ffn_x, ffn_y, their_down, *ffn_far = tie(query, ffn_x, ffn_y, their_down, *ffn_far)
+        theirs = jnp.concatenate([their_gu, their_down], axis=0)
         mine_all = collect((ffn_mine, ffn_x, ffn_y, *ffn_far), 3 * block)
-        got_1, got_2, mine_all, their_up, their_down = tie(
-            got_1, got_2, mine_all, their_up, their_down
-        )
+        got_1, got_2, mine_all, theirs = tie(got_1, got_2, mine_all, theirs)
         mine_other = swap(mine_all, "gc")
-        theirs = jnp.concatenate([their_gate, their_up, their_down], axis=0)
         their_x, their_y = send_near(theirs)
     got_3 = send(jnp.where(role == 2, got_2, send_3), route_3)
     heads_low, slots = attention_kernel(flags, query, pairs, got_1, got_2, got_3)
@@ -1117,19 +1134,12 @@
     if square():
         normed_ffn, their_x, their_y = tie(normed_ffn, their_x, their_y)
         their_far = send_far(their_x, their_y)
-        quarter_theirs = Blocks(
-            both_cores(
-                [
-                    (theirs, 0, 0),
-                    (their_x, 0, 2),
-                    (their_y, 0, 4),
-                    (their_far[0], 0, 6),
-                    (their_far[1], their_far[0].shape[0], 6),
-                ]
-            ),
-            block,
-        )
+        near_pieces = both_cores([(theirs, 0, 0), (their_x, 0, 2), (their_y, 0, 4)])
     act_m, slope_m, hidden_m, ffn_part = ffn_forward_kernel(quarter_mine, normed_ffn, None)
+    if square():
+        ffn_part, *their_far = tie(ffn_part, *their_far)
+        far_pieces = both_cores([(their_far[0], 0, 6), (their_far[1], their_far[0].shape[0], 6)])
+        quarter_theirs = Blocks(near_pieces + far_pieces, block)
     act_t, slope_t, hidden_t, ffn_part = ffn_forward_kernel(quarter_theirs, normed_ffn, ffn_part)
     ffn_got = across(ffn_part[SEG:].astype(BF16), 1)
     ffn_own = (ffn_part[:SEG] + ffn_got.astype(F32)).astype(BF16)
@@ -1143,17 +1153,20 @@
     if square():
         lefts = (normed_ffn.T, d_ffn_t)
         send_theirs = ffn_weight_grads(1 - core, *lefts, d_gate_t, d_up_t, hidden_t, block)
-        back, send_theirs, output_far[0] = tie(back, send_theirs, output_far[0])
+        keep_theirs = ffn_weight_grads(core, *lefts, d_gate_t, d_up_t, hidden_t, block)
+        back, send_theirs, keep_theirs, output_far[0] = tie(
+            back, send_theirs, keep_theirs, output_far[0]
+        )
         recv_theirs = swap(send_theirs, "gc")
     d_gate_m, d_up_m, back = ffn_backward_kernel(quarter_mine, d_ffn_low, act_m, slope_m, back)
-    back, d_gate_t = tie(back, d_gate_t)
+    if square():
+        back, recv_theirs = tie(back, recv_theirs)
+        theirs = Scatter(keep_theirs, recv_theirs)
     back_got = across(back[SEG:].astype(BF16), 1)
     if square():
-        keep_theirs = ffn_weight_grads(core, *lefts, d_gate_t, d_up_t, hidden_t, block)
-        back_got, recv_theirs, keep_theirs, output = tie(
-            back_got, recv_theirs, keep_theirs, output
-        )
-        theirs_far = Scatter(keep_theirs, recv_theirs).send_far()
+        theirs_far = send_xy(theirs.far_blocks())
+        theirs_first = send_xy(theirs.first_blocks())
+        back_got, output = tie(back_got, output)
     else:
         grads = []
         for d_gate, d_up, hidden in ((d_gate_m, d_up_m, hidden_m), (d_gate_t, d_up_t, hidden_t)):
@@ -1175,49 +1188,45 @@
         gain_query, slots, cos_table, sin_table, head_width,
     )
     if square():
-        d_a, d_b, output_far[1], output = tie(d_a, d_b, output_far[1], output)
+        d_a, d_b, output_far[1], output, d_gate_m = tie(
+            d_a, d_b, output_far[1], output, d_gate_m
+        )
     output_far.append(across(output[SEG + SEG // 2 :], 2))
     back_1 = send_back(d_a, route_1)
     back_3 = send_back(d_b, route_3)
     if square():
-        d_a, d_b, back_1, back_3, *theirs_far = tie(d_a, d_b, back_1, back_3, *theirs_far)
+        theirs_second = theirs.second_blocks(*theirs_far)
+        made = (*lefts, d_gate_m, d_up_m, hidden_m)
+        send_mine = ffn_weight_grads(1 - core, *made, block)
+        d_a, d_b, back_1, back_3, send_mine, d_gate_m, *flat = tie(
+            d_a, d_b, back_1, back_3, send_mine, d_gate_m, *theirs_first, *theirs_second
+        )
+        theirs_first, theirs_second = flat[:2], flat[2:]
     d_b_far = jnp.where(role == 2, d_b.astype(F32) + back_3.astype(F32), 0.0).astype(BF16)
     to_back_2 = jnp.where(role == 3, d_a, d_b_far)
-    if square():
-        to_back_2, keep_theirs, recv_theirs, d_gate_m, *theirs_far = tie(
-            to_back_2, keep_theirs, recv_theirs, d_gate_m, *theirs_far
-        )
     back_2 = send_back(to_back_2, route_2)
     if square():
-        to_near = Scatter(keep_theirs, recv_theirs).near_blocks(*theirs_far)
-        made = (*lefts, d_gate_m, d_up_m, hidden_m)
-        send_mine = ffn_weight_grads(1 - core, *made, block)
-        back_2, output_far[2], send_mine, *to_near = tie(
-            back_2, output_far[2], send_mine, *to_near
+        theirs_second = send_xy(theirs_second)
+        keep_mine = ffn_weight_grads(core, *lefts, d_gate_m, d_up_m, hidden_m, block)
+        back_2, output_far[2], keep_mine, send_mine = tie(
+            back_2, output_far[2], keep_mine, send_mine
         )
         recv_mine = swap(send_mine, "gc")
-        half = to_near[0].shape[0] // 32 * 16
-
-        near_first = swap(to_near[0][:half], "ga"), swap(to_near[1][:half], "gb")
     sent, kept = window_kernel(flags, d_self, d_a, d_b, back_1, back_2, back_3)
     kept, passed = z_first(sent, kept[0], kept[1])
     if square():
-        keep_mine = ffn_weight_grads(core, *made, block)
-        passed, keep_mine, recv_mine, *near = tie(passed, keep_mine, recv_mine, *near_first, *to_near)
-        near_first = near[:2]
-        near_second = swap(near[2][half:], "ga"), swap(near[3][half:], "gb")
+        passed, d_query_low, keep_mine, recv_mine = tie(
+            passed, d_query_low, keep_mine, recv_mine
+        )
     d_normed_query = dot(d_query_low, wq, (1, 1))
     own_terms = [kept, across(passed, 2)]
     if square():
-        own_terms[1], keep_theirs, recv_theirs, *near = tie(
-            own_terms[1], keep_theirs, recv_theirs, *near_first, *near_second
+        mine = Scatter(keep_mine, recv_mine)
+        mine_far = send_xy(mine.far_blocks())
+        theirs_sum = theirs.total(theirs_first, theirs_second).astype(BF16)
+        own_terms[1], theirs_sum, d_normed_query, d_gains_mid, d_gain_last, d_gain_query = tie(
+            own_terms[1], theirs_sum, d_normed_query, d_gains_mid, d_gain_last, d_gain_query
         )
-        theirs_near = [jnp.concatenate([near[i], near[i + 2]], axis=0) for i in range(2)]
-        theirs_sum = Scatter(keep_theirs, recv_theirs).total(*theirs_near).astype(BF16)
-        gate_sum = across(theirs_sum[:block], 2)
-        mine_far = Scatter(keep_mine, recv_mine).send_far()
-        theirs_sum = Scatter(keep_theirs, recv_theirs).total(*theirs_near).astype(BF16)
-        gate_sum = across(theirs_sum[:block], 2)
     d_kv_low, token_rows, d_gain_key, d_gain_in = tokens_back_kernel(
         plane, own_terms, key_raw, gain_key, cos_table, sin_table, wkv, d_normed_query, d_mid,
         tokens, gain_in,
@@ -1250,23 +1259,21 @@
         attn_send = attention_weight_grads(1 - core, *attn_lefts, block, planes)
         attn_keep = attention_weight_grads(core, *attn_lefts, block, planes)
         attn_received = swap(attn_send, "gc")
-        gate_sum, other_up, attn_keep, attn_received, keep_mine, recv_mine, *mine_far = tie(
-            gate_sum, theirs_sum[block : 2 * block], attn_keep, attn_received, keep_mine, recv_mine,
-            *mine_far,
+        attn_keep, attn_received, *mine_far = tie(attn_keep, attn_received, *mine_far)
+        attn_work = Scatter(attn_keep, attn_received)
+        attn_far = send_xy(attn_work.far_blocks())
+        tokens_far, theirs_sum, *attn_far = tie(tokens_far, theirs_sum, *attn_far)
+        attn_near = send_xy(attn_work.near_blocks(*attn_far))
+        tokens_near = across(jnp.concatenate([token_rows, tokens_far], axis=0), 1)
+        gate_sum = across(theirs_sum[:block], 2)
+        mine_second = mine.second_blocks(*mine_far)
+        gate_sum, tokens_near, other_up, *flat = tie(
+            gate_sum, tokens_near, theirs_sum[block : 2 * block], *attn_near, *mine_second
         )
-        attn_far = Scatter(attn_keep, attn_received).send_far()
-        tokens_far, other_down, attn_keep, attn_received, *attn_far = tie(
-            tokens_far, theirs_sum[2 * block :], attn_keep, attn_received, *attn_far
-        )
-        attn_work = Scatter(attn_keep, attn_received)
-        attn_near = attn_work.send_near(*attn_far)
         up_sum = across(other_up, 2)
-        tokens_near = across(jnp.concatenate([token_rows, tokens_far], axis=0), 1)
-        up_sum, keep_mine, recv_mine, *attn_near = tie(up_sum, keep_mine, recv_mine, *attn_near)
-        mine = Scatter(keep_mine, recv_mine)
-        mine_near = mine.send_near(*mine_far)
-        down_sum = across(other_down, 2)
-        grads = attn_work.total(*attn_near)
+        mine_first = send_xy(mine.first_blocks())
+        mine_second = flat[2:]
+        grads = attn_work.near_total(*flat[:2])
     else:
 
         def to_blocks(grad):
@@ -1291,12 +1298,16 @@
     grads = jnp.concatenate([grads[:, : block + small], rest], axis=1).astype(BF16)
     kept, passed = z_halve(grads)
     if square():
-        passed, down_sum = tie(passed, down_sum)
+        passed, up_sum, other_down, *mine_second = tie(
+            passed, up_sum, theirs_sum[2 * block :], *mine_second
+        )
+        mine_second = send_xy(mine_second)
+        down_sum = across(other_down, 2)
     else:
         tokens_near = across(jnp.concatenate([token_rows, tokens_far], axis=0), 1)
     grads = kept.astype(F32) + across(passed, 2).astype(F32)
     if square():
-        ffn_grad = mine.total(*mine_near) + jnp.concatenate(
+        ffn_grad = mine.total(mine_first, mine_second) + jnp.concatenate(
             [gate_sum, up_sum, down_sum], axis=0
         ).astype(F32)
     grad_tokens = spread_kernel(plane, (token_rows, tokens_far, tokens_near), (0, 2, 1, 3), F32)

time: 604 us -> 562 us (0.930)
  waiting for transfers between devices: 251 us -> 200 us
  other arithmetic: 40 us -> 52.1 us
    ppermute x36 -> x38, waiting for transfers between devices: 92.9 us -> 57.6 us  [swap(): return lax.ppermute(x, axis, SWAP)]
    ppermute x19 -> x18, waiting for transfers between devices: 154 us -> 135 us  [across(): return lax.ppermute(x, 'gx', [(i, i ^ distance) for i in range(4)])]
    convert_element_type x4 -> x10, other arithmetic: 9.37 us -> 25.1 us  [the longest x5 11.4 us: second_blocks(): return (to_x.astype(BF16), to_y.astype(BF16))]
    add x5 -> x4, other arithmetic: 12.8 us -> 5.41 us  [the longest x1 1.79 us: total(): self.part(self.here, True) + second[0].astype(F32) + first[1].astype(F32)]
    ppermute x19 -> x18, starting transfers between devices: 22.9 us -> 18.5 us  [across(): return lax.ppermute(x, 'gx', [(i, i ^ distance) for i in range(4)])]
    ppermute x36 -> x38, starting transfers between devices: 30.4 us -> 32 us  [swap(): return lax.ppermute(x, axis, SWAP)]
    unnamed x214 -> x230, local copies, waits for them, and re-layouts: 41.3 us -> 40.6 us
  transfers between devices with their start and end apart: 61 -> 62, of which waited for: 32 -> 28; matrix products, arithmetic and copies ran while one was open for 9% -> 11% of each run, Pallas kernels for 20% -> 22%
where the time goes in v3:
time: 562 us; the launch traced here: 555 us
  waiting for transfers between devices  200 us (36%)
  Pallas kernels  152 us (27%)
  local copies, waits for them, and re-layouts  65.9 us (12%)
  starting transfers between devices  60.5 us (11%)
  other arithmetic  52.1 us (9%)
  blocking collectives  19.9 us (4%)
    ppermute x18, waiting for transfers between devices, across(): return lax.ppermute(x, 'gx', [(i, i ^ distance) for i in range(4)])  135 us
    pallas_call x13, Pallas kernels, prefetch_call(): pl.pallas_call(kernel, grid_spec=pltpu.PrefetchScalarGridSpec(num_scalar_...  105 us
    ppermute x38, waiting for transfers between devices, swap(): return lax.ppermute(x, axis, SWAP)  57.6 us
    unnamed x230, local copies, waits for them, and re-layouts  40.6 us
    ppermute x38, starting transfers between devices, swap(): return lax.ppermute(x, axis, SWAP)  32 us
    pallas_call x4, Pallas kernels, ffn_weight_grads(): pl.pallas_call(kernel, grid_spec=pltpu.PrefetchScalarGridSpec(num_scalar_...  26.8 us
    all_gather x1, blocking collectives, body(): pack = lax.all_gather(pack, 'gx', axis=0)  19.9 us
    ppermute x18, starting transfers between devices, across(): return lax.ppermute(x, 'gx', [(i, i ^ distance) for i in range(4)])  18.5 us
  transfers between devices with their start and end apart: 62, of which 28 were waited for; matrix products, arithmetic and copies ran while one was open for 11% of the time, Pallas kernels for 22%

profile of v3, /device:TPU:0, one launch (start us, length us, event | category | flops | bytes accessed | tf_op | source)
XLA Modules:
  0.0 555.0 jit_solution(1917702378850355295)
XLA Ops:
  8.3 19.9 %all-gather = bf16[768,512]{1,0:T(8,128)(2,1)S(1)} all-gather(bf16[192,512]{1,0:T(8,128)(2,1)S(1)} %concatenate.58), channel_id=2, replica_groups=mesh['gx'=4,'gb'=2,'ga'=2,'gc'=2] {'gx'}, dimensions={0}, use_global_device_ids=true | all-gather | bytes 983040 | tf_op jit(solution)/shard_map/all_gather | solution.py:1049
  35.7 20.5 %collective-permute-done.2.refs_1_ = bf16[4,192,512]{2,1,0:T(8,128)(2,1)} collective-permute-done((bf16[4,192,512]{2,1,0:T(8,128)(2,1)S(1)}, bf16[4,192,512]{2,1,0:T(8,128)(2,1)}, u32[]{:S(2)}, u32[]{:S(2)}) %collective-permute-start.2) | collective-permute-done | bytes 786464 | tf_op jit(solution)/shard_map/ppermute | solution.py:44
  61.9 10.9 %collective-permute-done.6 = bf16[288,1728]{1,0:T(8,128)(2,1)} collective-permute-done((bf16[288,1728]{1,0:T(8,128)(2,1)}, bf16[288,1728]{1,0:T(8,128)(2,1)}, u32[]{:S(2)}, u32[]{:S(2)}) %collective-permute-start.6) | collective-permute-done | bytes 995360 | tf_op jit(solution)/shard_map/ppermute | solution.py:48
  140.8 12.7 %collective-permute-done.15.got = bf16[256,1024]{1,0:T(8,128)(2,1)S(1)} collective-permute-done((bf16[256,1024]{1,0:T(8,128)(2,1)}, bf16[256,1024]{1,0:T(8,128)(2,1)S(1)}, u32[]{:S(2)}, u32[]{:S(2)}) %collective-permute-start.15) | collective-permute-done | bytes 524320 | tf_op jit(solution)/shard_map/ppermute | solution.py:48
  167.2 15.5 %shard_map.306 = (bf16[512,1728]{1,0:T(8,128)(2,1)}, bf16[512,1728]{1,0:T(8,128)(2,1)}, bf16[512,1728]{1,0:T(8,128)(2,1)}, f32[512,1152]{1,0:T(8,128)}) custom-call(s32[8]{0:T(128)} %get-tuple-element.348.slots, bf16[512,1152]{1,0:T(8,128)(2,1)} %copy-done.9, bf16[1728,1728]{1,0:T(8,128)(2,1)} %shard_map.303.refs_0_.refs_1_, ...), custom_call_target="tpu_custom_call" | custom-call | flops 18400000000 | tf_op jit(solution)/shard_map/pallas_call | solution.py:325
  189.9 16.0 %shard_map.307 = (bf16[512,1728]{1,0:T(8,128)(2,1)}, bf16[512,1728]{1,0:T(8,128)(2,1)}, bf16[512,1728]{1,0:T(8,128)(2,1)}, f32[512,1152]{1,0:T(8,128)}) custom-call(s32[10]{0:T(128)} %xor_multiply_fusion.slots, bf16[512,1152]{1,0:T(8,128)(2,1)} %copy-done.9, f32[512,1152]{1,0:T(8,128)} %get-tuple-element.201.refs_0_, ...), custom_call_target="tpu_custom_call" | custom-call | flops 18400000000 | tf_op jit(solution)/shard_map/pallas_call | solution.py:325
  208.6 14.0 %collective-permute-done.25 = bf16[256,1152]{1,0:T(8,128)(2,1)S(1)} collective-permute-done((bf16[256,1152]{1,0:T(8,128)(2,1)S(1)}, bf16[256,1152]{1,0:T(8,128)(2,1)S(1)}, u32[]{:S(2)}, u32[]{:S(2)}) %collective-permute-start.25) | collective-permute-done | bytes 589856 | tf_op jit(solution)/shard_map/ppermute | solution.py:48
  228.6 10.1 %collective-permute-done.26.other_ref = bf16[256,1152]{1,0:T(8,128)(2,1)} collective-permute-done((bf16[256,1152]{1,0:T(8,128)(2,1)S(1)}, bf16[256,1152]{1,0:T(8,128)(2,1)}, u32[]{:S(2)}, u32[]{:S(2)}) %collective-permute-start.26) | collective-permute-done | bytes 589856 | tf_op jit(solution)/shard_map/ppermute | solution.py:48
  245.7 16.2 %shard_map.309 = (bf16[512,1728]{1,0:T(8,128)(2,1)}, bf16[512,1728]{1,0:T(8,128)(2,1)}, f32[512,1152]{1,0:T(8,128)}) custom-call(s32[10]{0:T(128)} %xor_multiply_fusion.slots, bf16[512,1152]{1,0:T(8,128)(2,1)} %copy-done.68, bf16[512,1728]{1,0:T(8,128)(2,1)} %get-tuple-element.209.act_ref, bf16[512,1728]{1,0:T(8,128)(2,1)} %get-tuple-element.210.slope_ref, ...), custom_call_target="tpu_custom_call" | custom-call | flops 18400000000 | tf_op jit(solution)/shard_map/pallas_call | solution.py:325
  266.2 6.7 %shard_map.311 = bf16[4,432,1728]{2,1,0:T(8,128)(2,1)} custom-call(s32[1]{0:T(128)} %bitcast.7.core_ref, bf16[1152,512]{1,0:T(8,128)(2,1)S(1)} %bitcast.113, bf16[1152,512]{1,0:T(8,128)(2,1)S(1)} %copy-done.66, bf16[512,1728]{1,0:T(8,128)(2,1)S(1)} %copy-done.76, bf16[512,1728]{1,0:T(8,128)(2,1)S(1)} %copy-done.77, ...), custom_call_target="tpu_custom_call" | custom-call | flops 7704999936 | tf_op jit(solution)/shard_map/pallas_call | solution.py:208
  272.9 6.6 %shard_map.310 = bf16[4,432,1728]{2,1,0:T(8,128)(2,1)} custom-call(s32[1]{0:T(128)} %bitcast.5.core_ref, bf16[1152,512]{1,0:T(8,128)(2,1)S(1)} %bitcast.114, bf16[1152,512]{1,0:T(8,128)(2,1)S(1)} %copy-done.66, bf16[512,1728]{1,0:T(8,128)(2,1)S(1)} %copy-done.76, bf16[512,1728]{1,0:T(8,128)(2,1)S(1)} %copy-done.77, ...), custom_call_target="tpu_custom_call" | custom-call | flops 7704999936 | tf_op jit(solution)/shard_map/pallas_call | solution.py:208
  279.5 15.9 %shard_map.312 = (bf16[512,1728]{1,0:T(8,128)(2,1)}, bf16[512,1728]{1,0:T(8,128)(2,1)}, f32[512,1152]{1,0:T(8,128)}) custom-call(s32[8]{0:T(128)} %get-tuple-element.348.slots, bf16[512,1152]{1,0:T(8,128)(2,1)} %copy-done.68, bf16[512,1728]{1,0:T(8,128)(2,1)} %get-tuple-element.207.act_ref, bf16[512,1728]{1,0:T(8,128)(2,1)} %get-tuple-element.208.slope_ref, ...), custom_call_target="tpu_custom_call" | custom-call | flops 18400000000 | tf_op jit(solution)/shard_map/pallas_call | solution.py:325
  315.1 11.7 %shard_map.313 = (f32[256,1152]{1,0:T(8,128)}, bf16[256,1152]{1,0:T(8,128)(2,1)}, bf16[1152,256]{1,0:T(8,128)(2,1)S(1)}, f32[2,1152]{1,0:T(2,128)S(1)}, bf16[256...) custom-call(s32[13]{0:T(128)S(1)} %copy-done.54, ...), custom_call_target="tpu_custom_call" | custom-call | flops 13799999488 | tf_op jit(solution)/shard_map/pallas_call | solution.py:325
  337.1 6.6 %shard_map.314 = bf16[4,432,1728]{2,1,0:T(8,128)(2,1)} custom-call(s32[1]{0:T(128)} %bitcast.5.core_ref, bf16[1152,512]{1,0:T(8,128)(2,1)S(1)} %bitcast.115, bf16[1152,512]{1,0:T(8,128)(2,1)S(1)} %copy-done.67, bf16[512,1728]{1,0:T(8,128)(2,1)S(1)} %copy-done.74, bf16[512,1728]{1,0:T(8,128)(2,1)S(1)} %copy-done.75, ...), custom_call_target="tpu_custom_call" | custom-call | flops 7704999936 | tf_op jit(solution)/shard_map/pallas_call | solution.py:208
  345.2 6.9 %shard_map.315 = bf16[4,432,1728]{2,1,0:T(8,128)(2,1)} custom-call(s32[1]{0:T(128)} %bitcast.7.core_ref, bf16[1152,512]{1,0:T(8,128)(2,1)S(1)} %bitcast.116, bf16[1152,512]{1,0:T(8,128)(2,1)S(1)} %copy-done.67, bf16[512,1728]{1,0:T(8,128)(2,1)S(1)} %copy-done.74, bf16[512,1728]{1,0:T(8,128)(2,1)S(1)} %copy-done.75, ...), custom_call_target="tpu_custom_call" | custom-call | flops 7704999936 | tf_op jit(solution)/shard_map/pallas_call | solution.py:208
  367.6 7.4 %collective-permute-done.42 = bf16[208,1728]{1,0:T(8,128)(2,1)} collective-permute-done((bf16[208,1728]{1,0:T(8,128)(2,1)}, bf16[208,1728]{1,0:T(8,128)(2,1)}, u32[]{:S(2)}, u32[]{:S(2)}) %collective-permute-start.42) | collective-permute-done | bytes 718880 | tf_op jit(solution)/shard_map/ppermute | solution.py:44
  383.3 12.1 %collective-permute-done.41.refs_1_ = bf16[256,512]{1,0:T(8,128)(2,1)S(1)} collective-permute-done((bf16[256,512]{1,0:T(8,128)(2,1)S(1)}, bf16[256,512]{1,0:T(8,128)(2,1)S(1)}, u32[]{:S(2)}, u32[]{:S(2)}) %collective-permute-start.41) | collective-permute-done | bytes 262176 | tf_op jit(solution)/shard_map/ppermute | solution.py:48
  423.5 12.2 %collective-permute-done.46 = bf16[208,1728]{1,0:T(8,128)(2,1)} collective-permute-done((bf16[208,1728]{1,0:T(8,128)(2,1)}, bf16[208,1728]{1,0:T(8,128)(2,1)}, u32[]{:S(2)}, u32[]{:S(2)}) %collective-permute-start.46) | collective-permute-done | bytes 718880 | tf_op jit(solution)/shard_map/ppermute | solution.py:44
  439.8 5.9 %collective-permute-done.44.refs_1_ = bf16[256,1152]{1,0:T(8,128)(2,1)} collective-permute-done((bf16[256,1152]{1,0:T(8,128)(2,1)}, bf16[256,1152]{1,0:T(8,128)(2,1)}, u32[]{:S(2)}, u32[]{:S(2)}) %collective-permute-start.44) | collective-permute-done | bytes 589856 | tf_op jit(solution)/shard_map/ppermute | solution.py:48
  462.0 27.6 %collective-permute-done.50 = bf16[144,1728]{1,0:T(8,128)(2,1)S(1)} collective-permute-done((bf16[144,1728]{1,0:T(8,128)(2,1)S(1)}, bf16[144,1728]{1,0:T(8,128)(2,1)S(1)}, u32[]{:S(2)}, u32[]{:S(2)}) %collective-permute-start.50) | collective-permute-done | bytes 497696 | tf_op jit(solution)/shard_map/ppermute | solution.py:48
  501.1 8.8 %collective-permute-done.54 = bf16[2,192,512]{2,1,0:T(8,128)(2,1)S(1)} collective-permute-done((bf16[2,192,512]{2,1,0:T(8,128)(2,1)S(1)}, bf16[2,192,512]{2,1,0:T(8,128)(2,1)S(1)}, u32[]{:S(2)}, u32[]{:S(2)}) %collective-permute-start.54) | collective-permute-done | bytes 393248 | tf_op jit(solution)/shard_map/ppermute | solution.py:48
  510.1 9.9 %collective-permute-done.55 = bf16[144,1728]{1,0:T(8,128)(2,1)S(1)} collective-permute-done((bf16[144,1728]{1,0:T(8,128)(2,1)S(1)}, bf16[144,1728]{1,0:T(8,128)(2,1)S(1)}, u32[]{:S(2)}, u32[]{:S(2)}) %collective-permute-start.55) | collective-permute-done | bytes 497696 | tf_op jit(solution)/shard_map/ppermute | solution.py:48
  532.1 7.8 %collective-permute-done.58 = bf16[208,1728]{1,0:T(8,128)(2,1)S(1)} collective-permute-done((bf16[208,1728]{1,0:T(8,128)(2,1)S(1)}, bf16[208,1728]{1,0:T(8,128)(2,1)S(1)}, u32[]{:S(2)}, u32[]{:S(2)}) %collective-permute-start.58) | collective-permute-done | bytes 718880 | tf_op jit(solution)/shard_map/ppermute | solution.py:44
  543.6 8.9 %collective-permute-done.61 = bf16[144,1728]{1,0:T(8,128)(2,1)S(1)} collective-permute-done((bf16[144,1728]{1,0:T(8,128)(2,1)S(1)}, bf16[144,1728]{1,0:T(8,128)(2,1)S(1)}, u32[]{:S(2)}, u32[]{:S(2)}) %collective-permute-start.61) | collective-permute-done | bytes 497696 | tf_op jit(solution)/shard_map/ppermute | solution.py:48
  (459 shorter events, 261.9 us)
Async XLA Ops:
  2.4 55.3 %collective-permute-start = (bf16[432,1728]{1,0:T(8,128)(2,1)S(1)}, bf16[432,1728]{1,0:T(8,128)(2,1)}, u32[]{:S(2)}, u32[]{:S(2)}) collective-permute-start(bf16[432,1728]{1,0:T(8,128)(2,1)S(1)} %pad_maximum_fusion.refs_0_), channel_id=1, source_target_pairs={{0,2},{2,0},{1,3},{3,1},{4,6},{6,4},{5,7},{7,5},{8,10},{10,8},{9,1... | collective-permute-start | bytes 4478984 | tf_op jit(solution)/shard_map/ppermute | solution.py:44
  5.4 52.3 %collective-permute-start.1 = (bf16[432,1728]{1,0:T(8,128)(2,1)S(1)}, bf16[432,1728]{1,0:T(8,128)(2,1)}, u32[]{:S(2)}, u32[]{:S(2)}) collective-permute-start(bf16[432,1728]{1,0:T(8,128)(2,1)S(1)} %pad_maximum_fusion.refs_0_), channel_id=1, source_target_pairs={{0,4},{4,0},{1,5},{5,1},{2,6},{6,2},{3,7},{7,3},{8,12},{12,8},{9,1... | collective-permute-start | bytes 4478984 | tf_op jit(solution)/shard_map/ppermute | solution.py:44
  28.2 28.0 %collective-permute-start.2 = (bf16[4,192,512]{2,1,0:T(8,128)(2,1)S(1)}, bf16[4,192,512]{2,1,0:T(8,128)(2,1)}, u32[]{:S(2)}, u32[]{:S(2)}) collective-permute-start(bf16[4,192,512]{2,1,0:T(8,128)(2,1)S(1)} %bitcast.117), channel_id=1, source_target_pairs={{0,2},{2,0},{1,3},{3,1},{4,6},{6,4},{5,7},{7,5},{8,10},{10,8},{9,1... | collective-permute-start | bytes 2359304 | tf_op jit(solution)/shard_map/ppermute | solution.py:44
  28.7 28.9 %collective-permute-start.3 = (bf16[4,192,512]{2,1,0:T(8,128)(2,1)S(1)}, bf16[4,192,512]{2,1,0:T(8,128)(2,1)}, u32[]{:S(2)}, u32[]{:S(2)}) collective-permute-start(bf16[4,192,512]{2,1,0:T(8,128)(2,1)S(1)} %bitcast.118), channel_id=1, source_target_pairs={{0,4},{4,0},{1,5},{5,1},{2,6},{6,2},{3,7},{7,3},{8,12},{12,8},{9,1... | collective-permute-start | bytes 2359304 | tf_op jit(solution)/shard_map/ppermute | solution.py:44
  29.3 43.5 %collective-permute-start.6 = (bf16[288,1728]{1,0:T(8,128)(2,1)}, bf16[288,1728]{1,0:T(8,128)(2,1)}, u32[]{:S(2)}, u32[]{:S(2)}) collective-permute-start(bf16[288,1728]{1,0:T(8,128)(2,1)} %pad_maximum_fusion.4), channel_id=1, source_target_pairs={{0,16},{8,24},{16,0},{24,8},{1,17},{9,25},{17,1},{25,9},{2,18},{10... | collective-permute-start | bytes 2985992 | tf_op jit(solution)/shard_map/ppermute | solution.py:48
  77.5 29.0 %collective-permute-start.10 = (bf16[224,1728]{1,0:T(8,128)(2,1)}, bf16[224,1728]{1,0:T(8,128)(2,1)}, u32[]{:S(2)}, u32[]{:S(2)}) collective-permute-start(bf16[224,1728]{1,0:T(8,128)(2,1)} %slice.334), channel_id=1, source_target_pairs={{0,4},{4,0},{1,5},{5,1},{2,6},{6,2},{3,7},{7,3},{8,12},{12,8},{9,1... | collective-permute-start | bytes 2322440 | tf_op jit(solution)/shard_map/ppermute | solution.py:44
  81.0 25.4 %collective-permute-start.9 = (bf16[208,1728]{1,0:T(8,128)(2,1)}, bf16[208,1728]{1,0:T(8,128)(2,1)}, u32[]{:S(2)}, u32[]{:S(2)}) collective-permute-start(bf16[208,1728]{1,0:T(8,128)(2,1)} %slice.333), channel_id=1, source_target_pairs={{0,2},{2,0},{1,3},{3,1},{4,6},{6,4},{5,7},{7,5},{8,10},{10,8},{9,1... | collective-permute-start | bytes 2156552 | tf_op jit(solution)/shard_map/ppermute | solution.py:44
  82.5 25.4 %collective-permute-start.8 = (bf16[144,1728]{1,0:T(8,128)(2,1)}, bf16[144,1728]{1,0:T(8,128)(2,1)}, u32[]{:S(2)}, u32[]{:S(2)}) collective-permute-start(bf16[144,1728]{1,0:T(8,128)(2,1)} %bitcast.2), channel_id=1, source_target_pairs={{0,16},{8,24},{16,0},{24,8},{1,17},{9,25},{17,1},{25,9},{2,18},{10... | collective-permute-start | bytes 1493000 | tf_op jit(solution)/shard_map/ppermute | solution.py:48
  122.2 39.5 %collective-permute-start.16 = (bf16[432,1728]{1,0:T(8,128)(2,1)}, bf16[432,1728]{1,0:T(8,128)(2,1)}, u32[]{:S(2)}, u32[]{:S(2)}) collective-permute-start(bf16[432,1728]{1,0:T(8,128)(2,1)} %pad_maximum_fusion.1.refs_1_.refs_0_), channel_id=1, source_target_pairs={{0,2},{2,0},{1,3},{3,1},{4,6},{6,4},{5,7},{7,5},{8,10},{10,8},{9,1... | collective-permute-start | bytes 4478984 | tf_op jit(solution)/shard_map/ppermute | solution.py:44
  123.8 37.8 %collective-permute-start.17 = (bf16[432,1728]{1,0:T(8,128)(2,1)}, bf16[432,1728]{1,0:T(8,128)(2,1)}, u32[]{:S(2)}, u32[]{:S(2)}) collective-permute-start(bf16[432,1728]{1,0:T(8,128)(2,1)} %pad_maximum_fusion.1.refs_1_.refs_0_), channel_id=1, source_target_pairs={{0,4},{4,0},{1,5},{5,1},{2,6},{6,2},{3,7},{7,3},{8,12},{12,8},{9,1... | collective-permute-start | bytes 4478984 | tf_op jit(solution)/shard_map/ppermute | solution.py:44
  140.7 44.9 %collective-permute-start.20 = (bf16[432,1728]{1,0:T(8,128)(2,1)}, bf16[432,1728]{1,0:T(8,128)(2,1)}, u32[]{:S(2)}, u32[]{:S(2)}) collective-permute-start(bf16[432,1728]{1,0:T(8,128)(2,1)} %pad_maximum_fusion.1.refs_1_.refs_0_), channel_id=1, source_target_pairs={{0,1},{1,0},{2,3},{3,2},{4,5},{5,4},{6,7},{7,6},{8,9},{9,8},{10,11... | collective-permute-start | bytes 4478984 | tf_op jit(solution)/shard_map/ppermute | solution.py:44
  162.9 25.2 %collective-permute-start.21 = (bf16[432,1728]{1,0:T(8,128)(2,1)}, bf16[432,1728]{1,0:T(8,128)(2,1)}, u32[]{:S(2)}, u32[]{:S(2)}) collective-permute-start(bf16[432,1728]{1,0:T(8,128)(2,1)} %collective-permute-done.16.refs_2_.refs_1_), channel_id=1, source_target_pairs={{0,1},{1,0},{2,3},{3,2},{4,5},{5,4},{6,7},{7,6},{8,9},{9,8},{10,11... | collective-permute-start | bytes 4478984 | tf_op jit(solution)/shard_map/ppermute | solution.py:44
  244.2 35.3 %collective-permute-start.27 = (bf16[256,1152]{1,0:T(8,128)(2,1)S(1)}, bf16[256,1152]{1,0:T(8,128)(2,1)S(1)}, u32[]{:S(2)}, u32[]{:S(2)}) collective-permute-start(bf16[256,1152]{1,0:T(8,128)(2,1)S(1)} %slice.342), channel_id=1, source_target_pairs={{0,16},{8,24},{16,0},{24,8},{1,17},{9,25},{17,1},{25,9},{2,18},{10... | collective-permute-start | bytes 1769480 | tf_op jit(solution)/shard_map/ppermute | solution.py:48
  301.4 25.5 %collective-permute-start.36 = (bf16[208,1728]{1,0:T(8,128)(2,1)S(1)}, bf16[208,1728]{1,0:T(8,128)(2,1)S(1)}, u32[]{:S(2)}, u32[]{:S(2)}) collective-permute-start(bf16[208,1728]{1,0:T(8,128)(2,1)S(1)} %get-tuple-element.307), channel_id=1, source_target_pairs={{0,2},{2,0},{1,3},{3,1},{4,6},{6,4},{5,7},{7,5},{8,10},{10,8},{9,1... | collective-permute-start | bytes 2156552 | tf_op jit(solution)/shard_map/ppermute | solution.py:44
  306.4 37.3 %collective-permute-start.34 = (bf16[224,1728]{1,0:T(8,128)(2,1)S(1)}, bf16[224,1728]{1,0:T(8,128)(2,1)S(1)}, u32[]{:S(2)}, u32[]{:S(2)}) collective-permute-start(bf16[224,1728]{1,0:T(8,128)(2,1)S(1)} %get-tuple-element.310), channel_id=1, source_target_pairs={{0,4},{4,0},{1,5},{5,1},{2,6},{6,2},{3,7},{7,3},{8,12},{12,8},{9,1... | collective-permute-start | bytes 2322440 | tf_op jit(solution)/shard_map/ppermute | solution.py:44
  307.7 36.0 %collective-permute-start.33 = (bf16[208,1728]{1,0:T(8,128)(2,1)}, bf16[208,1728]{1,0:T(8,128)(2,1)}, u32[]{:S(2)}, u32[]{:S(2)}) collective-permute-start(bf16[208,1728]{1,0:T(8,128)(2,1)} %get-tuple-element.308), channel_id=1, source_target_pairs={{0,2},{2,0},{1,3},{3,1},{4,6},{6,4},{5,7},{7,5},{8,10},{10,8},{9,1... | collective-permute-start | bytes 2156552 | tf_op jit(solution)/shard_map/ppermute | solution.py:44
  409.8 25.9 %collective-permute-start.45 = (bf16[4,768,512]{2,1,0:T(8,128)(2,1)}, bf16[4,768,512]{2,1,0:T(8,128)(2,1)}, u32[]{:S(2)}, u32[]{:S(2)}) collective-permute-start(bf16[4,768,512]{2,1,0:T(8,128)(2,1)} %shard_map.320), channel_id=1, source_target_pairs={{0,1},{1,0},{2,3},{3,2},{4,5},{5,4},{6,7},{7,6},{8,9},{9,8},{10,11... | collective-permute-start | bytes 9437192 | tf_op jit(solution)/shard_map/ppermute | solution.py:44
  417.1 28.6 %collective-permute-start.44 = (bf16[256,1152]{1,0:T(8,128)(2,1)}, bf16[256,1152]{1,0:T(8,128)(2,1)}, u32[]{:S(2)}, u32[]{:S(2)}) collective-permute-start(bf16[256,1152]{1,0:T(8,128)(2,1)} %get-tuple-element.268.refs_0_), channel_id=1, source_target_pairs={{0,16},{8,24},{16,0},{24,8},{1,17},{9,25},{17,1},{25,9},{2,18},{10... | collective-permute-start | bytes 1769480 | tf_op jit(solution)/shard_map/ppermute | solution.py:48
  451.0 38.6 %collective-permute-start.53 = (bf16[768,512]{1,0:T(8,128)(2,1)S(1)}, bf16[768,512]{1,0:T(8,128)(2,1)S(1)}, u32[]{:S(2)}, u32[]{:S(2)}) collective-permute-start(bf16[768,512]{1,0:T(8,128)(2,1)S(1)} %pad_maximum_fusion.6), channel_id=1, source_target_pairs={{0,4},{4,0},{1,5},{5,1},{2,6},{6,2},{3,7},{7,3},{8,12},{12,8},{9,1... | collective-permute-start | bytes 2359304 | tf_op jit(solution)/shard_map/ppermute | solution.py:44
  452.1 37.5 %collective-permute-start.52 = (bf16[768,512]{1,0:T(8,128)(2,1)S(1)}, bf16[768,512]{1,0:T(8,128)(2,1)S(1)}, u32[]{:S(2)}, u32[]{:S(2)}) collective-permute-start(bf16[768,512]{1,0:T(8,128)(2,1)S(1)} %pad_maximum_fusion.5), channel_id=1, source_target_pairs={{0,2},{2,0},{1,3},{3,1},{4,6},{6,4},{5,7},{7,5},{8,10},{10,8},{9,1... | collective-permute-start | bytes 2359304 | tf_op jit(solution)/shard_map/ppermute | solution.py:44
  455.2 36.6 %collective-permute-start.51 = (bf16[512,1152]{1,0:T(8,128)(2,1)S(1)}, bf16[512,1152]{1,0:T(8,128)(2,1)S(1)}, u32[]{:S(2)}, u32[]{:S(2)}) collective-permute-start(bf16[512,1152]{1,0:T(8,128)(2,1)S(1)} %pad_maximum_fusion.3), channel_id=1, source_target_pairs={{0,8},{8,0},{16,24},{24,16},{1,9},{9,1},{17,25},{25,17},{2,10},{10... | collective-permute-start | bytes 3538952 | tf_op jit(solution)/shard_map/ppermute | solution.py:48
  455.4 34.2 %collective-permute-start.50 = (bf16[144,1728]{1,0:T(8,128)(2,1)S(1)}, bf16[144,1728]{1,0:T(8,128)(2,1)S(1)}, u32[]{:S(2)}, u32[]{:S(2)}) collective-permute-start(bf16[144,1728]{1,0:T(8,128)(2,1)S(1)} %get-tuple-element.326), channel_id=1, source_target_pairs={{0,16},{8,24},{16,0},{24,8},{1,17},{9,25},{17,1},{25,9},{2,18},{10... | collective-permute-start | bytes 1493000 | tf_op jit(solution)/shard_map/ppermute | solution.py:48
  499.5 32.6 %collective-permute-start.57 = (bf16[208,1728]{1,0:T(8,128)(2,1)S(1)}, bf16[208,1728]{1,0:T(8,128)(2,1)S(1)}, u32[]{:S(2)}, u32[]{:S(2)}) collective-permute-start(bf16[208,1728]{1,0:T(8,128)(2,1)S(1)} %copy-done.92), channel_id=1, source_target_pairs={{0,2},{2,0},{1,3},{3,1},{4,6},{6,4},{5,7},{7,5},{8,10},{10,8},{9,1... | collective-permute-start | bytes 2156552 | tf_op jit(solution)/shard_map/ppermute | solution.py:44
  500.1 41.5 %collective-permute-start.60 = (bf16[224,1728]{1,0:T(8,128)(2,1)S(1)}, bf16[224,1728]{1,0:T(8,128)(2,1)S(1)}, u32[]{:S(2)}, u32[]{:S(2)}) collective-permute-start(bf16[224,1728]{1,0:T(8,128)(2,1)S(1)} %copy-done.91), channel_id=1, source_target_pairs={{0,4},{4,0},{1,5},{5,1},{2,6},{6,2},{3,7},{7,3},{8,12},{12,8},{9,1... | collective-permute-start | bytes 2322440 | tf_op jit(solution)/shard_map/ppermute | solution.py:44
  (151 other events, 1377.2 us)

commit v4 on v3

--- a/solution.py
+++ b/solution.py
@@ -971,7 +971,7 @@
         out_shape=[like(shape, BF16)] * 2,
         in_specs=[whole(pltpu.SMEM)] + [whole(pltpu.VMEM)] * 6,
         out_specs=[whole(pltpu.VMEM)] * 2,
-        compiler_params=params(32),
+        compiler_params=params(58),
         cost_estimate=cost(2.4),
     )(flags, d_self, d_a, d_b, back_1, back_2, back_3)
 
@@ -1222,11 +1222,12 @@
     own_terms = [kept, across(passed, 2)]
     if square():
         mine = Scatter(keep_mine, recv_mine)
-        mine_far = send_xy(mine.far_blocks())
+        mine_far = mine.far_blocks()
         theirs_sum = theirs.total(theirs_first, theirs_second).astype(BF16)
-        own_terms[1], theirs_sum, d_normed_query, d_gains_mid, d_gain_last, d_gain_query = tie(
-            own_terms[1], theirs_sum, d_normed_query, d_gains_mid, d_gain_last, d_gain_query
+        own_terms[1], theirs_sum, d_normed_query, d_gains_mid, d_gain_last, d_gain_query, *mine_far = tie(
+            own_terms[1], theirs_sum, d_normed_query, d_gains_mid, d_gain_last, d_gain_query, *mine_far
         )
+        mine_far = send_xy(mine_far)
     d_kv_low, token_rows, d_gain_key, d_gain_in = tokens_back_kernel(
         plane, own_terms, key_raw, gain_key, cos_table, sin_table, wkv, d_normed_query, d_mid,
         tokens, gain_in,
@@ -1259,10 +1260,11 @@
         attn_send = attention_weight_grads(1 - core, *attn_lefts, block, planes)
         attn_keep = attention_weight_grads(core, *attn_lefts, block, planes)
         attn_received = swap(attn_send, "gc")
-        attn_keep, attn_received, *mine_far = tie(attn_keep, attn_received, *mine_far)
+        attn_keep, attn_received = tie(attn_keep, attn_received)
         attn_work = Scatter(attn_keep, attn_received)
         attn_far = send_xy(attn_work.far_blocks())
-        tokens_far, theirs_sum, *attn_far = tie(tokens_far, theirs_sum, *attn_far)
+        tokens_far, theirs_sum, *flat = tie(tokens_far, theirs_sum, *attn_far, *mine_far)
+        attn_far, mine_far = flat[:2], flat[2:]
         attn_near = send_xy(attn_work.near_blocks(*attn_far))
         tokens_near = across(jnp.concatenate([token_rows, tokens_far], axis=0), 1)
         gate_sum = across(theirs_sum[:block], 2)

time: 562 us -> 547 us (0.973)
  waiting for transfers between devices: 200 us -> 186 us
  local copies, waits for them, and re-layouts: 65.9 us -> 58.4 us
    ppermute x38, waiting for transfers between devices: 57.6 us -> 46.9 us  [swap(): return lax.ppermute(x, axis, SWAP)]
    unnamed x230 -> x216, local copies, waits for them, and re-layouts: 40.6 us -> 35.6 us
  transfers between devices with their start and end apart: 62 -> 62, of which waited for: 28 -> 25; matrix products, arithmetic and copies ran while one was open for 11% -> 11% of each run, Pallas kernels for 22% -> 23%
where the time goes in v4:
time: 547 us; the launch traced here: 536 us
  waiting for transfers between devices  186 us (34%)
  Pallas kernels  153 us (28%)
  starting transfers between devices  62.8 us (11%)
  local copies, waits for them, and re-layouts  58.4 us (11%)
  other arithmetic  52.4 us (10%)
  blocking collectives  19.9 us (4%)
    ppermute x18, waiting for transfers between devices, across(): return lax.ppermute(x, 'gx', [(i, i ^ distance) for i in range(4)])  132 us
    pallas_call x13, Pallas kernels, prefetch_call(): pl.pallas_call(kernel, grid_spec=pltpu.PrefetchScalarGridSpec(num_scalar_...  105 us
    ppermute x38, waiting for transfers between devices, swap(): return lax.ppermute(x, axis, SWAP)  46.9 us
    unnamed x216, local copies, waits for them, and re-layouts  35.6 us
    ppermute x38, starting transfers between devices, swap(): return lax.ppermute(x, axis, SWAP)  33.7 us
    pallas_call x4, Pallas kernels, ffn_weight_grads(): pl.pallas_call(kernel, grid_spec=pltpu.PrefetchScalarGridSpec(num_scalar_...  26.8 us
    all_gather x1, blocking collectives, body(): pack = lax.all_gather(pack, 'gx', axis=0)  19.9 us
    ppermute x18, starting transfers between devices, across(): return lax.ppermute(x, 'gx', [(i, i ^ distance) for i in range(4)])  19.2 us
  transfers between devices with their start and end apart: 62, of which 25 were waited for; matrix products, arithmetic and copies ran while one was open for 11% of the time, Pallas kernels for 23%

profile of v4, /device:TPU:0, one launch (start us, length us, event | category | flops | bytes accessed | tf_op | source)
XLA Modules:
  0.0 536.3 jit_solution(6735791909909342494)
XLA Ops:
  8.3 19.9 %all-gather = bf16[768,512]{1,0:T(8,128)(2,1)S(1)} all-gather(bf16[192,512]{1,0:T(8,128)(2,1)S(1)} %concatenate.58), channel_id=2, replica_groups=mesh['gx'=4,'gb'=2,'ga'=2,'gc'=2] {'gx'}, dimensions={0}, use_global_device_ids=true | all-gather | bytes 983040 | tf_op jit(solution)/shard_map/all_gather | solution.py:1049
  35.7 20.5 %collective-permute-done.2.refs_1_ = bf16[4,192,512]{2,1,0:T(8,128)(2,1)} collective-permute-done((bf16[4,192,512]{2,1,0:T(8,128)(2,1)S(1)}, bf16[4,192,512]{2,1,0:T(8,128)(2,1)}, u32[]{:S(2)}, u32[]{:S(2)}) %collective-permute-start.2) | collective-permute-done | bytes 786464 | tf_op jit(solution)/shard_map/ppermute | solution.py:44
  61.9 10.9 %collective-permute-done.6 = bf16[288,1728]{1,0:T(8,128)(2,1)} collective-permute-done((bf16[288,1728]{1,0:T(8,128)(2,1)}, bf16[288,1728]{1,0:T(8,128)(2,1)}, u32[]{:S(2)}, u32[]{:S(2)}) %collective-permute-start.6) | collective-permute-done | bytes 995360 | tf_op jit(solution)/shard_map/ppermute | solution.py:48
  92.4 5.8 %shard_map.301 = (bf16[1024,512]{1,0:T(8,128)(2,1)S(1)}, bf16[256,1152]{1,0:T(8,128)(2,1)S(1)}, f32[256,256]{1,0:T(8,128)S(1)}, bf16[256,512]{1,0:T(8,128)(2,1)}...) custom-call(s32[13]{0:T(128)S(1)} %copy-done.45, bf16[1024,1152]{1,0:T(8,128)(2,1)} %refs_9_.1, ...), custom_call_target="tpu_custom_call" | custom-call | flops 6899999744 | tf_op jit(solution)/shard_map/pallas_call | solution.py:325
  140.7 12.7 %collective-permute-done.15.got = bf16[256,1024]{1,0:T(8,128)(2,1)S(1)} collective-permute-done((bf16[256,1024]{1,0:T(8,128)(2,1)}, bf16[256,1024]{1,0:T(8,128)(2,1)S(1)}, u32[]{:S(2)}, u32[]{:S(2)}) %collective-permute-start.15) | collective-permute-done | bytes 524320 | tf_op jit(solution)/shard_map/ppermute | solution.py:48
  167.2 15.5 %shard_map.306 = (bf16[512,1728]{1,0:T(8,128)(2,1)}, bf16[512,1728]{1,0:T(8,128)(2,1)}, bf16[512,1728]{1,0:T(8,128)(2,1)}, f32[512,1152]{1,0:T(8,128)}) custom-call(s32[8]{0:T(128)} %get-tuple-element.352.slots, bf16[512,1152]{1,0:T(8,128)(2,1)} %copy-done.9, bf16[1728,1728]{1,0:T(8,128)(2,1)} %shard_map.303.refs_0_.refs_1_, ...), custom_call_target="tpu_custom_call" | custom-call | flops 18400000000 | tf_op jit(solution)/shard_map/pallas_call | solution.py:325
  189.8 15.8 %shard_map.307 = (bf16[512,1728]{1,0:T(8,128)(2,1)}, bf16[512,1728]{1,0:T(8,128)(2,1)}, bf16[512,1728]{1,0:T(8,128)(2,1)}, f32[512,1152]{1,0:T(8,128)}) custom-call(s32[10]{0:T(128)} %xor_multiply_fusion.slots, bf16[512,1152]{1,0:T(8,128)(2,1)} %copy-done.9, f32[512,1152]{1,0:T(8,128)} %get-tuple-element.203.refs_0_, ...), custom_call_target="tpu_custom_call" | custom-call | flops 18400000000 | tf_op jit(solution)/shard_map/pallas_call | solution.py:325
  208.3 14.1 %collective-permute-done.25 = bf16[256,1152]{1,0:T(8,128)(2,1)S(1)} collective-permute-done((bf16[256,1152]{1,0:T(8,128)(2,1)S(1)}, bf16[256,1152]{1,0:T(8,128)(2,1)S(1)}, u32[]{:S(2)}, u32[]{:S(2)}) %collective-permute-start.25) | collective-permute-done | bytes 589856 | tf_op jit(solution)/shard_map/ppermute | solution.py:48
  228.4 10.1 %collective-permute-done.26.other_ref = bf16[256,1152]{1,0:T(8,128)(2,1)} collective-permute-done((bf16[256,1152]{1,0:T(8,128)(2,1)S(1)}, bf16[256,1152]{1,0:T(8,128)(2,1)}, u32[]{:S(2)}, u32[]{:S(2)}) %collective-permute-start.26) | collective-permute-done | bytes 589856 | tf_op jit(solution)/shard_map/ppermute | solution.py:48
  245.6 16.2 %shard_map.309 = (bf16[512,1728]{1,0:T(8,128)(2,1)}, bf16[512,1728]{1,0:T(8,128)(2,1)}, f32[512,1152]{1,0:T(8,128)}) custom-call(s32[10]{0:T(128)} %xor_multiply_fusion.slots, bf16[512,1152]{1,0:T(8,128)(2,1)} %copy-done.59, bf16[512,1728]{1,0:T(8,128)(2,1)} %get-tuple-element.211.act_ref, bf16[512,1728]{1,0:T(8,128)(2,1)} %get-tuple-element.212.slope_ref, ...), custom_call_target="tpu_custom_call" | custom-call | flops 18400000000 | tf_op jit(solution)/shard_map/pallas_call | solution.py:325
  266.0 6.6 %shard_map.311 = bf16[4,432,1728]{2,1,0:T(8,128)(2,1)} custom-call(s32[1]{0:T(128)} %bitcast.7.core_ref, bf16[1152,512]{1,0:T(8,128)(2,1)S(1)} %bitcast.113, bf16[1152,512]{1,0:T(8,128)(2,1)S(1)} %copy-done.57, bf16[512,1728]{1,0:T(8,128)(2,1)S(1)} %copy-done.67, bf16[512,1728]{1,0:T(8,128)(2,1)S(1)} %copy-done.68, ...), custom_call_target="tpu_custom_call" | custom-call | flops 7704999936 | tf_op jit(solution)/shard_map/pallas_call | solution.py:208
  272.7 6.6 %shard_map.310 = bf16[4,432,1728]{2,1,0:T(8,128)(2,1)} custom-call(s32[1]{0:T(128)} %bitcast.5.core_ref, bf16[1152,512]{1,0:T(8,128)(2,1)S(1)} %bitcast.114, bf16[1152,512]{1,0:T(8,128)(2,1)S(1)} %copy-done.57, bf16[512,1728]{1,0:T(8,128)(2,1)S(1)} %copy-done.67, bf16[512,1728]{1,0:T(8,128)(2,1)S(1)} %copy-done.68, ...), custom_call_target="tpu_custom_call" | custom-call | flops 7704999936 | tf_op jit(solution)/shard_map/pallas_call | solution.py:208
  279.3 16.1 %shard_map.312 = (bf16[512,1728]{1,0:T(8,128)(2,1)}, bf16[512,1728]{1,0:T(8,128)(2,1)}, f32[512,1152]{1,0:T(8,128)}) custom-call(s32[8]{0:T(128)} %get-tuple-element.352.slots, bf16[512,1152]{1,0:T(8,128)(2,1)} %copy-done.59, bf16[512,1728]{1,0:T(8,128)(2,1)} %get-tuple-element.209.act_ref, bf16[512,1728]{1,0:T(8,128)(2,1)} %get-tuple-element.210.slope_ref, ...), custom_call_target="tpu_custom_call" | custom-call | flops 18400000000 | tf_op jit(solution)/shard_map/pallas_call | solution.py:325
  308.0 5.5 %collective-permute-done.29.got_ref = bf16[256,1152]{1,0:T(8,128)(2,1)S(1)} collective-permute-done((bf16[256,1152]{1,0:T(8,128)(2,1)}, bf16[256,1152]{1,0:T(8,128)(2,1)S(1)}, u32[]{:S(2)}, u32[]{:S(2)}) %collective-permute-start.29) | collective-permute-done | bytes 589856 | tf_op jit(solution)/shard_map/ppermute | solution.py:48
  315.1 11.7 %shard_map.313 = (f32[256,1152]{1,0:T(8,128)}, bf16[256,1152]{1,0:T(8,128)(2,1)}, bf16[1152,256]{1,0:T(8,128)(2,1)S(1)}, f32[2,1152]{1,0:T(2,128)S(1)}, bf16[256...) custom-call(s32[13]{0:T(128)S(1)} %copy-done.46, ...), custom_call_target="tpu_custom_call" | custom-call | flops 13799999488 | tf_op jit(solution)/shard_map/pallas_call | solution.py:325
  337.1 6.7 %shard_map.314 = bf16[4,432,1728]{2,1,0:T(8,128)(2,1)} custom-call(s32[1]{0:T(128)} %bitcast.5.core_ref, bf16[1152,512]{1,0:T(8,128)(2,1)S(1)} %bitcast.115, bf16[1152,512]{1,0:T(8,128)(2,1)S(1)} %copy-done.58, bf16[512,1728]{1,0:T(8,128)(2,1)S(1)} %copy-done.65, bf16[512,1728]{1,0:T(8,128)(2,1)S(1)} %copy-done.66, ...), custom_call_target="tpu_custom_call" | custom-call | flops 7704999936 | tf_op jit(solution)/shard_map/pallas_call | solution.py:208
  345.3 6.8 %shard_map.315 = bf16[4,432,1728]{2,1,0:T(8,128)(2,1)} custom-call(s32[1]{0:T(128)} %bitcast.7.core_ref, bf16[1152,512]{1,0:T(8,128)(2,1)S(1)} %bitcast.116, bf16[1152,512]{1,0:T(8,128)(2,1)S(1)} %copy-done.58, bf16[512,1728]{1,0:T(8,128)(2,1)S(1)} %copy-done.65, bf16[512,1728]{1,0:T(8,128)(2,1)S(1)} %copy-done.66, ...), custom_call_target="tpu_custom_call" | custom-call | flops 7704999936 | tf_op jit(solution)/shard_map/pallas_call | solution.py:208
  362.4 12.7 %collective-permute-done.42 = bf16[208,1728]{1,0:T(8,128)(2,1)} collective-permute-done((bf16[208,1728]{1,0:T(8,128)(2,1)}, bf16[208,1728]{1,0:T(8,128)(2,1)}, u32[]{:S(2)}, u32[]{:S(2)}) %collective-permute-start.42) | collective-permute-done | bytes 718880 | tf_op jit(solution)/shard_map/ppermute | solution.py:44
  390.2 6.9 %collective-permute-done.41.refs_1_ = bf16[256,512]{1,0:T(8,128)(2,1)S(1)} collective-permute-done((bf16[256,512]{1,0:T(8,128)(2,1)S(1)}, bf16[256,512]{1,0:T(8,128)(2,1)S(1)}, u32[]{:S(2)}, u32[]{:S(2)}) %collective-permute-start.41) | collective-permute-done | bytes 262176 | tf_op jit(solution)/shard_map/ppermute | solution.py:48
  421.4 16.0 %collective-permute-done.44.refs_1_ = bf16[256,1152]{1,0:T(8,128)(2,1)} collective-permute-done((bf16[256,1152]{1,0:T(8,128)(2,1)}, bf16[256,1152]{1,0:T(8,128)(2,1)}, u32[]{:S(2)}, u32[]{:S(2)}) %collective-permute-start.44) | collective-permute-done | bytes 589856 | tf_op jit(solution)/shard_map/ppermute | solution.py:48
  448.3 31.3 %collective-permute-done.50 = bf16[144,1728]{1,0:T(8,128)(2,1)S(1)} collective-permute-done((bf16[144,1728]{1,0:T(8,128)(2,1)S(1)}, bf16[144,1728]{1,0:T(8,128)(2,1)S(1)}, u32[]{:S(2)}, u32[]{:S(2)}) %collective-permute-start.50) | collective-permute-done | bytes 497696 | tf_op jit(solution)/shard_map/ppermute | solution.py:48
  491.4 7.5 %collective-permute-done.54 = bf16[2,192,512]{2,1,0:T(8,128)(2,1)S(1)} collective-permute-done((bf16[2,192,512]{2,1,0:T(8,128)(2,1)S(1)}, bf16[2,192,512]{2,1,0:T(8,128)(2,1)S(1)}, u32[]{:S(2)}, u32[]{:S(2)}) %collective-permute-start.54) | collective-permute-done | bytes 393248 | tf_op jit(solution)/shard_map/ppermute | solution.py:48
  499.0 9.7 %collective-permute-done.55 = bf16[144,1728]{1,0:T(8,128)(2,1)S(1)} collective-permute-done((bf16[144,1728]{1,0:T(8,128)(2,1)S(1)}, bf16[144,1728]{1,0:T(8,128)(2,1)S(1)}, u32[]{:S(2)}, u32[]{:S(2)}) %collective-permute-start.55) | collective-permute-done | bytes 497696 | tf_op jit(solution)/shard_map/ppermute | solution.py:48
  520.7 7.5 %collective-permute-done.58 = bf16[208,1728]{1,0:T(8,128)(2,1)S(1)} collective-permute-done((bf16[208,1728]{1,0:T(8,128)(2,1)S(1)}, bf16[208,1728]{1,0:T(8,128)(2,1)S(1)}, u32[]{:S(2)}, u32[]{:S(2)}) %collective-permute-start.58) | collective-permute-done | bytes 718880 | tf_op jit(solution)/shard_map/ppermute | solution.py:44
  (445 shorter events, 241.0 us)
Async XLA Ops:
  2.4 55.3 %collective-permute-start = (bf16[432,1728]{1,0:T(8,128)(2,1)S(1)}, bf16[432,1728]{1,0:T(8,128)(2,1)}, u32[]{:S(2)}, u32[]{:S(2)}) collective-permute-start(bf16[432,1728]{1,0:T(8,128)(2,1)S(1)} %pad_maximum_fusion.refs_0_), channel_id=1, source_target_pairs={{0,2},{2,0},{1,3},{3,1},{4,6},{6,4},{5,7},{7,5},{8,10},{10,8},{9,1... | collective-permute-start | bytes 4478984 | tf_op jit(solution)/shard_map/ppermute | solution.py:44
  5.4 52.3 %collective-permute-start.1 = (bf16[432,1728]{1,0:T(8,128)(2,1)S(1)}, bf16[432,1728]{1,0:T(8,128)(2,1)}, u32[]{:S(2)}, u32[]{:S(2)}) collective-permute-start(bf16[432,1728]{1,0:T(8,128)(2,1)S(1)} %pad_maximum_fusion.refs_0_), channel_id=1, source_target_pairs={{0,4},{4,0},{1,5},{5,1},{2,6},{6,2},{3,7},{7,3},{8,12},{12,8},{9,1... | collective-permute-start | bytes 4478984 | tf_op jit(solution)/shard_map/ppermute | solution.py:44
  28.2 28.0 %collective-permute-start.2 = (bf16[4,192,512]{2,1,0:T(8,128)(2,1)S(1)}, bf16[4,192,512]{2,1,0:T(8,128)(2,1)}, u32[]{:S(2)}, u32[]{:S(2)}) collective-permute-start(bf16[4,192,512]{2,1,0:T(8,128)(2,1)S(1)} %bitcast.117), channel_id=1, source_target_pairs={{0,2},{2,0},{1,3},{3,1},{4,6},{6,4},{5,7},{7,5},{8,10},{10,8},{9,1... | collective-permute-start | bytes 2359304 | tf_op jit(solution)/shard_map/ppermute | solution.py:44
  28.7 28.9 %collective-permute-start.3 = (bf16[4,192,512]{2,1,0:T(8,128)(2,1)S(1)}, bf16[4,192,512]{2,1,0:T(8,128)(2,1)}, u32[]{:S(2)}, u32[]{:S(2)}) collective-permute-start(bf16[4,192,512]{2,1,0:T(8,128)(2,1)S(1)} %bitcast.118), channel_id=1, source_target_pairs={{0,4},{4,0},{1,5},{5,1},{2,6},{6,2},{3,7},{7,3},{8,12},{12,8},{9,1... | collective-permute-start | bytes 2359304 | tf_op jit(solution)/shard_map/ppermute | solution.py:44
  29.3 43.5 %collective-permute-start.6 = (bf16[288,1728]{1,0:T(8,128)(2,1)}, bf16[288,1728]{1,0:T(8,128)(2,1)}, u32[]{:S(2)}, u32[]{:S(2)}) collective-permute-start(bf16[288,1728]{1,0:T(8,128)(2,1)} %pad_maximum_fusion.4), channel_id=1, source_target_pairs={{0,16},{8,24},{16,0},{24,8},{1,17},{9,25},{17,1},{25,9},{2,18},{10... | collective-permute-start | bytes 2985992 | tf_op jit(solution)/shard_map/ppermute | solution.py:48
  77.5 29.0 %collective-permute-start.10 = (bf16[224,1728]{1,0:T(8,128)(2,1)}, bf16[224,1728]{1,0:T(8,128)(2,1)}, u32[]{:S(2)}, u32[]{:S(2)}) collective-permute-start(bf16[224,1728]{1,0:T(8,128)(2,1)} %slice.334), channel_id=1, source_target_pairs={{0,4},{4,0},{1,5},{5,1},{2,6},{6,2},{3,7},{7,3},{8,12},{12,8},{9,1... | collective-permute-start | bytes 2322440 | tf_op jit(solution)/shard_map/ppermute | solution.py:44
  81.0 25.4 %collective-permute-start.9 = (bf16[208,1728]{1,0:T(8,128)(2,1)}, bf16[208,1728]{1,0:T(8,128)(2,1)}, u32[]{:S(2)}, u32[]{:S(2)}) collective-permute-start(bf16[208,1728]{1,0:T(8,128)(2,1)} %slice.333), channel_id=1, source_target_pairs={{0,2},{2,0},{1,3},{3,1},{4,6},{6,4},{5,7},{7,5},{8,10},{10,8},{9,1... | collective-permute-start | bytes 2156552 | tf_op jit(solution)/shard_map/ppermute | solution.py:44
  82.5 25.4 %collective-permute-start.8 = (bf16[144,1728]{1,0:T(8,128)(2,1)}, bf16[144,1728]{1,0:T(8,128)(2,1)}, u32[]{:S(2)}, u32[]{:S(2)}) collective-permute-start(bf16[144,1728]{1,0:T(8,128)(2,1)} %bitcast.2), channel_id=1, source_target_pairs={{0,16},{8,24},{16,0},{24,8},{1,17},{9,25},{17,1},{25,9},{2,18},{10... | collective-permute-start | bytes 1493000 | tf_op jit(solution)/shard_map/ppermute | solution.py:48
  122.2 39.5 %collective-permute-start.16 = (bf16[432,1728]{1,0:T(8,128)(2,1)}, bf16[432,1728]{1,0:T(8,128)(2,1)}, u32[]{:S(2)}, u32[]{:S(2)}) collective-permute-start(bf16[432,1728]{1,0:T(8,128)(2,1)} %pad_maximum_fusion.1.refs_1_.refs_0_), channel_id=1, source_target_pairs={{0,2},{2,0},{1,3},{3,1},{4,6},{6,4},{5,7},{7,5},{8,10},{10,8},{9,1... | collective-permute-start | bytes 4478984 | tf_op jit(solution)/shard_map/ppermute | solution.py:44
  123.8 37.8 %collective-permute-start.17 = (bf16[432,1728]{1,0:T(8,128)(2,1)}, bf16[432,1728]{1,0:T(8,128)(2,1)}, u32[]{:S(2)}, u32[]{:S(2)}) collective-permute-start(bf16[432,1728]{1,0:T(8,128)(2,1)} %pad_maximum_fusion.1.refs_1_.refs_0_), channel_id=1, source_target_pairs={{0,4},{4,0},{1,5},{5,1},{2,6},{6,2},{3,7},{7,3},{8,12},{12,8},{9,1... | collective-permute-start | bytes 4478984 | tf_op jit(solution)/shard_map/ppermute | solution.py:44
  140.6 45.0 %collective-permute-start.20 = (bf16[432,1728]{1,0:T(8,128)(2,1)}, bf16[432,1728]{1,0:T(8,128)(2,1)}, u32[]{:S(2)}, u32[]{:S(2)}) collective-permute-start(bf16[432,1728]{1,0:T(8,128)(2,1)} %pad_maximum_fusion.1.refs_1_.refs_0_), channel_id=1, source_target_pairs={{0,1},{1,0},{2,3},{3,2},{4,5},{5,4},{6,7},{7,6},{8,9},{9,8},{10,11... | collective-permute-start | bytes 4478984 | tf_op jit(solution)/shard_map/ppermute | solution.py:44
  244.0 35.3 %collective-permute-start.27 = (bf16[256,1152]{1,0:T(8,128)(2,1)S(1)}, bf16[256,1152]{1,0:T(8,128)(2,1)S(1)}, u32[]{:S(2)}, u32[]{:S(2)}) collective-permute-start(bf16[256,1152]{1,0:T(8,128)(2,1)S(1)} %slice.342), channel_id=1, source_target_pairs={{0,16},{8,24},{16,0},{24,8},{1,17},{9,25},{17,1},{25,9},{2,18},{10... | collective-permute-start | bytes 1769480 | tf_op jit(solution)/shard_map/ppermute | solution.py:48
  301.4 25.5 %collective-permute-start.36 = (bf16[208,1728]{1,0:T(8,128)(2,1)S(1)}, bf16[208,1728]{1,0:T(8,128)(2,1)S(1)}, u32[]{:S(2)}, u32[]{:S(2)}) collective-permute-start(bf16[208,1728]{1,0:T(8,128)(2,1)S(1)} %get-tuple-element.311), channel_id=1, source_target_pairs={{0,2},{2,0},{1,3},{3,1},{4,6},{6,4},{5,7},{7,5},{8,10},{10,8},{9,1... | collective-permute-start | bytes 2156552 | tf_op jit(solution)/shard_map/ppermute | solution.py:44
  306.4 37.4 %collective-permute-start.34 = (bf16[224,1728]{1,0:T(8,128)(2,1)S(1)}, bf16[224,1728]{1,0:T(8,128)(2,1)S(1)}, u32[]{:S(2)}, u32[]{:S(2)}) collective-permute-start(bf16[224,1728]{1,0:T(8,128)(2,1)S(1)} %get-tuple-element.314), channel_id=1, source_target_pairs={{0,4},{4,0},{1,5},{5,1},{2,6},{6,2},{3,7},{7,3},{8,12},{12,8},{9,1... | collective-permute-start | bytes 2322440 | tf_op jit(solution)/shard_map/ppermute | solution.py:44
  307.8 36.0 %collective-permute-start.33 = (bf16[208,1728]{1,0:T(8,128)(2,1)}, bf16[208,1728]{1,0:T(8,128)(2,1)}, u32[]{:S(2)}, u32[]{:S(2)}) collective-permute-start(bf16[208,1728]{1,0:T(8,128)(2,1)} %get-tuple-element.312), channel_id=1, source_target_pairs={{0,2},{2,0},{1,3},{3,1},{4,6},{6,4},{5,7},{7,5},{8,10},{10,8},{9,1... | collective-permute-start | bytes 2156552 | tf_op jit(solution)/shard_map/ppermute | solution.py:44
  408.1 29.2 %collective-permute-start.44 = (bf16[256,1152]{1,0:T(8,128)(2,1)}, bf16[256,1152]{1,0:T(8,128)(2,1)}, u32[]{:S(2)}, u32[]{:S(2)}) collective-permute-start(bf16[256,1152]{1,0:T(8,128)(2,1)} %get-tuple-element.272.refs_0_), channel_id=1, source_target_pairs={{0,16},{8,24},{16,0},{24,8},{1,17},{9,25},{17,1},{25,9},{2,18},{10... | collective-permute-start | bytes 1769480 | tf_op jit(solution)/shard_map/ppermute | solution.py:48
  408.1 29.2 %collective-permute-start.49 = (bf16[224,1728]{1,0:T(8,128)(2,1)}, bf16[224,1728]{1,0:T(8,128)(2,1)}, u32[]{:S(2)}, u32[]{:S(2)}) collective-permute-start(bf16[224,1728]{1,0:T(8,128)(2,1)} %get-tuple-element.284), channel_id=1, source_target_pairs={{0,4},{4,0},{1,5},{5,1},{2,6},{6,2},{3,7},{7,3},{8,12},{12,8},{9,1... | collective-permute-start | bytes 2322440 | tf_op jit(solution)/shard_map/ppermute | solution.py:44
  409.1 28.2 %collective-permute-start.48 = (bf16[208,1728]{1,0:T(8,128)(2,1)}, bf16[208,1728]{1,0:T(8,128)(2,1)}, u32[]{:S(2)}, u32[]{:S(2)}) collective-permute-start(bf16[208,1728]{1,0:T(8,128)(2,1)} %get-tuple-element.283), channel_id=1, source_target_pairs={{0,2},{2,0},{1,3},{3,1},{4,6},{6,4},{5,7},{7,5},{8,10},{10,8},{9,1... | collective-permute-start | bytes 2156552 | tf_op jit(solution)/shard_map/ppermute | solution.py:44
  439.1 40.5 %collective-permute-start.53 = (bf16[768,512]{1,0:T(8,128)(2,1)S(1)}, bf16[768,512]{1,0:T(8,128)(2,1)S(1)}, u32[]{:S(2)}, u32[]{:S(2)}) collective-permute-start(bf16[768,512]{1,0:T(8,128)(2,1)S(1)} %pad_maximum_fusion.6), channel_id=1, source_target_pairs={{0,4},{4,0},{1,5},{5,1},{2,6},{6,2},{3,7},{7,3},{8,12},{12,8},{9,1... | collective-permute-start | bytes 2359304 | tf_op jit(solution)/shard_map/ppermute | solution.py:44
  440.1 39.5 %collective-permute-start.52 = (bf16[768,512]{1,0:T(8,128)(2,1)S(1)}, bf16[768,512]{1,0:T(8,128)(2,1)S(1)}, u32[]{:S(2)}, u32[]{:S(2)}) collective-permute-start(bf16[768,512]{1,0:T(8,128)(2,1)S(1)} %pad_maximum_fusion.5), channel_id=1, source_target_pairs={{0,2},{2,0},{1,3},{3,1},{4,6},{6,4},{5,7},{7,5},{8,10},{10,8},{9,1... | collective-permute-start | bytes 2359304 | tf_op jit(solution)/shard_map/ppermute | solution.py:44
  441.7 38.8 %collective-permute-start.51 = (bf16[512,1152]{1,0:T(8,128)(2,1)S(1)}, bf16[512,1152]{1,0:T(8,128)(2,1)S(1)}, u32[]{:S(2)}, u32[]{:S(2)}) collective-permute-start(bf16[512,1152]{1,0:T(8,128)(2,1)S(1)} %pad_maximum_fusion.3), channel_id=1, source_target_pairs={{0,8},{8,0},{16,24},{24,16},{1,9},{9,1},{17,25},{25,17},{2,10},{10... | collective-permute-start | bytes 3538952 | tf_op jit(solution)/shard_map/ppermute | solution.py:48
  444.2 35.5 %collective-permute-start.50 = (bf16[144,1728]{1,0:T(8,128)(2,1)S(1)}, bf16[144,1728]{1,0:T(8,128)(2,1)S(1)}, u32[]{:S(2)}, u32[]{:S(2)}) collective-permute-start(bf16[144,1728]{1,0:T(8,128)(2,1)S(1)} %get-tuple-element.330), channel_id=1, source_target_pairs={{0,16},{8,24},{16,0},{24,8},{1,17},{9,25},{17,1},{25,9},{2,18},{10... | collective-permute-start | bytes 1493000 | tf_op jit(solution)/shard_map/ppermute | solution.py:48
  488.6 32.1 %collective-permute-start.57 = (bf16[208,1728]{1,0:T(8,128)(2,1)S(1)}, bf16[208,1728]{1,0:T(8,128)(2,1)S(1)}, u32[]{:S(2)}, u32[]{:S(2)}) collective-permute-start(bf16[208,1728]{1,0:T(8,128)(2,1)S(1)} %copy-done.82), channel_id=1, source_target_pairs={{0,2},{2,0},{1,3},{3,1},{4,6},{6,4},{5,7},{7,5},{8,10},{10,8},{9,1... | collective-permute-start | bytes 2156552 | tf_op jit(solution)/shard_map/ppermute | solution.py:44
  490.2 39.7 %collective-permute-start.60 = (bf16[224,1728]{1,0:T(8,128)(2,1)S(1)}, bf16[224,1728]{1,0:T(8,128)(2,1)S(1)}, u32[]{:S(2)}, u32[]{:S(2)}) collective-permute-start(bf16[224,1728]{1,0:T(8,128)(2,1)S(1)} %copy-done.81), channel_id=1, source_target_pairs={{0,4},{4,0},{1,5},{5,1},{2,6},{6,2},{3,7},{7,3},{8,12},{12,8},{9,1... | collective-permute-start | bytes 2322440 | tf_op jit(solution)/shard_map/ppermute | solution.py:44
  (144 other events, 1375.2 us)

commit v5 on v4

--- a/solution.py
+++ b/solution.py
@@ -1055,9 +1055,9 @@
         )
         pack_far = send_far(pack_x, pack_y)
         ffn_far = send_far(ffn_x, ffn_y)
-        *pack_far, their_gu, other_down = tie(*pack_far, their_gu, down_t)
+        pack_all = collect((pack, pack_x, pack_y, *pack_far), planes)
+        pack_all, their_gu, other_down = tie(pack_all, their_gu, down_t)
         their_down = across(other_down, 2)
-        pack_all = collect((pack, pack_x, pack_y, *pack_far), planes)
         pack_other = swap(pack_all, "gc")
         wq, wo_t, wkv, gains = unpack(
             [pack_all, pack_other], block, head_width, gain_spot, gain_rows

time: 547 us -> 545 us (level)
    ppermute x18, waiting for transfers between devices: 132 us -> 120 us  [across(): return lax.ppermute(x, 'gx', [(i, i ^ distance) for i in range(4)])]
    ppermute x38, waiting for transfers between devices: 46.9 us -> 54 us  [swap(): return lax.ppermute(x, axis, SWAP)]
  transfers between devices with their start and end apart: 62 -> 62, of which waited for: 25 -> 27; matrix products, arithmetic and copies ran while one was open for 11% -> 11% of each run, Pallas kernels for 23% -> 24%
where the time goes in v5:
time: 545 us; the launch traced here: 535 us
  waiting for transfers between devices  181 us (33%)
  Pallas kernels  153 us (28%)
  starting transfers between devices  66.5 us (12%)
  local copies, waits for them, and re-layouts  58.4 us (11%)
  other arithmetic  52.4 us (10%)
  blocking collectives  19.9 us (4%)
    ppermute x18, waiting for transfers between devices, across(): return lax.ppermute(x, 'gx', [(i, i ^ distance) for i in range(4)])  120 us
    pallas_call x13, Pallas kernels, prefetch_call(): pl.pallas_call(kernel, grid_spec=pltpu.PrefetchScalarGridSpec(num_scalar_...  105 us
    ppermute x38, waiting for transfers between devices, swap(): return lax.ppermute(x, axis, SWAP)  54 us
    unnamed x216, local copies, waits for them, and re-layouts  35.6 us
    ppermute x38, starting transfers between devices, swap(): return lax.ppermute(x, axis, SWAP)  33.6 us
    pallas_call x4, Pallas kernels, ffn_weight_grads(): pl.pallas_call(kernel, grid_spec=pltpu.PrefetchScalarGridSpec(num_scalar_...  26.8 us
    ppermute x18, starting transfers between devices, across(): return lax.ppermute(x, 'gx', [(i, i ^ distance) for i in range(4)])  22.9 us
    all_gather x1, blocking collectives, body(): pack = lax.all_gather(pack, 'gx', axis=0)  19.9 us
  transfers between devices with their start and end apart: 62, of which 27 were waited for; matrix products, arithmetic and copies ran while one was open for 11% of the time, Pallas kernels for 24%

profile of v5, /device:TPU:0, one launch (start us, length us, event | category | flops | bytes accessed | tf_op | source)
XLA Modules:
  0.0 534.7 jit_solution(17645143401593397554)
XLA Ops:
  8.3 19.9 %all-gather = bf16[768,512]{1,0:T(8,128)(2,1)S(1)} all-gather(bf16[192,512]{1,0:T(8,128)(2,1)S(1)} %concatenate.58), channel_id=2, replica_groups=mesh['gx'=4,'gb'=2,'ga'=2,'gc'=2] {'gx'}, dimensions={0}, use_global_device_ids=true | all-gather | bytes 983040 | tf_op jit(solution)/shard_map/all_gather | solution.py:1049
  35.7 20.5 %collective-permute-done.2.refs_1_ = bf16[4,192,512]{2,1,0:T(8,128)(2,1)} collective-permute-done((bf16[4,192,512]{2,1,0:T(8,128)(2,1)S(1)}, bf16[4,192,512]{2,1,0:T(8,128)(2,1)}, u32[]{:S(2)}, u32[]{:S(2)}) %collective-permute-start.2) | collective-permute-done | bytes 786464 | tf_op jit(solution)/shard_map/ppermute | solution.py:44
  61.9 6.5 %collective-permute-done.4.refs_3_ = bf16[2,192,512]{2,1,0:T(8,128)(2,1)S(1)} collective-permute-done((bf16[2,192,512]{2,1,0:T(8,128)(2,1)S(1)}, bf16[2,192,512]{2,1,0:T(8,128)(2,1)S(1)}, u32[]{:S(2)}, u32[]{:S(2)}) %collective-permute-start.4) | collective-permute-done | bytes 393248 | tf_op jit(solution)/shard_map/ppermute | solution.py:44
  91.9 5.8 %shard_map.301 = (bf16[1024,512]{1,0:T(8,128)(2,1)S(1)}, bf16[256,1152]{1,0:T(8,128)(2,1)S(1)}, f32[256,256]{1,0:T(8,128)S(1)}, bf16[256,512]{1,0:T(8,128)(2,1)}...) custom-call(s32[13]{0:T(128)S(1)} %copy-done.45, bf16[1024,1152]{1,0:T(8,128)(2,1)} %refs_9_.1, ...), custom_call_target="tpu_custom_call" | custom-call | flops 6899999744 | tf_op jit(solution)/shard_map/pallas_call | solution.py:325
  122.7 5.5 %collective-permute-done.13.g3 = bf16[256,512]{1,0:T(8,128)(2,1)S(1)} collective-permute-done((bf16[256,512]{1,0:T(8,128)(2,1)S(1)}, bf16[256,512]{1,0:T(8,128)(2,1)S(1)}, u32[]{:S(2)}, u32[]{:S(2)}) %collective-permute-start.13) | collective-permute-done | bytes 262176 | tf_op jit(solution)/shard_map/ppermute | solution.py:1100
  139.2 12.7 %collective-permute-done.15.got = bf16[256,1024]{1,0:T(8,128)(2,1)S(1)} collective-permute-done((bf16[256,1024]{1,0:T(8,128)(2,1)}, bf16[256,1024]{1,0:T(8,128)(2,1)S(1)}, u32[]{:S(2)}, u32[]{:S(2)}) %collective-permute-start.15) | collective-permute-done | bytes 524320 | tf_op jit(solution)/shard_map/ppermute | solution.py:48
  165.6 15.5 %shard_map.306 = (bf16[512,1728]{1,0:T(8,128)(2,1)}, bf16[512,1728]{1,0:T(8,128)(2,1)}, bf16[512,1728]{1,0:T(8,128)(2,1)}, f32[512,1152]{1,0:T(8,128)}) custom-call(s32[8]{0:T(128)} %get-tuple-element.350.slots, bf16[512,1152]{1,0:T(8,128)(2,1)} %copy-done.9, bf16[1728,1728]{1,0:T(8,128)(2,1)} %shard_map.303.refs_0_.refs_1_, ...), custom_call_target="tpu_custom_call" | custom-call | flops 18400000000 | tf_op jit(solution)/shard_map/pallas_call | solution.py:325
  188.3 15.8 %shard_map.307 = (bf16[512,1728]{1,0:T(8,128)(2,1)}, bf16[512,1728]{1,0:T(8,128)(2,1)}, bf16[512,1728]{1,0:T(8,128)(2,1)}, f32[512,1152]{1,0:T(8,128)}) custom-call(s32[10]{0:T(128)} %xor_multiply_fusion.slots, bf16[512,1152]{1,0:T(8,128)(2,1)} %copy-done.9, f32[512,1152]{1,0:T(8,128)} %get-tuple-element.201.refs_0_, ...), custom_call_target="tpu_custom_call" | custom-call | flops 18400000000 | tf_op jit(solution)/shard_map/pallas_call | solution.py:325
  206.8 14.0 %collective-permute-done.25 = bf16[256,1152]{1,0:T(8,128)(2,1)S(1)} collective-permute-done((bf16[256,1152]{1,0:T(8,128)(2,1)S(1)}, bf16[256,1152]{1,0:T(8,128)(2,1)S(1)}, u32[]{:S(2)}, u32[]{:S(2)}) %collective-permute-start.25) | collective-permute-done | bytes 589856 | tf_op jit(solution)/shard_map/ppermute | solution.py:48
  226.8 10.1 %collective-permute-done.26.other_ref = bf16[256,1152]{1,0:T(8,128)(2,1)} collective-permute-done((bf16[256,1152]{1,0:T(8,128)(2,1)S(1)}, bf16[256,1152]{1,0:T(8,128)(2,1)}, u32[]{:S(2)}, u32[]{:S(2)}) %collective-permute-start.26) | collective-permute-done | bytes 589856 | tf_op jit(solution)/shard_map/ppermute | solution.py:48
  244.0 16.2 %shard_map.309 = (bf16[512,1728]{1,0:T(8,128)(2,1)}, bf16[512,1728]{1,0:T(8,128)(2,1)}, f32[512,1152]{1,0:T(8,128)}) custom-call(s32[10]{0:T(128)} %xor_multiply_fusion.slots, bf16[512,1152]{1,0:T(8,128)(2,1)} %copy-done.59, bf16[512,1728]{1,0:T(8,128)(2,1)} %get-tuple-element.209.act_ref, bf16[512,1728]{1,0:T(8,128)(2,1)} %get-tuple-element.210.slope_ref, ...), custom_call_target="tpu_custom_call" | custom-call | flops 18400000000 | tf_op jit(solution)/shard_map/pallas_call | solution.py:325
  264.4 6.6 %shard_map.311 = bf16[4,432,1728]{2,1,0:T(8,128)(2,1)} custom-call(s32[1]{0:T(128)} %bitcast.7.core_ref, bf16[1152,512]{1,0:T(8,128)(2,1)S(1)} %bitcast.113, bf16[1152,512]{1,0:T(8,128)(2,1)S(1)} %copy-done.57, bf16[512,1728]{1,0:T(8,128)(2,1)S(1)} %copy-done.67, bf16[512,1728]{1,0:T(8,128)(2,1)S(1)} %copy-done.68, ...), custom_call_target="tpu_custom_call" | custom-call | flops 7704999936 | tf_op jit(solution)/shard_map/pallas_call | solution.py:208
  271.1 6.6 %shard_map.310 = bf16[4,432,1728]{2,1,0:T(8,128)(2,1)} custom-call(s32[1]{0:T(128)} %bitcast.5.core_ref, bf16[1152,512]{1,0:T(8,128)(2,1)S(1)} %bitcast.114, bf16[1152,512]{1,0:T(8,128)(2,1)S(1)} %copy-done.57, bf16[512,1728]{1,0:T(8,128)(2,1)S(1)} %copy-done.67, bf16[512,1728]{1,0:T(8,128)(2,1)S(1)} %copy-done.68, ...), custom_call_target="tpu_custom_call" | custom-call | flops 7704999936 | tf_op jit(solution)/shard_map/pallas_call | solution.py:208
  277.7 16.1 %shard_map.312 = (bf16[512,1728]{1,0:T(8,128)(2,1)}, bf16[512,1728]{1,0:T(8,128)(2,1)}, f32[512,1152]{1,0:T(8,128)}) custom-call(s32[8]{0:T(128)} %get-tuple-element.350.slots, bf16[512,1152]{1,0:T(8,128)(2,1)} %copy-done.59, bf16[512,1728]{1,0:T(8,128)(2,1)} %get-tuple-element.207.act_ref, bf16[512,1728]{1,0:T(8,128)(2,1)} %get-tuple-element.208.slope_ref, ...), custom_call_target="tpu_custom_call" | custom-call | flops 18400000000 | tf_op jit(solution)/shard_map/pallas_call | solution.py:325
  313.6 11.7 %shard_map.313 = (f32[256,1152]{1,0:T(8,128)}, bf16[256,1152]{1,0:T(8,128)(2,1)}, bf16[1152,256]{1,0:T(8,128)(2,1)S(1)}, f32[2,1152]{1,0:T(2,128)S(1)}, bf16[256...) custom-call(s32[13]{0:T(128)S(1)} %copy-done.46, ...), custom_call_target="tpu_custom_call" | custom-call | flops 13799999488 | tf_op jit(solution)/shard_map/pallas_call | solution.py:325
  335.5 6.7 %shard_map.314 = bf16[4,432,1728]{2,1,0:T(8,128)(2,1)} custom-call(s32[1]{0:T(128)} %bitcast.5.core_ref, bf16[1152,512]{1,0:T(8,128)(2,1)S(1)} %bitcast.115, bf16[1152,512]{1,0:T(8,128)(2,1)S(1)} %copy-done.58, bf16[512,1728]{1,0:T(8,128)(2,1)S(1)} %copy-done.65, bf16[512,1728]{1,0:T(8,128)(2,1)S(1)} %copy-done.66, ...), custom_call_target="tpu_custom_call" | custom-call | flops 7704999936 | tf_op jit(solution)/shard_map/pallas_call | solution.py:208
  343.7 6.8 %shard_map.315 = bf16[4,432,1728]{2,1,0:T(8,128)(2,1)} custom-call(s32[1]{0:T(128)} %bitcast.7.core_ref, bf16[1152,512]{1,0:T(8,128)(2,1)S(1)} %bitcast.116, bf16[1152,512]{1,0:T(8,128)(2,1)S(1)} %copy-done.58, bf16[512,1728]{1,0:T(8,128)(2,1)S(1)} %copy-done.65, bf16[512,1728]{1,0:T(8,128)(2,1)S(1)} %copy-done.66, ...), custom_call_target="tpu_custom_call" | custom-call | flops 7704999936 | tf_op jit(solution)/shard_map/pallas_call | solution.py:208
  361.7 11.8 %collective-permute-done.42 = bf16[208,1728]{1,0:T(8,128)(2,1)} collective-permute-done((bf16[208,1728]{1,0:T(8,128)(2,1)}, bf16[208,1728]{1,0:T(8,128)(2,1)}, u32[]{:S(2)}, u32[]{:S(2)}) %collective-permute-start.42) | collective-permute-done | bytes 718880 | tf_op jit(solution)/shard_map/ppermute | solution.py:44
  388.6 7.0 %collective-permute-done.41.refs_1_ = bf16[256,512]{1,0:T(8,128)(2,1)S(1)} collective-permute-done((bf16[256,512]{1,0:T(8,128)(2,1)S(1)}, bf16[256,512]{1,0:T(8,128)(2,1)S(1)}, u32[]{:S(2)}, u32[]{:S(2)}) %collective-permute-start.41) | collective-permute-done | bytes 262176 | tf_op jit(solution)/shard_map/ppermute | solution.py:48
  419.8 16.0 %collective-permute-done.44.refs_1_ = bf16[256,1152]{1,0:T(8,128)(2,1)} collective-permute-done((bf16[256,1152]{1,0:T(8,128)(2,1)}, bf16[256,1152]{1,0:T(8,128)(2,1)}, u32[]{:S(2)}, u32[]{:S(2)}) %collective-permute-start.44) | collective-permute-done | bytes 589856 | tf_op jit(solution)/shard_map/ppermute | solution.py:48
  446.7 31.3 %collective-permute-done.50 = bf16[144,1728]{1,0:T(8,128)(2,1)S(1)} collective-permute-done((bf16[144,1728]{1,0:T(8,128)(2,1)S(1)}, bf16[144,1728]{1,0:T(8,128)(2,1)S(1)}, u32[]{:S(2)}, u32[]{:S(2)}) %collective-permute-start.50) | collective-permute-done | bytes 497696 | tf_op jit(solution)/shard_map/ppermute | solution.py:48
  489.8 7.5 %collective-permute-done.54 = bf16[2,192,512]{2,1,0:T(8,128)(2,1)S(1)} collective-permute-done((bf16[2,192,512]{2,1,0:T(8,128)(2,1)S(1)}, bf16[2,192,512]{2,1,0:T(8,128)(2,1)S(1)}, u32[]{:S(2)}, u32[]{:S(2)}) %collective-permute-start.54) | collective-permute-done | bytes 393248 | tf_op jit(solution)/shard_map/ppermute | solution.py:48
  497.6 9.6 %collective-permute-done.55 = bf16[144,1728]{1,0:T(8,128)(2,1)S(1)} collective-permute-done((bf16[144,1728]{1,0:T(8,128)(2,1)S(1)}, bf16[144,1728]{1,0:T(8,128)(2,1)S(1)}, u32[]{:S(2)}, u32[]{:S(2)}) %collective-permute-start.55) | collective-permute-done | bytes 497696 | tf_op jit(solution)/shard_map/ppermute | solution.py:48
  519.2 7.4 %collective-permute-done.58 = bf16[208,1728]{1,0:T(8,128)(2,1)S(1)} collective-permute-done((bf16[208,1728]{1,0:T(8,128)(2,1)S(1)}, bf16[208,1728]{1,0:T(8,128)(2,1)S(1)}, u32[]{:S(2)}, u32[]{:S(2)}) %collective-permute-start.58) | collective-permute-done | bytes 718880 | tf_op jit(solution)/shard_map/ppermute | solution.py:44
  (445 shorter events, 244.9 us)
Async XLA Ops:
  2.4 55.3 %collective-permute-start = (bf16[432,1728]{1,0:T(8,128)(2,1)S(1)}, bf16[432,1728]{1,0:T(8,128)(2,1)}, u32[]{:S(2)}, u32[]{:S(2)}) collective-permute-start(bf16[432,1728]{1,0:T(8,128)(2,1)S(1)} %pad_maximum_fusion.refs_0_), channel_id=1, source_target_pairs={{0,2},{2,0},{1,3},{3,1},{4,6},{6,4},{5,7},{7,5},{8,10},{10,8},{9,1... | collective-permute-start | bytes 4478984 | tf_op jit(solution)/shard_map/ppermute | solution.py:44
  5.4 52.3 %collective-permute-start.1 = (bf16[432,1728]{1,0:T(8,128)(2,1)S(1)}, bf16[432,1728]{1,0:T(8,128)(2,1)}, u32[]{:S(2)}, u32[]{:S(2)}) collective-permute-start(bf16[432,1728]{1,0:T(8,128)(2,1)S(1)} %pad_maximum_fusion.refs_0_), channel_id=1, source_target_pairs={{0,4},{4,0},{1,5},{5,1},{2,6},{6,2},{3,7},{7,3},{8,12},{12,8},{9,1... | collective-permute-start | bytes 4478984 | tf_op jit(solution)/shard_map/ppermute | solution.py:44
  28.2 28.0 %collective-permute-start.2 = (bf16[4,192,512]{2,1,0:T(8,128)(2,1)S(1)}, bf16[4,192,512]{2,1,0:T(8,128)(2,1)}, u32[]{:S(2)}, u32[]{:S(2)}) collective-permute-start(bf16[4,192,512]{2,1,0:T(8,128)(2,1)S(1)} %bitcast.117), channel_id=1, source_target_pairs={{0,2},{2,0},{1,3},{3,1},{4,6},{6,4},{5,7},{7,5},{8,10},{10,8},{9,1... | collective-permute-start | bytes 2359304 | tf_op jit(solution)/shard_map/ppermute | solution.py:44
  28.7 28.9 %collective-permute-start.3 = (bf16[4,192,512]{2,1,0:T(8,128)(2,1)S(1)}, bf16[4,192,512]{2,1,0:T(8,128)(2,1)}, u32[]{:S(2)}, u32[]{:S(2)}) collective-permute-start(bf16[4,192,512]{2,1,0:T(8,128)(2,1)S(1)} %bitcast.118), channel_id=1, source_target_pairs={{0,4},{4,0},{1,5},{5,1},{2,6},{6,2},{3,7},{7,3},{8,12},{12,8},{9,1... | collective-permute-start | bytes 2359304 | tf_op jit(solution)/shard_map/ppermute | solution.py:44
  29.3 43.5 %collective-permute-start.6 = (bf16[288,1728]{1,0:T(8,128)(2,1)}, bf16[288,1728]{1,0:T(8,128)(2,1)}, u32[]{:S(2)}, u32[]{:S(2)}) collective-permute-start(bf16[288,1728]{1,0:T(8,128)(2,1)} %pad_maximum_fusion.4), channel_id=1, source_target_pairs={{0,16},{8,24},{16,0},{24,8},{1,17},{9,25},{17,1},{25,9},{2,18},{10... | collective-permute-start | bytes 2985992 | tf_op jit(solution)/shard_map/ppermute | solution.py:48
  75.4 30.6 %collective-permute-start.10 = (bf16[224,1728]{1,0:T(8,128)(2,1)}, bf16[224,1728]{1,0:T(8,128)(2,1)}, u32[]{:S(2)}, u32[]{:S(2)}) collective-permute-start(bf16[224,1728]{1,0:T(8,128)(2,1)} %slice.334), channel_id=1, source_target_pairs={{0,4},{4,0},{1,5},{5,1},{2,6},{6,2},{3,7},{7,3},{8,12},{12,8},{9,1... | collective-permute-start | bytes 2322440 | tf_op jit(solution)/shard_map/ppermute | solution.py:44
  79.0 27.0 %collective-permute-start.9 = (bf16[208,1728]{1,0:T(8,128)(2,1)}, bf16[208,1728]{1,0:T(8,128)(2,1)}, u32[]{:S(2)}, u32[]{:S(2)}) collective-permute-start(bf16[208,1728]{1,0:T(8,128)(2,1)} %slice.333), channel_id=1, source_target_pairs={{0,2},{2,0},{1,3},{3,1},{4,6},{6,4},{5,7},{7,5},{8,10},{10,8},{9,1... | collective-permute-start | bytes 2156552 | tf_op jit(solution)/shard_map/ppermute | solution.py:44
  80.5 25.9 %collective-permute-start.8 = (bf16[144,1728]{1,0:T(8,128)(2,1)}, bf16[144,1728]{1,0:T(8,128)(2,1)}, u32[]{:S(2)}, u32[]{:S(2)}) collective-permute-start(bf16[144,1728]{1,0:T(8,128)(2,1)} %bitcast.2), channel_id=1, source_target_pairs={{0,16},{8,24},{16,0},{24,8},{1,17},{9,25},{17,1},{25,9},{2,18},{10... | collective-permute-start | bytes 1493000 | tf_op jit(solution)/shard_map/ppermute | solution.py:48
  120.6 39.5 %collective-permute-start.16 = (bf16[432,1728]{1,0:T(8,128)(2,1)}, bf16[432,1728]{1,0:T(8,128)(2,1)}, u32[]{:S(2)}, u32[]{:S(2)}) collective-permute-start(bf16[432,1728]{1,0:T(8,128)(2,1)} %pad_maximum_fusion.1.refs_1_.refs_0_), channel_id=1, source_target_pairs={{0,2},{2,0},{1,3},{3,1},{4,6},{6,4},{5,7},{7,5},{8,10},{10,8},{9,1... | collective-permute-start | bytes 4478984 | tf_op jit(solution)/shard_map/ppermute | solution.py:44
  122.2 37.8 %collective-permute-start.17 = (bf16[432,1728]{1,0:T(8,128)(2,1)}, bf16[432,1728]{1,0:T(8,128)(2,1)}, u32[]{:S(2)}, u32[]{:S(2)}) collective-permute-start(bf16[432,1728]{1,0:T(8,128)(2,1)} %pad_maximum_fusion.1.refs_1_.refs_0_), channel_id=1, source_target_pairs={{0,4},{4,0},{1,5},{5,1},{2,6},{6,2},{3,7},{7,3},{8,12},{12,8},{9,1... | collective-permute-start | bytes 4478984 | tf_op jit(solution)/shard_map/ppermute | solution.py:44
  139.0 44.9 %collective-permute-start.20 = (bf16[432,1728]{1,0:T(8,128)(2,1)}, bf16[432,1728]{1,0:T(8,128)(2,1)}, u32[]{:S(2)}, u32[]{:S(2)}) collective-permute-start(bf16[432,1728]{1,0:T(8,128)(2,1)} %pad_maximum_fusion.1.refs_1_.refs_0_), channel_id=1, source_target_pairs={{0,1},{1,0},{2,3},{3,2},{4,5},{5,4},{6,7},{7,6},{8,9},{9,8},{10,11... | collective-permute-start | bytes 4478984 | tf_op jit(solution)/shard_map/ppermute | solution.py:44
  242.5 35.2 %collective-permute-start.27 = (bf16[256,1152]{1,0:T(8,128)(2,1)S(1)}, bf16[256,1152]{1,0:T(8,128)(2,1)S(1)}, u32[]{:S(2)}, u32[]{:S(2)}) collective-permute-start(bf16[256,1152]{1,0:T(8,128)(2,1)S(1)} %slice.342), channel_id=1, source_target_pairs={{0,16},{8,24},{16,0},{24,8},{1,17},{9,25},{17,1},{25,9},{2,18},{10... | collective-permute-start | bytes 1769480 | tf_op jit(solution)/shard_map/ppermute | solution.py:48
  305.7 36.5 %collective-permute-start.34 = (bf16[224,1728]{1,0:T(8,128)(2,1)S(1)}, bf16[224,1728]{1,0:T(8,128)(2,1)S(1)}, u32[]{:S(2)}, u32[]{:S(2)}) collective-permute-start(bf16[224,1728]{1,0:T(8,128)(2,1)S(1)} %get-tuple-element.312), channel_id=1, source_target_pairs={{0,4},{4,0},{1,5},{5,1},{2,6},{6,2},{3,7},{7,3},{8,12},{12,8},{9,1... | collective-permute-start | bytes 2322440 | tf_op jit(solution)/shard_map/ppermute | solution.py:44
  307.1 35.1 %collective-permute-start.33 = (bf16[208,1728]{1,0:T(8,128)(2,1)}, bf16[208,1728]{1,0:T(8,128)(2,1)}, u32[]{:S(2)}, u32[]{:S(2)}) collective-permute-start(bf16[208,1728]{1,0:T(8,128)(2,1)} %get-tuple-element.310), channel_id=1, source_target_pairs={{0,2},{2,0},{1,3},{3,1},{4,6},{6,4},{5,7},{7,5},{8,10},{10,8},{9,1... | collective-permute-start | bytes 2156552 | tf_op jit(solution)/shard_map/ppermute | solution.py:44
  354.1 25.4 %collective-permute-start.40 = (bf16[4,432,1728]{2,1,0:T(8,128)(2,1)}, bf16[4,432,1728]{2,1,0:T(8,128)(2,1)}, u32[]{:S(2)}, u32[]{:S(2)}) collective-permute-start(bf16[4,432,1728]{2,1,0:T(8,128)(2,1)} %shard_map.314), channel_id=1, source_target_pairs={{0,1},{1,0},{2,3},{3,2},{4,5},{5,4},{6,7},{7,6},{8,9},{9,8},{10,11... | collective-permute-start | bytes 17915912 | tf_op jit(solution)/shard_map/ppermute | solution.py:44
  406.6 29.2 %collective-permute-start.44 = (bf16[256,1152]{1,0:T(8,128)(2,1)}, bf16[256,1152]{1,0:T(8,128)(2,1)}, u32[]{:S(2)}, u32[]{:S(2)}) collective-permute-start(bf16[256,1152]{1,0:T(8,128)(2,1)} %get-tuple-element.270.refs_0_), channel_id=1, source_target_pairs={{0,16},{8,24},{16,0},{24,8},{1,17},{9,25},{17,1},{25,9},{2,18},{10... | collective-permute-start | bytes 1769480 | tf_op jit(solution)/shard_map/ppermute | solution.py:48
  406.6 29.2 %collective-permute-start.49 = (bf16[224,1728]{1,0:T(8,128)(2,1)}, bf16[224,1728]{1,0:T(8,128)(2,1)}, u32[]{:S(2)}, u32[]{:S(2)}) collective-permute-start(bf16[224,1728]{1,0:T(8,128)(2,1)} %get-tuple-element.282), channel_id=1, source_target_pairs={{0,4},{4,0},{1,5},{5,1},{2,6},{6,2},{3,7},{7,3},{8,12},{12,8},{9,1... | collective-permute-start | bytes 2322440 | tf_op jit(solution)/shard_map/ppermute | solution.py:44
  407.5 28.3 %collective-permute-start.48 = (bf16[208,1728]{1,0:T(8,128)(2,1)}, bf16[208,1728]{1,0:T(8,128)(2,1)}, u32[]{:S(2)}, u32[]{:S(2)}) collective-permute-start(bf16[208,1728]{1,0:T(8,128)(2,1)} %get-tuple-element.281), channel_id=1, source_target_pairs={{0,2},{2,0},{1,3},{3,1},{4,6},{6,4},{5,7},{7,5},{8,10},{10,8},{9,1... | collective-permute-start | bytes 2156552 | tf_op jit(solution)/shard_map/ppermute | solution.py:44
  437.6 40.5 %collective-permute-start.53 = (bf16[768,512]{1,0:T(8,128)(2,1)S(1)}, bf16[768,512]{1,0:T(8,128)(2,1)S(1)}, u32[]{:S(2)}, u32[]{:S(2)}) collective-permute-start(bf16[768,512]{1,0:T(8,128)(2,1)S(1)} %pad_maximum_fusion.6), channel_id=1, source_target_pairs={{0,4},{4,0},{1,5},{5,1},{2,6},{6,2},{3,7},{7,3},{8,12},{12,8},{9,1... | collective-permute-start | bytes 2359304 | tf_op jit(solution)/shard_map/ppermute | solution.py:44
  438.6 39.5 %collective-permute-start.52 = (bf16[768,512]{1,0:T(8,128)(2,1)S(1)}, bf16[768,512]{1,0:T(8,128)(2,1)S(1)}, u32[]{:S(2)}, u32[]{:S(2)}) collective-permute-start(bf16[768,512]{1,0:T(8,128)(2,1)S(1)} %pad_maximum_fusion.5), channel_id=1, source_target_pairs={{0,2},{2,0},{1,3},{3,1},{4,6},{6,4},{5,7},{7,5},{8,10},{10,8},{9,1... | collective-permute-start | bytes 2359304 | tf_op jit(solution)/shard_map/ppermute | solution.py:44
  440.1 38.8 %collective-permute-start.51 = (bf16[512,1152]{1,0:T(8,128)(2,1)S(1)}, bf16[512,1152]{1,0:T(8,128)(2,1)S(1)}, u32[]{:S(2)}, u32[]{:S(2)}) collective-permute-start(bf16[512,1152]{1,0:T(8,128)(2,1)S(1)} %pad_maximum_fusion.3), channel_id=1, source_target_pairs={{0,8},{8,0},{16,24},{24,16},{1,9},{9,1},{17,25},{25,17},{2,10},{10... | collective-permute-start | bytes 3538952 | tf_op jit(solution)/shard_map/ppermute | solution.py:48
  442.6 35.5 %collective-permute-start.50 = (bf16[144,1728]{1,0:T(8,128)(2,1)S(1)}, bf16[144,1728]{1,0:T(8,128)(2,1)S(1)}, u32[]{:S(2)}, u32[]{:S(2)}) collective-permute-start(bf16[144,1728]{1,0:T(8,128)(2,1)S(1)} %get-tuple-element.328), channel_id=1, source_target_pairs={{0,16},{8,24},{16,0},{24,8},{1,17},{9,25},{17,1},{25,9},{2,18},{10... | collective-permute-start | bytes 1493000 | tf_op jit(solution)/shard_map/ppermute | solution.py:48
  487.1 32.1 %collective-permute-start.57 = (bf16[208,1728]{1,0:T(8,128)(2,1)S(1)}, bf16[208,1728]{1,0:T(8,128)(2,1)S(1)}, u32[]{:S(2)}, u32[]{:S(2)}) collective-permute-start(bf16[208,1728]{1,0:T(8,128)(2,1)S(1)} %copy-done.82), channel_id=1, source_target_pairs={{0,2},{2,0},{1,3},{3,1},{4,6},{6,4},{5,7},{7,5},{8,10},{10,8},{9,1... | collective-permute-start | bytes 2156552 | tf_op jit(solution)/shard_map/ppermute | solution.py:44
  488.7 39.6 %collective-permute-start.60 = (bf16[224,1728]{1,0:T(8,128)(2,1)S(1)}, bf16[224,1728]{1,0:T(8,128)(2,1)S(1)}, u32[]{:S(2)}, u32[]{:S(2)}) collective-permute-start(bf16[224,1728]{1,0:T(8,128)(2,1)S(1)} %copy-done.81), channel_id=1, source_target_pairs={{0,4},{4,0},{1,5},{5,1},{2,6},{6,2},{3,7},{7,3},{8,12},{12,8},{9,1... | collective-permute-start | bytes 2322440 | tf_op jit(solution)/shard_map/ppermute | solution.py:44
  (144 other events, 1356.1 us)
